TPU v7x, 32 devices: a whole 2x2x4 slice. The times are simulated.
32 devices in a mesh: aux: 4 (over y, x), tile: 8 (over z, core).
Axes of the slice: x: 2, y: 2, z: 4, core: 2. Of those that a mesh axis runs over, the one named last changes fastest.
Arguments:
- integrals: bfloat16 [11904, 2, 2944], P(('aux', 'tile')), may hold values from -0.57421875 to 0.57421875
- coefficients: bfloat16 [2944, 2048], replicated, may hold values from -0.109375 to 0.109375
- owned_tiles: int32 [2, 16], replicated, may hold values from 0 to 15, each once within a row
- pair_list: int32 [2, 16, 4], P(None, 'tile'), may hold values from -1 to 15, as said below
- amplitudes: bfloat16 [2, 16, 4, 128, 128], P(None, 'tile'), may hold values from -0.25 to 0.25
Outputs:
- residual: float32 [2, 16, 128, 128], P(None, 'tile')
Inputs may be any that keep to these rules, and one draw needn't show every extreme that they name: `pair_list`: every live entry of slot s is a slot within 2 of s; the live entries of one slot are distinct; -1 marks an entry dropped by screening.
All inputs are finite; a program needn't handle non-finite values.
Results may differ from a plain program's by a relative error of at most 0.00087.
Values may be sent and summed in bfloat16 or wider, within the bound.
No kernel may reach another device: no remote copies, remote signals or barrier semaphores. Data moves between devices by JAX's collectives and lax.ppermute only.
A program may use at most 128 MiB of HBM per device.

v0:
```python
import jax
import jax.numpy as jnp
from jax import lax
from jax.sharding import PartitionSpec as P

NB = 2


def per_device(integrals, coefficients, owned_tiles, pair_list, amplitudes):
    tile_count = lax.axis_size("tile")
    q_rows, occ_all, ao_count = integrals.shape
    virt_count = coefficients.shape[1]
    tile_width = amplitudes.shape[-1]
    virt_tiles = virt_count // tile_width
    per_dev = pair_list.shape[1]
    occ_batch = occ_all // NB
    total_slots = owned_tiles.shape[1]
    first_slot = lax.axis_index("tile") * per_dev
    positions = jnp.arange(3 * per_dev, dtype=jnp.int32)
    results = []
    for occ_group in range(NB):
        int_block = integrals[:, occ_group * occ_batch : (occ_group + 1) * occ_batch, :].reshape(
            q_rows * occ_batch, ao_count
        )
        half_done = jnp.dot(int_block, coefficients, preferred_element_type=jnp.float32).astype(
            jnp.bfloat16
        )
        half_done = half_done.reshape(q_rows, occ_batch * virt_tiles, tile_width)
        ordered = jnp.take(half_done, owned_tiles[occ_group], axis=1)
        zero_pad = jnp.zeros((q_rows, per_dev, tile_width), jnp.bfloat16)
        padded = jnp.concatenate([zero_pad, ordered, zero_pad], axis=1)
        below_part = padded[:, :total_slots].reshape(q_rows, tile_count, per_dev, tile_width)
        middle = ordered.reshape(q_rows, tile_count, per_dev, tile_width)
        above_part = padded[:, 2 * per_dev :].reshape(q_rows, tile_count, per_dev, tile_width)
        bundle = jnp.concatenate([below_part, middle, above_part], axis=2)
        arrived = lax.all_to_all(bundle, "tile", split_axis=1, concat_axis=0, tiled=True)
        extended = arrived.reshape(q_rows * tile_count, 3 * per_dev, tile_width)
        mine = extended[:, per_dev : 2 * per_dev]
        listed = pair_list[occ_group]
        ext_place = listed - (first_slot - per_dev)
        selector = (
            (ext_place[:, :, None] == positions[None, None, :]) & (listed[:, :, None] >= 0)
        ).astype(jnp.float32)
        amp_tiles = amplitudes[occ_group]
        cross_ints = jnp.einsum("qja,qeb->jeab", mine, extended, preferred_element_type=jnp.float32)
        partial_value = jnp.einsum(
            "jke,jeab->jkab", selector, cross_ints, precision=lax.Precision.HIGHEST
        )
        summed = lax.psum(partial_value, "aux")
        residue = jnp.einsum(
            "jkab,jkbc->jac", summed, amp_tiles.astype(jnp.float32), precision=lax.Precision.HIGHEST
        )
        results.append(residue)
    return jnp.stack(results)


def solution(mesh):
    in_specs = (
        P(("aux", "tile"), None, None),
        P(),
        P(),
        P(None, "tile", None),
        P(None, "tile", None, None, None),
    )
    out_specs = P(None, "tile", None, None)
    return jax.shard_map(
        per_device, mesh=mesh, in_specs=in_specs, out_specs=out_specs, check_vma=False
    )
```

profile of v0, /device:TPU:11, one launch (start us, length us, event | category | flops | bytes accessed | tf_op | source)
XLA Modules:
  0.0 348.4 jit_solution(14311729647392719935)
XLA Ops:
  6.5 0.8 compare_and_fusion.1
  7.3 0.0 copy-start.2
  7.3 9.7 %fusion.28 = (bf16[372,1,2944]{2,1,0:T(2,128)(2,1)S(1)}, bf16[372,1,2944]{2,1,0:T(2,128)(2,1)S(1)}) fusion(bf16[372,2,2944]{2,1,0:T(2,128)(2,1)} %param.7), kind=kLoop, calls=%fused_computation.53 | loop fusion | bytes 8761344 | tf_op jit(solution)/shard_map/slice | solution.py:22
  17.0 0.0 copy-done.2
  17.0 5.1 %convolution_convert_fusion.1 = bf16[372,2048]{1,0:T(8,128)(2,1)S(1)} fusion(bf16[2944,2048]{1,0:T(8,128)(2,1)S(1)} %copy-done.2, bf16[372,1,2944]{2,1,0:T(2,128)(2,1)S(1)} %get-tuple-element.12), kind=kOutput, calls=%fused_computation.9 | convolution fusion | flops 4486569984 | bytes 15772672 | tf_op jit(solution)/shard_map/dot_general | solution.py:25
  22.2 0.4 copy.34
  22.6 0.3 slice.66
  22.8 0.4 copy.17
  23.3 5.1 %convolution_convert_fusion = bf16[372,2048]{1,0:T(8,128)(2,1)S(1)} fusion(bf16[2944,2048]{1,0:T(8,128)(2,1)S(1)} %copy-done.2, bf16[372,1,2944]{2,1,0:T(2,128)(2,1)S(1)} %get-tuple-element.13), kind=kOutput, calls=%fused_computation.8 | convolution fusion | flops 4486569984 | bytes 15772672 | tf_op jit(solution)/shard_map/dot_general | solution.py:25
  28.4 0.4 copy.35
  28.7 0.3 slice.67
  29.0 1.6 copy.22
  30.6 0.8 gather_fusion
  31.4 3.3 gather_fusion.1
  34.7 1.7 broadcast_select_fusion
  36.4 0.4 pad_slice_fusion.3
  36.8 2.4 pad_maximum_fusion
  39.2 5.6 %all-to-all-start = ((bf16[372,8,6,128]{3,0,2,1:T(8,128)(2,1)}), bf16[372,8,6,128]{3,0,2,1:T(8,128)(2,1)}, u32[]{:S(2)}, u32[]{:S(2)}) async-start(bf16[372,8,6,128]{3,0,2,1:T(8,128)(2,1)} %pad_maximum_fusion), calls=%async_computation | async-start | bytes 9240576 | tf_op jit(solution)/shard_map/all_to_all | solution.py:36
  44.9 0.4 pad_slice_fusion.1
  45.2 2.4 pad_maximum_fusion.1
  47.6 0.0 copy-start.1
  47.6 96.8 %all-to-all-done = bf16[372,8,6,128]{3,0,2,1:T(8,128)(2,1)} async-done(((bf16[372,8,6,128]{3,0,2,1:T(8,128)(2,1)}), bf16[372,8,6,128]{3,0,2,1:T(8,128)(2,1)}, u32[]{:S(2)}, u32[]{:S(2)}) %all-to-all-start) | async-done | bytes 4571168 | tf_op jit(solution)/shard_map/all_to_all | solution.py:36
  144.5 8.1 %all-to-all-start.1 = ((bf16[372,8,6,128]{3,0,2,1:T(8,128)(2,1)}), bf16[372,8,6,128]{3,0,2,1:T(8,128)(2,1)}, u32[]{:S(2)}, u32[]{:S(2)}) async-start(bf16[372,8,6,128]{3,0,2,1:T(8,128)(2,1)} %pad_maximum_fusion.1), calls=%async_computation.1 | async-start | bytes 9240576 | tf_op jit(solution)/shard_map/all_to_all | solution.py:36
  152.6 0.0 all-reduce.7.cloned.1.call-start
  152.6 0.0 copy-done.1
  152.6 5.0 %copy.18 = bf16[8,372,1,6,128]{4,1,0,3,2:T(8,128)(2,1)} copy(bf16[8,372,1,6,128]{4,1,3,0,2:T(8,128)(2,1)} %bitcast.11) | data formatting | bytes 9142272 | tf_op jit(solution)/shard_map/all_to_all | solution.py:36
  157.6 7.1 %reshape.109 = bf16[2976,6,128,1]{2,0,1,3:T(8,128)(2,1)} reshape(bf16[8,372,1,6,128]{4,1,0,3,2:T(8,128)(2,1)} %copy.18) | data formatting | bytes 9142272 | tf_op jit(solution)/shard_map/reshape | solution.py:37
  164.7 7.0 %reshape.80 = bf16[2976,6,128]{2,0,1:T(8,128)(2,1)} reshape(bf16[8,372,1,6,128]{4,1,0,3,2:T(8,128)(2,1)} %copy.18) | data formatting | bytes 9142272 | tf_op jit(solution)/shard_map/reshape | solution.py:37
  171.7 80.4 %all-to-all-done.1 = bf16[372,8,6,128]{3,0,2,1:T(8,128)(2,1)} async-done(((bf16[372,8,6,128]{3,0,2,1:T(8,128)(2,1)}), bf16[372,8,6,128]{3,0,2,1:T(8,128)(2,1)}, u32[]{:S(2)}, u32[]{:S(2)}) %all-to-all-start.1) | async-done | bytes 4571168 | tf_op jit(solution)/shard_map/all_to_all | solution.py:36
  252.2 5.0 %copy.23 = bf16[8,372,1,6,128]{4,1,0,3,2:T(8,128)(2,1)} copy(bf16[8,372,1,6,128]{4,1,3,0,2:T(8,128)(2,1)} %bitcast.30) | data formatting | bytes 9142272 | tf_op jit(solution)/shard_map/all_to_all | solution.py:36
  257.2 7.0 %reshape.113 = bf16[2976,6,128,1]{2,0,1,3:T(8,128)(2,1)} reshape(bf16[8,372,1,6,128]{4,1,0,3,2:T(8,128)(2,1)} %copy.23) | data formatting | bytes 9142272 | tf_op jit(solution)/shard_map/reshape | solution.py:37
  264.2 7.0 %reshape.86 = bf16[2976,6,128]{2,0,1:T(8,128)(2,1)} reshape(bf16[8,372,1,6,128]{4,1,0,3,2:T(8,128)(2,1)} %copy.23) | data formatting | bytes 9142272 | tf_op jit(solution)/shard_map/reshape | solution.py:37
  271.2 4.2 %fusion.4 = f32[2,6,128,128]{2,3,0,1:T(8,128)S(1)} fusion(bf16[2976,6,128]{2,0,1:T(8,128)(2,1)} %reshape.80, bf16[2976,6,128,1]{2,0,1,3:T(8,128)(2,1)} %reshape.109), kind=kOutput, calls=%fused_computation.20 | convolution fusion | flops 1170210816 | bytes 6881280 | tf_op jit(solution)/shard_map/qja,qeb->jeab/dot_general | solution.py:45
  275.4 0.4 copy.19
  275.8 4.2 %fusion.7 = f32[2,6,128,128]{2,3,0,1:T(8,128)S(1)} fusion(bf16[2976,6,128]{2,0,1:T(8,128)(2,1)} %reshape.86, bf16[2976,6,128,1]{2,0,1,3:T(8,128)(2,1)} %reshape.113), kind=kOutput, calls=%fused_computation.21 | convolution fusion | flops 1170210816 | bytes 6881280 | tf_op jit(solution)/shard_map/qja,qeb->jeab/dot_general | solution.py:45
  280.0 0.4 copy.24
  280.5 0.0 copy-start
  280.5 1.5 fusion.18
  281.9 1.5 fusion.22
  283.4 0.0 all-reduce.7.cloned.1.call-update
  283.4 54.6 %all-reduce.7.cloned.1.call-done = (f32[2,4,128,128]{3,1,2,0:T(4,128)}, f32[2,4,128,128]{3,1,2,0:T(4,128)}) async-done(((f32[2,4,128,128]{3,1,2,0:T(4,128)}, f32[2,4,128,128]{3,1,2,0:T(4,128)}), (f32[2,4,128,128]{3,1,2,0:T(4,128)}, f32[2,4,128,128]{3,1,2,0:T(4,128)})) %all-reduce.7.cloned.1.call-update) | async-done | bytes 1048592 | tf_op jit(solution)/shard_map/psum | solution.py:49
  338.0 0.0 copy-done
  338.0 1.4 convolution_bitcast_fusion
  339.4 1.4 convolution_bitcast_fusion.1
  340.9 0.7 pad_maximum_fusion.2
  (4 shorter events, 0.0 us)
Async XLA Ops:
  7.3 9.7 %copy-start.2 = (bf16[2944,2048]{1,0:T(8,128)(2,1)S(1)}, bf16[2944,2048]{1,0:T(8,128)(2,1)}, u32[]{:S(2)}) copy-start(bf16[2944,2048]{1,0:T(8,128)(2,1)} %param.8) | copy-start | bytes 36175876
  39.2 105.2 %all-to-all-start = ((bf16[372,8,6,128]{3,0,2,1:T(8,128)(2,1)}), bf16[372,8,6,128]{3,0,2,1:T(8,128)(2,1)}, u32[]{:S(2)}, u32[]{:S(2)}) async-start(bf16[372,8,6,128]{3,0,2,1:T(8,128)(2,1)} %pad_maximum_fusion), calls=%async_computation | async-start | bytes 9240576 | tf_op jit(solution)/shard_map/all_to_all | solution.py:36
  47.6 105.0 %copy-start.1 = (s32[2,2,4]{2,1,0:T(2,128)S(1)}, s32[2,2,4]{2,1,0:T(2,128)}, u32[]{:S(2)}) copy-start(s32[2,2,4]{2,1,0:T(2,128)} %param.10) | copy-start | bytes 196
  144.5 107.7 %all-to-all-start.1 = ((bf16[372,8,6,128]{3,0,2,1:T(8,128)(2,1)}), bf16[372,8,6,128]{3,0,2,1:T(8,128)(2,1)}, u32[]{:S(2)}, u32[]{:S(2)}) async-start(bf16[372,8,6,128]{3,0,2,1:T(8,128)(2,1)} %pad_maximum_fusion.1), calls=%async_computation.1 | async-start | bytes 9240576 | tf_op jit(solution)/shard_map/all_to_all | solution.py:36
  152.6 185.4 %all-reduce.7.cloned.1.call-start = ((), (), s32[]{:S(2)}) async-start(), calls=%async_computation.2 | async-start | bytes 2097152 | tf_op jit(solution)/shard_map/psum | solution.py:49
  280.5 57.6 %copy-start = (bf16[2,2,4,128,128]{4,3,2,1,0:T(8,128)(2,1)S(1)}, bf16[2,2,4,128,128]{4,3,2,1,0:T(8,128)(2,1)}, u32[]{:S(2)}) copy-start(bf16[2,2,4,128,128]{4,3,2,1,0:T(8,128)(2,1)} %param.11) | copy-start | bytes 1572868
Sparse Core Ops, SparseCore 0:
  283.5 54.4 all-reduce.6
where the time goes:
time: 351 us; the launch traced here: 348 us
  waiting for transfers between devices  232 us (66%)
  local copies, waits for them, and re-layouts  56.8 us (16%)
  matrix products  24.3 us (7%)
  starting transfers between devices  13.8 us (4%)
  between operations  13.6 us (4%)
  other arithmetic  8.02 us (2%)
    all_to_all x2, waiting for transfers between devices, per_device(): lax.all_to_all(bundle, 'tile', split_axis=1, concat_axis=0, tiled=True)  177 us
    psum x1, waiting for transfers between devices, per_device(): summed = lax.psum(partial_value, 'aux')  54.6 us
    reshape x4, local copies, waits for them, and re-layouts, per_device(): extended = arrived.reshape(q_rows * tile_count, 3 * per_dev, tile_width)  28.2 us
    all_to_all x2, starting transfers between devices, per_device(): lax.all_to_all(bundle, 'tile', split_axis=1, concat_axis=0, tiled=True)  13.8 us
    dot_general x2, matrix products, per_device(): jnp.dot(int_block, coefficients, preferred_element_type=jnp.float32)  10.2 us
    all_to_all x2, local copies, waits for them, and re-layouts, per_device(): lax.all_to_all(bundle, 'tile', split_axis=1, concat_axis=0, tiled=True)  10 us
    slice x1, local copies, waits for them, and re-layouts, per_device(): integrals[:, occ_group * occ_batch:(occ_group + 1) * occ_batch, :]  9.71 us
    dot_general x2, matrix products, per_device(): jnp.einsum('qja,qeb->jeab', mine, extended, preferred_element_type=jnp.fl...  8.4 us
  transfers between devices with their start and end apart: 3, of which 3 were waited for; matrix products, arithmetic and copies ran while one was open for 6% of the time, Pallas kernels for 0%

commit v1 on v0

v1 whole, which is shorter than its diff:
```python
import functools

import jax
import jax.numpy as jnp
from jax import lax
from jax.experimental import pallas as pl
from jax.experimental.pallas import tpu as pltpu
from jax.sharding import PartitionSpec as P

NB = 2
BAND = 5
AXES = ("aux", "tile")
VMEM = pl.BlockSpec(memory_space=pltpu.VMEM)
SMEM = pl.BlockSpec(memory_space=pltpu.SMEM)
PARAMS = pltpu.CompilerParams(vmem_limit_bytes=56 * 2**20)
F32, BF16 = jnp.float32, jnp.bfloat16


def shape(dims, dtype):
    return jax.ShapeDtypeStruct(tuple(dims), dtype)


def place():
    t = lax.axis_index("tile")
    return lax.axis_index("aux"), t // 2, t % 2


def chip_slot(a, batch):
    return 2 * ((a % 2) ^ batch) + a // 2


def pack_kernel(pairs, amps, zmsg, mine, other, *, npart, width):
    a, z, c = place()
    per_dev = amps.shape[1]
    first = lax.axis_index("tile") * per_dev

    def pack(batch, s, dst):
        offsets, live, seen = [], [], [jnp.int32(0)] * BAND
        for k in range(npart):
            p = pairs[batch, s, k]
            o = p - (first + s) + BAND // 2
            ok = p >= 0
            offsets.append(o)
            live.append(ok)
            for n in range(BAND):
                seen[n] = jnp.where(ok & (o == n), 1, seen[n])
        m = jnp.int32(BAND - 1)
        for n in reversed(range(BAND)):
            m = jnp.where(seen[n] == 0, n, m)
        for j in range(npart):
            want = j + jnp.where(j >= m, 1, 0)
            found, at = jnp.int32(0), jnp.int32(0)
            for k in range(npart):
                hit = live[k] & (offsets[k] == want)
                found = jnp.where(hit, 1, found)
                at = jnp.where(hit, k, at)
            block = amps[batch, s, at]
            dst[pl.ds(j * width, width), :] = jnp.where(found == 1, block, jnp.zeros_like(block))
        code = jnp.full((16, width), m.astype(F32), F32)
        dst[pl.ds(npart * width, 16), :] = code.astype(BF16)

    pack(c ^ (a % 2), a // 2, zmsg)
    for s in range(per_dev):
        pack(c, s, mine.at[s])
        pack(1 - c, s, other.at[s])


def half_kernel(x_ref, c_ref, mine, other, acc, *, batch_occ):
    core = lax.axis_index("tile") % 2
    rows, occ, ao = x_ref.shape
    cols = c_ref.shape[1]
    padded = mine.shape[1]
    prod = jnp.dot(x_ref[...].reshape(rows * occ, ao), c_ref[...], preferred_element_type=F32)
    for n in range(cols // 128):
        acc[n] = prod[:, n * 128 : (n + 1) * 128]
    for i in range(batch_occ):
        for n in range(cols // 128):
            lanes = slice(n * 128, (n + 1) * 128)
            for dst, b in ((mine, core), (other, 1 - core)):
                part = acc[n, pl.ds(b * batch_occ + i, rows, stride=occ), :]
                dst[i, :rows, lanes] = part.astype(BF16)
    for dst in (mine, other):
        dst[:, rows:, :] = jnp.zeros((batch_occ, padded - rows, cols), BF16)


def pair_kernel(owned, y_mine, y_other, out, *, width, step_slots):
    core = lax.axis_index("tile") % 2
    slots = owned.shape[1]
    virt_tiles = y_mine.shape[2] // width
    first = pl.program_id(0) * step_slots

    def tile(ref, s):
        ident = owned[core, jnp.clip(s, 0, slots - 1)]
        col = pl.multiple_of(ident % virt_tiles * width, width)
        return ref[ident // virt_tiles, :, pl.ds(col, width)]

    reach = BAND // 2
    for t in range(0, step_slots, 2):
        total = None
        for ref in (y_mine, y_other):
            tiles = [tile(ref, first + t + n) for n in range(-reach, 2 + reach)]
            left = jnp.concatenate(tiles[reach : reach + 2], axis=1)
            right = jnp.concatenate(tiles, axis=1)
            part = lax.dot_general(left, right, (((0,), (0,)), ((), ())), preferred_element_type=F32)
            total = part if total is None else total + part
        for u in range(2):
            for o in range(BAND):
                out[t + u, o] = total[u * width : (u + 1) * width, (u + o) * width : (u + o + 1) * width]


def residual_kernel(*refs, aux_count, chips, npart, width):
    a, z, c = place()
    ints, mine, other = refs[:3]
    far = refs[3 : 3 + (chips - 1) * aux_count]
    outs = refs[3 + (chips - 1) * aux_count :]
    per_chip = aux_count

    def residual(slot, amp):
        rows = amp[: npart * width]
        m = amp[npart * width :].astype(F32)[:1, :]
        picked = [
            jnp.where(m > j, ints[slot, j], ints[slot, j + 1]) for j in range(npart)
        ]
        picked = jnp.concatenate(picked, axis=1)
        high = picked.astype(BF16)
        low = (picked - high.astype(F32)).astype(BF16)
        return jnp.dot(high, rows, preferred_element_type=F32) + jnp.dot(
            low, rows, preferred_element_type=F32
        )

    for e in range(aux_count):
        peer = a ^ e
        at = peer // 2
        own = jnp.where(peer % 2 == 0, mine[at], other[at])
        outs[e][0] = residual(per_chip * z + chip_slot(peer, c), own)
        for d in range(1, chips):
            amp = far[(d - 1) * aux_count + e][...]
            outs[e][d] = residual(per_chip * (z ^ d) + chip_slot(peer, c), amp)


def sum_split_kernel(*refs, count):
    ins, outs = refs[:count], refs[count:]
    for d, out in enumerate(outs):
        total = ins[0][d]
        for ref in ins[1:]:
            total = total + ref[d]
        out[...] = total


def sum_kernel(*refs):
    total = refs[0][...]
    for ref in refs[1:-1]:
        total = total + ref[...]
    refs[-1][...] = total


def place_kernel(*refs):
    a, _, c = place()
    out = refs[-1]
    for j, ref in enumerate(refs[:-1]):
        src = a ^ j
        out[(src % 2) ^ c, src // 2] = ref[...]


def call(kernel, outs, count, params=PARAMS, **kw):
    return pl.pallas_call(
        kernel, in_specs=[VMEM] * count, out_specs=jax.tree.map(lambda _: VMEM, outs), out_shape=outs,
        compiler_params=params, **kw,
    )


def per_device(integrals, coefficients, owned_tiles, pair_list, amplitudes):
    aux_count, tile_count = lax.axis_size("aux"), lax.axis_size("tile")
    chips = tile_count // 2
    rows, occ, ao = integrals.shape
    virt = coefficients.shape[1]
    batch_occ = occ // NB
    _, per_dev, npart, width, _ = amplitudes.shape
    slots = owned_tiles.shape[1]
    assert aux_count == 2 * per_dev and per_dev == 2

    def exchange(x, target):
        perm = []
        for a in range(aux_count):
            for z in range(chips):
                for c in range(2):
                    a2, z2, c2 = target(a, z, c)
                    perm.append((a * tile_count + 2 * z + c, a2 * tile_count + 2 * z2 + c2))
        return lax.ppermute(x, AXES, perm)

    msg_rows = npart * width + 16
    msg = shape((msg_rows, width), BF16)
    pair = shape((per_dev, msg_rows, width), BF16)
    zmsg, mine, other = pl.pallas_call(
        functools.partial(pack_kernel, npart=npart, width=width),
        in_specs=[SMEM, VMEM], out_specs=[VMEM] * 3, out_shape=[msg, pair, pair], compiler_params=PARAMS,
    )(pair_list, amplitudes)
    along = [
        exchange(zmsg, lambda a, z, c, d=d: (a, z ^ d, c ^ (a % 2))) for d in range(1, chips)
    ]
    other = exchange(other, lambda a, z, c: (a, z, 1 - c))
    far = []
    for got in along:
        far.append(got)
        for e in range(1, aux_count):
            far.append(exchange(got, lambda a, z, c, e=e: (a ^ e, z, c)))

    block = 512
    padded = -(-rows // 16) * 16
    half = shape((batch_occ, padded, virt), BF16)
    half_spec = pl.BlockSpec((batch_occ, padded, block), lambda n: (0, 0, n))
    y_mine, y_send = pl.pallas_call(
        functools.partial(half_kernel, batch_occ=batch_occ),
        grid=(virt // block,),
        in_specs=[pl.BlockSpec((rows, occ, ao), lambda n: (0, 0, 0)), pl.BlockSpec((ao, block), lambda n: (0, n))],
        out_specs=[half_spec, half_spec],
        out_shape=[half, half],
        scratch_shapes=[pltpu.VMEM((block // 128, rows * occ, 128), F32)],
        compiler_params=PARAMS,
        cost_estimate=pl.CostEstimate(
            flops=2 * rows * occ * ao * virt, bytes_accessed=2 * (rows * occ * ao + ao * virt), transcendentals=0
        ),
    )(integrals, coefficients)
    y_other = exchange(y_send, lambda a, z, c: (a, z, 1 - c))

    step_slots = 16
    pair_ints = pl.pallas_call(
        functools.partial(pair_kernel, width=width, step_slots=step_slots),
        grid=(slots // step_slots,),
        in_specs=[SMEM, VMEM, VMEM],
        out_specs=pl.BlockSpec((step_slots, BAND, width, width), lambda n: (n, 0, 0, 0)),
        out_shape=shape((slots, BAND, width, width), F32),
        compiler_params=PARAMS,
    )(owned_tiles, y_mine, y_other)

    shares = call(
        functools.partial(residual_kernel, aux_count=aux_count, chips=chips, npart=npart, width=width),
        [shape((chips, width, width), F32)] * aux_count, 3 + len(far),
    )(pair_ints, mine, other, *far)

    got = [shares[0]]
    for e in range(1, aux_count):
        got.append(exchange(shares[e], lambda a, z, c, e=e: (a ^ e, z, c)))
    sums = call(
        functools.partial(sum_split_kernel, count=aux_count), [shape((width, width), F32)] * chips, aux_count
    )(*got)
    got = [sums[0]] + [exchange(sums[d], lambda a, z, c, d=d: (a, z ^ d, c)) for d in range(1, chips)]
    done = call(sum_kernel, shape((width, width), F32), chips)(*got)
    got = [exchange(done, lambda a, z, c, j=j: (a ^ j, z, (a % 2) ^ c)) for j in range(aux_count)]
    return call(place_kernel, shape((NB, per_dev, width, width), F32), aux_count)(*got)


def solution(mesh):
    in_specs = (
        P(("aux", "tile"), None, None),
        P(),
        P(),
        P(None, "tile", None),
        P(None, "tile", None, None, None),
    )
    out_specs = P(None, "tile", None, None)
    return jax.shard_map(
        per_device, mesh=mesh, in_specs=in_specs, out_specs=out_specs, check_vma=False
    )
```

time: 351 us -> 102 us (0.29)
  the two profiles are of different devices: /device:TPU:11 before, /device:TPU:0 now
where the time goes in v1:
time: 102 us; the launch traced here: 101 us
  Pallas kernels  35.6 us (35%)
  starting transfers between devices  32.7 us (32%)
  waiting for transfers between devices  30 us (29%)
  local copies, waits for them, and re-layouts  2.79 us (3%)
    ppermute x24, starting transfers between devices, exchange(): return lax.ppermute(x, AXES, perm)  32.7 us
    ppermute x24, waiting for transfers between devices, exchange(): return lax.ppermute(x, AXES, perm)  30 us
    pallas_call x1, Pallas kernels, per_device(): pl.pallas_call(functools.partial(half_kernel, batch_occ=batch_occ), grid=...  15.1 us
    pallas_call x1, Pallas kernels, per_device(): pl.pallas_call(functools.partial(pair_kernel, width=width, step_slots=ste...  8.04 us
    pallas_call x1, Pallas kernels, per_device(): call(functools.partial(residual_kernel, aux_count=aux_count, chips=chips,...  5.14 us
    unnamed x48, local copies, waits for them, and re-layouts  2.79 us
    pallas_call x1, Pallas kernels, per_device(): pl.pallas_call(functools.partial(pack_kernel, npart=npart, width=width),...  2.21 us
  transfers between devices with their start and end apart: 24, of which 10 were waited for; matrix products, arithmetic and copies ran while one was open for 0% of the time, Pallas kernels for 10%

profile of v1, /device:TPU:0, one launch (start us, length us, event | category | flops | bytes accessed | tf_op | source)
XLA Modules:
  0.0 101.3 jit_solution(16143576428571308175)
XLA Ops:
  0.0 15.1 %shard_map.55 = (bf16[1,384,2048]{2,1,0:T(8,128)(2,1)}, bf16[1,384,2048]{2,1,0:T(8,128)(2,1)}) custom-call(bf16[372,2,2944]{2,1,0:T(2,128)(2,1)} %x_ref.1, bf16[2944,2048]{1,0:T(8,128)(2,1)} %c_ref.1), custom_call_target="tpu_custom_call" | custom-call | flops 8971616256 | bytes 16439296 | tf_op jit(solution)/shard_map/pallas_call | solution.py:212
  15.1 0.5 collective-permute-start
  15.5 2.2 %shard_map.57 = (bf16[528,128]{1,0:T(8,128)(2,1)}, bf16[2,528,128]{2,1,0:T(8,128)(2,1)}, bf16[2,528,128]{2,1,0:T(8,128)(2,1)}) custom-call(s32[2,2,4]{2,1,0:T(2,128)} %pairs.1, bf16[2,2,4,128,128]{4,3,2,1,0:T(8,128)(2,1)} %amps.1), custom_call_target="tpu_custom_call" | custom-call | tf_op jit(solution)/shard_map/pallas_call | solution.py:194
  17.7 0.1 collective-permute-start.1
  17.8 3.0 %collective-permute-start.2 = (bf16[528,128]{1,0:T(8,128)(2,1)}, bf16[528,128]{1,0:T(8,128)(2,1)S(1)}, u32[]{:S(2)}, u32[]{:S(2)}) collective-permute-start(bf16[528,128]{1,0:T(8,128)(2,1)} %get-tuple-element.22), channel_id=1, source_target_pairs={{0,2},{1,3},{2,0},{3,1},{4,6},{5,7},{6,4},{7,5},{8,11},{9,10},{10,... | collective-permute-start | bytes 405512 | tf_op jit(solution)/shard_map/ppermute | solution.py:189
  20.8 2.6 %collective-permute-start.6 = (bf16[528,128]{1,0:T(8,128)(2,1)}, bf16[528,128]{1,0:T(8,128)(2,1)S(1)}, u32[]{:S(2)}, u32[]{:S(2)}) collective-permute-start(bf16[528,128]{1,0:T(8,128)(2,1)} %get-tuple-element.22), channel_id=1, source_target_pairs={{0,4},{1,5},{2,6},{3,7},{4,0},{5,1},{6,2},{7,3},{8,13},{9,12},{10,... | collective-permute-start | bytes 405512 | tf_op jit(solution)/shard_map/ppermute | solution.py:189
  23.4 0.0 collective-permute-start.10
  23.4 3.2 %collective-permute-done.2.refs_3_ = bf16[528,128]{1,0:T(8,128)(2,1)S(1)} collective-permute-done((bf16[528,128]{1,0:T(8,128)(2,1)}, bf16[528,128]{1,0:T(8,128)(2,1)S(1)}, u32[]{:S(2)}, u32[]{:S(2)}) %collective-permute-start.2) | collective-permute-done | bytes 135200 | tf_op jit(solution)/shard_map/ppermute | solution.py:189
  26.6 2.6 %collective-permute-start.3 = (bf16[528,128]{1,0:T(8,128)(2,1)S(1)}, bf16[528,128]{1,0:T(8,128)(2,1)S(1)}, u32[]{:S(2)}, u32[]{:S(2)}) collective-permute-start(bf16[528,128]{1,0:T(8,128)(2,1)S(1)} %collective-permute-done.2.refs_3_), channel_id=1, source_target_pairs={{0,8},{1,9},{2,10},{3,11},{4,12},{5,13},{6,14},{7,15},{8,0},{9,1},... | collective-permute-start | bytes 405512 | tf_op jit(solution)/shard_map/ppermute | solution.py:189
  29.2 5.0 %collective-permute-done.6.refs_7_ = bf16[528,128]{1,0:T(8,128)(2,1)S(1)} collective-permute-done((bf16[528,128]{1,0:T(8,128)(2,1)}, bf16[528,128]{1,0:T(8,128)(2,1)S(1)}, u32[]{:S(2)}, u32[]{:S(2)}) %collective-permute-start.6) | collective-permute-done | bytes 135200 | tf_op jit(solution)/shard_map/ppermute | solution.py:189
  34.2 1.5 %collective-permute-start.4 = (bf16[528,128]{1,0:T(8,128)(2,1)S(1)}, bf16[528,128]{1,0:T(8,128)(2,1)S(1)}, u32[]{:S(2)}, u32[]{:S(2)}) collective-permute-start(bf16[528,128]{1,0:T(8,128)(2,1)S(1)} %collective-permute-done.2.refs_3_), channel_id=1, source_target_pairs={{0,16},{1,17},{2,18},{3,19},{4,20},{5,21},{6,22},{7,23},{8,24},{9,... | collective-permute-start | bytes 405512 | tf_op jit(solution)/shard_map/ppermute | solution.py:189
  35.7 0.0 collective-permute-done.10.refs_11_
  35.7 0.0 collective-permute-start.5
  35.7 0.0 collective-permute-done.1.refs_2_
  35.8 2.0 %collective-permute-start.7 = (bf16[528,128]{1,0:T(8,128)(2,1)S(1)}, bf16[528,128]{1,0:T(8,128)(2,1)S(1)}, u32[]{:S(2)}, u32[]{:S(2)}) collective-permute-start(bf16[528,128]{1,0:T(8,128)(2,1)S(1)} %collective-permute-done.6.refs_7_), channel_id=1, source_target_pairs={{0,8},{1,9},{2,10},{3,11},{4,12},{5,13},{6,14},{7,15},{8,0},{9,1},... | collective-permute-start | bytes 405512 | tf_op jit(solution)/shard_map/ppermute | solution.py:189
  37.7 0.0 collective-permute-done.3.refs_4_
  37.7 1.5 %collective-permute-start.8 = (bf16[528,128]{1,0:T(8,128)(2,1)S(1)}, bf16[528,128]{1,0:T(8,128)(2,1)S(1)}, u32[]{:S(2)}, u32[]{:S(2)}) collective-permute-start(bf16[528,128]{1,0:T(8,128)(2,1)S(1)} %collective-permute-done.6.refs_7_), channel_id=1, source_target_pairs={{0,16},{1,17},{2,18},{3,19},{4,20},{5,21},{6,22},{7,23},{8,24},{9,... | collective-permute-start | bytes 405512 | tf_op jit(solution)/shard_map/ppermute | solution.py:189
  39.2 3.6 %collective-permute-done.4.refs_5_ = bf16[528,128]{1,0:T(8,128)(2,1)S(1)} collective-permute-done((bf16[528,128]{1,0:T(8,128)(2,1)S(1)}, bf16[528,128]{1,0:T(8,128)(2,1)S(1)}, u32[]{:S(2)}, u32[]{:S(2)}) %collective-permute-start.4) | collective-permute-done | bytes 135200 | tf_op jit(solution)/shard_map/ppermute | solution.py:189
  42.8 0.0 collective-permute-start.9
  42.8 0.0 collective-permute-done.5.refs_6_
  42.9 4.0 %collective-permute-start.11 = (bf16[528,128]{1,0:T(8,128)(2,1)S(1)}, bf16[528,128]{1,0:T(8,128)(2,1)S(1)}, u32[]{:S(2)}, u32[]{:S(2)}) collective-permute-start(bf16[528,128]{1,0:T(8,128)(2,1)S(1)} %collective-permute-done.10.refs_11_), channel_id=1, source_target_pairs={{0,8},{1,9},{2,10},{3,11},{4,12},{5,13},{6,14},{7,15},{8,0},{9,1},... | collective-permute-start | bytes 405512 | tf_op jit(solution)/shard_map/ppermute | solution.py:189
  46.9 0.0 collective-permute-done.7.refs_8_
  46.9 0.0 collective-permute-start.12
  46.9 0.0 collective-permute-done.y_other
  46.9 1.5 %collective-permute-start.13 = (bf16[528,128]{1,0:T(8,128)(2,1)S(1)}, bf16[528,128]{1,0:T(8,128)(2,1)S(1)}, u32[]{:S(2)}, u32[]{:S(2)}) collective-permute-start(bf16[528,128]{1,0:T(8,128)(2,1)S(1)} %collective-permute-done.10.refs_11_), channel_id=1, source_target_pairs={{0,24},{1,25},{2,26},{3,27},{4,28},{5,29},{6,30},{7,31},{8,16},{9,... | collective-permute-start | bytes 405512 | tf_op jit(solution)/shard_map/ppermute | solution.py:189
  48.4 8.0 %shard_map.56.refs_0_ = f32[16,5,128,128]{3,2,1,0:T(8,128)} custom-call(s32[2,16]{1,0:T(2,128)} %owned.1, bf16[1,384,2048]{2,1,0:T(8,128)(2,1)} %get-tuple-element.18.y_mine, bf16[1,384,2048]{2,1,0:T(8,128)(2,1)} %copy-done), custom_call_target="tpu_custom_call" | custom-call | tf_op jit(solution)/shard_map/pallas_call | solution.py:227
  56.5 0.0 collective-permute-done.8.refs_9_
  56.5 0.0 collective-permute-done.9.refs_10_
  56.5 0.0 collective-permute-done.11.refs_12_
  56.5 0.0 collective-permute-done.12.refs_13_
  56.5 0.0 collective-permute-done.13.refs_14_
  56.6 0.5 copy-done.12
  57.1 0.1 copy-done.13
  57.2 0.0 copy-done.14
  57.2 0.1 copy-done.15
  57.3 0.0 copy-done.16
  57.3 5.1 %shard_map.58 = (f32[4,128,128]{2,1,0:T(8,128)}, f32[4,128,128]{2,1,0:T(8,128)}, f32[4,128,128]{2,1,0:T(8,128)}, f32[4,128,128]{2,1,0:T(8,128)}) custom-call(f32[16,5,128,128]{3,2,1,0:T(8,128)} %shard_map.56.refs_0_, bf16[2,528,128]{2,1,0:T(8,128)(2,1)} %get-tuple-element.20.refs_1_, bf16[2,528,128]{2,1,0:T(8,128)(2,1)} %copy-done.1, ...), custom_call_target="tpu_custom_call" | custom-call | tf_op jit(solution)/shard_map/pallas_call | solution.py:236
  62.5 1.9 %collective-permute-start.14 = (f32[4,128,128]{2,1,0:T(8,128)}, f32[4,128,128]{2,1,0:T(8,128)S(1)}, u32[]{:S(2)}, u32[]{:S(2)}) collective-permute-start(f32[4,128,128]{2,1,0:T(8,128)} %get-tuple-element.24), channel_id=1, source_target_pairs={{0,8},{1,9},{2,10},{3,11},{4,12},{5,13},{6,14},{7,15},{8,0},{9,1},... | collective-permute-start | bytes 786440 | tf_op jit(solution)/shard_map/ppermute | solution.py:189
  64.4 0.1 collective-permute-start.15
  64.5 1.5 %collective-permute-start.16 = (f32[4,128,128]{2,1,0:T(8,128)}, f32[4,128,128]{2,1,0:T(8,128)S(1)}, u32[]{:S(2)}, u32[]{:S(2)}) collective-permute-start(f32[4,128,128]{2,1,0:T(8,128)} %get-tuple-element.26), channel_id=1, source_target_pairs={{0,24},{1,25},{2,26},{3,27},{4,28},{5,29},{6,30},{7,31},{8,16},{9,... | collective-permute-start | bytes 786440 | tf_op jit(solution)/shard_map/ppermute | solution.py:189
  65.9 5.1 %collective-permute-done.14.refs_1_ = f32[4,128,128]{2,1,0:T(8,128)S(1)} collective-permute-done((f32[4,128,128]{2,1,0:T(8,128)}, f32[4,128,128]{2,1,0:T(8,128)S(1)}, u32[]{:S(2)}, u32[]{:S(2)}) %collective-permute-start.14) | collective-permute-done | bytes 262176 | tf_op jit(solution)/shard_map/ppermute | solution.py:189
  71.0 3.4 %collective-permute-done.15.refs_2_ = f32[4,128,128]{2,1,0:T(8,128)S(1)} collective-permute-done((f32[4,128,128]{2,1,0:T(8,128)}, f32[4,128,128]{2,1,0:T(8,128)S(1)}, u32[]{:S(2)}, u32[]{:S(2)}) %collective-permute-start.15) | collective-permute-done | bytes 262176 | tf_op jit(solution)/shard_map/ppermute | solution.py:189
  74.4 0.0 collective-permute-done.16.refs_3_
  74.4 0.7 copy-done.3
  75.1 0.1 copy-done.4
  75.2 1.9 %shard_map.59 = (f32[128,128]{1,0:T(8,128)}, f32[128,128]{1,0:T(8,128)}, f32[128,128]{1,0:T(8,128)}, f32[128,128]{1,0:T(8,128)}) custom-call(f32[4,128,128]{2,1,0:T(8,128)} %get-tuple-element.23.refs_0_, f32[4,128,128]{2,1,0:T(8,128)} %copy-done.2, f32[4,128,128]{2,1,0:T(8,128)} %copy-done.3, f32[4,128,128]{2,1,0:T(8,128)} %copy-done.4), custom_call_target="tpu_custom_call" | custom-call | tf_op jit(solution)/shard_map/pallas_call | solution.py:244
  77.1 1.8 %collective-permute-start.17 = (f32[128,128]{1,0:T(8,128)}, f32[128,128]{1,0:T(8,128)S(1)}, u32[]{:S(2)}, u32[]{:S(2)}) collective-permute-start(f32[128,128]{1,0:T(8,128)} %get-tuple-element.28), channel_id=1, source_target_pairs={{0,2},{1,3},{2,0},{3,1},{4,6},{5,7},{6,4},{7,5},{8,10},{9,11},{10,... | collective-permute-start | bytes 196616 | tf_op jit(solution)/shard_map/ppermute | solution.py:189
  79.0 2.2 %collective-permute-start.18 = (f32[128,128]{1,0:T(8,128)}, f32[128,128]{1,0:T(8,128)S(1)}, u32[]{:S(2)}, u32[]{:S(2)}) collective-permute-start(f32[128,128]{1,0:T(8,128)} %get-tuple-element.29), channel_id=1, source_target_pairs={{0,4},{1,5},{2,6},{3,7},{4,0},{5,1},{6,2},{7,3},{8,12},{9,13},{10,... | collective-permute-start | bytes 196616 | tf_op jit(solution)/shard_map/ppermute | solution.py:189
  81.2 0.8 collective-permute-start.19
  82.0 0.0 collective-permute-done.17.refs_1_
  82.0 2.3 %collective-permute-done.18.refs_2_ = f32[128,128]{1,0:T(8,128)S(1)} collective-permute-done((f32[128,128]{1,0:T(8,128)}, f32[128,128]{1,0:T(8,128)S(1)}, u32[]{:S(2)}, u32[]{:S(2)}) %collective-permute-start.18) | collective-permute-done | bytes 65568 | tf_op jit(solution)/shard_map/ppermute | solution.py:189
  84.3 3.1 %collective-permute-done.19.refs_3_ = f32[128,128]{1,0:T(8,128)S(1)} collective-permute-done((f32[128,128]{1,0:T(8,128)}, f32[128,128]{1,0:T(8,128)S(1)}, u32[]{:S(2)}, u32[]{:S(2)}) %collective-permute-start.19) | collective-permute-done | bytes 65568 | tf_op jit(solution)/shard_map/ppermute | solution.py:189
  87.5 0.6 copy-done.19
  88.1 1.6 %shard_map.60 = f32[128,128]{1,0:T(8,128)} custom-call(f32[128,128]{1,0:T(8,128)} %get-tuple-element.27.refs_0_, f32[128,128]{1,0:T(8,128)} %copy-done.17, f32[128,128]{1,0:T(8,128)} %copy-done.18, f32[128,128]{1,0:T(8,128)} %copy-done.19), custom_call_target="tpu_custom_call" | custom-call | tf_op jit(solution)/shard_map/pallas_call | solution.py:248
  89.7 1.5 %collective-permute-start.20 = (f32[128,128]{1,0:T(8,128)}, f32[128,128]{1,0:T(8,128)S(1)}, u32[]{:S(2)}, u32[]{:S(2)}) collective-permute-start(f32[128,128]{1,0:T(8,128)} %shard_map.60), channel_id=1, source_target_pairs={{0,0},{1,1},{2,2},{3,3},{4,4},{5,5},{6,6},{7,7},{8,9},{9,8},{10,11... | collective-permute-start | bytes 196616 | tf_op jit(solution)/shard_map/ppermute | solution.py:189
  91.1 1.9 %collective-permute-start.21 = (f32[128,128]{1,0:T(8,128)}, f32[128,128]{1,0:T(8,128)S(1)}, u32[]{:S(2)}, u32[]{:S(2)}) collective-permute-start(f32[128,128]{1,0:T(8,128)} %shard_map.60), channel_id=1, source_target_pairs={{0,8},{1,9},{2,10},{3,11},{4,12},{5,13},{6,14},{7,15},{8,1},{9,0},... | collective-permute-start | bytes 196616 | tf_op jit(solution)/shard_map/ppermute | solution.py:189
  93.1 0.5 collective-permute-start.22
  93.6 1.1 %collective-permute-start.23 = (f32[128,128]{1,0:T(8,128)}, f32[128,128]{1,0:T(8,128)S(1)}, u32[]{:S(2)}, u32[]{:S(2)}) collective-permute-start(f32[128,128]{1,0:T(8,128)} %shard_map.60), channel_id=1, source_target_pairs={{0,24},{1,25},{2,26},{3,27},{4,28},{5,29},{6,30},{7,31},{8,17},{9,... | collective-permute-start | bytes 196616 | tf_op jit(solution)/shard_map/ppermute | solution.py:189
  94.7 0.0 collective-permute-done.20.refs_0_
  94.7 1.1 %collective-permute-done.21.refs_1_ = f32[128,128]{1,0:T(8,128)S(1)} collective-permute-done((f32[128,128]{1,0:T(8,128)}, f32[128,128]{1,0:T(8,128)S(1)}, u32[]{:S(2)}, u32[]{:S(2)}) %collective-permute-start.21) | collective-permute-done | bytes 65568 | tf_op jit(solution)/shard_map/ppermute | solution.py:189
  95.8 1.7 %collective-permute-done.22.refs_2_ = f32[128,128]{1,0:T(8,128)S(1)} collective-permute-done((f32[128,128]{1,0:T(8,128)}, f32[128,128]{1,0:T(8,128)S(1)}, u32[]{:S(2)}, u32[]{:S(2)}) %collective-permute-start.22) | collective-permute-done | bytes 65568 | tf_op jit(solution)/shard_map/ppermute | solution.py:189
  97.5 1.4 %collective-permute-done.23.refs_3_ = f32[128,128]{1,0:T(8,128)S(1)} collective-permute-done((f32[128,128]{1,0:T(8,128)}, f32[128,128]{1,0:T(8,128)S(1)}, u32[]{:S(2)}, u32[]{:S(2)}) %collective-permute-start.23) | collective-permute-done | bytes 65568 | tf_op jit(solution)/shard_map/ppermute | solution.py:189
  99.0 0.6 copy-done.23
  99.6 1.7 %shard_map.61 = f32[2,2,128,128]{3,2,1,0:T(8,128)} custom-call(f32[128,128]{1,0:T(8,128)} %copy-done.20, f32[128,128]{1,0:T(8,128)} %copy-done.21, f32[128,128]{1,0:T(8,128)} %copy-done.22, f32[128,128]{1,0:T(8,128)} %copy-done.23), custom_call_target="tpu_custom_call" | custom-call | tf_op jit(solution)/shard_map/pallas_call | solution.py:250
  (39 shorter events, 0.1 us)
Async XLA Ops:
  15.1 31.8 %collective-permute-start = (bf16[1,384,2048]{2,1,0:T(8,128)(2,1)}, bf16[1,384,2048]{2,1,0:T(8,128)(2,1)S(1)}, u32[]{:S(2)}, u32[]{:S(2)}) collective-permute-start(bf16[1,384,2048]{2,1,0:T(8,128)(2,1)} %get-tuple-element.19), channel_id=1, source_target_pairs={{0,1},{1,0},{2,3},{3,2},{4,5},{5,4},{6,7},{7,6},{8,9},{9,8},{10,11... | collective-permute-start | bytes 4718600 | tf_op jit(solution)/shard_map/ppermute | solution.py:189
  17.7 18.0 %collective-permute-start.1 = (bf16[2,528,128]{2,1,0:T(8,128)(2,1)}, bf16[2,528,128]{2,1,0:T(8,128)(2,1)S(1)}, u32[]{:S(2)}, u32[]{:S(2)}) collective-permute-start(bf16[2,528,128]{2,1,0:T(8,128)(2,1)} %get-tuple-element.21), channel_id=1, source_target_pairs={{0,1},{1,0},{2,3},{3,2},{4,5},{5,4},{6,7},{7,6},{8,9},{9,8},{10,11... | collective-permute-start | bytes 811016 | tf_op jit(solution)/shard_map/ppermute | solution.py:189
  17.8 8.8 %collective-permute-start.2 = (bf16[528,128]{1,0:T(8,128)(2,1)}, bf16[528,128]{1,0:T(8,128)(2,1)S(1)}, u32[]{:S(2)}, u32[]{:S(2)}) collective-permute-start(bf16[528,128]{1,0:T(8,128)(2,1)} %get-tuple-element.22), channel_id=1, source_target_pairs={{0,2},{1,3},{2,0},{3,1},{4,6},{5,7},{6,4},{7,5},{8,11},{9,10},{10,... | collective-permute-start | bytes 405512 | tf_op jit(solution)/shard_map/ppermute | solution.py:189
  20.8 13.4 %collective-permute-start.6 = (bf16[528,128]{1,0:T(8,128)(2,1)}, bf16[528,128]{1,0:T(8,128)(2,1)S(1)}, u32[]{:S(2)}, u32[]{:S(2)}) collective-permute-start(bf16[528,128]{1,0:T(8,128)(2,1)} %get-tuple-element.22), channel_id=1, source_target_pairs={{0,4},{1,5},{2,6},{3,7},{4,0},{5,1},{6,2},{7,3},{8,13},{9,12},{10,... | collective-permute-start | bytes 405512 | tf_op jit(solution)/shard_map/ppermute | solution.py:189
  23.4 12.3 %collective-permute-start.10 = (bf16[528,128]{1,0:T(8,128)(2,1)}, bf16[528,128]{1,0:T(8,128)(2,1)S(1)}, u32[]{:S(2)}, u32[]{:S(2)}) collective-permute-start(bf16[528,128]{1,0:T(8,128)(2,1)} %get-tuple-element.22), channel_id=1, source_target_pairs={{0,6},{1,7},{2,4},{3,5},{4,2},{5,3},{6,0},{7,1},{8,15},{9,14},{10,... | collective-permute-start | bytes 405512 | tf_op jit(solution)/shard_map/ppermute | solution.py:189
  26.6 29.9 %copy-start.5 = (bf16[528,128]{1,0:T(8,128)(2,1)}, bf16[528,128]{1,0:T(8,128)(2,1)S(1)}, u32[]{:S(2)}) copy-start(bf16[528,128]{1,0:T(8,128)(2,1)S(1)} %collective-permute-done.2.refs_3_) | copy-start | bytes 405508
  26.6 11.1 %collective-permute-start.3 = (bf16[528,128]{1,0:T(8,128)(2,1)S(1)}, bf16[528,128]{1,0:T(8,128)(2,1)S(1)}, u32[]{:S(2)}, u32[]{:S(2)}) collective-permute-start(bf16[528,128]{1,0:T(8,128)(2,1)S(1)} %collective-permute-done.2.refs_3_), channel_id=1, source_target_pairs={{0,8},{1,9},{2,10},{3,11},{4,12},{5,13},{6,14},{7,15},{8,0},{9,1},... | collective-permute-start | bytes 405512 | tf_op jit(solution)/shard_map/ppermute | solution.py:189
  34.2 22.4 %copy-start.6 = (bf16[528,128]{1,0:T(8,128)(2,1)}, bf16[528,128]{1,0:T(8,128)(2,1)S(1)}, u32[]{:S(2)}) copy-start(bf16[528,128]{1,0:T(8,128)(2,1)S(1)} %collective-permute-done.6.refs_7_) | copy-start | bytes 405508
  34.2 8.6 %collective-permute-start.4 = (bf16[528,128]{1,0:T(8,128)(2,1)S(1)}, bf16[528,128]{1,0:T(8,128)(2,1)S(1)}, u32[]{:S(2)}, u32[]{:S(2)}) collective-permute-start(bf16[528,128]{1,0:T(8,128)(2,1)S(1)} %collective-permute-done.2.refs_3_), channel_id=1, source_target_pairs={{0,16},{1,17},{2,18},{3,19},{4,20},{5,21},{6,22},{7,23},{8,24},{9,... | collective-permute-start | bytes 405512 | tf_op jit(solution)/shard_map/ppermute | solution.py:189
  35.7 20.8 %copy-start.7 = (bf16[528,128]{1,0:T(8,128)(2,1)}, bf16[528,128]{1,0:T(8,128)(2,1)S(1)}, u32[]{:S(2)}) copy-start(bf16[528,128]{1,0:T(8,128)(2,1)S(1)} %collective-permute-done.10.refs_11_) | copy-start | bytes 405508
  35.7 7.1 %collective-permute-start.5 = (bf16[528,128]{1,0:T(8,128)(2,1)S(1)}, bf16[528,128]{1,0:T(8,128)(2,1)S(1)}, u32[]{:S(2)}, u32[]{:S(2)}) collective-permute-start(bf16[528,128]{1,0:T(8,128)(2,1)S(1)} %collective-permute-done.2.refs_3_), channel_id=1, source_target_pairs={{0,24},{1,25},{2,26},{3,27},{4,28},{5,29},{6,30},{7,31},{8,16},{9,... | collective-permute-start | bytes 405512 | tf_op jit(solution)/shard_map/ppermute | solution.py:189
  35.7 20.8 %copy-start.1 = (bf16[2,528,128]{2,1,0:T(8,128)(2,1)}, bf16[2,528,128]{2,1,0:T(8,128)(2,1)S(1)}, u32[]{:S(2)}) copy-start(bf16[2,528,128]{2,1,0:T(8,128)(2,1)S(1)} %collective-permute-done.1.refs_2_) | copy-start | bytes 811012
  35.8 11.1 %collective-permute-start.7 = (bf16[528,128]{1,0:T(8,128)(2,1)S(1)}, bf16[528,128]{1,0:T(8,128)(2,1)S(1)}, u32[]{:S(2)}, u32[]{:S(2)}) collective-permute-start(bf16[528,128]{1,0:T(8,128)(2,1)S(1)} %collective-permute-done.6.refs_7_), channel_id=1, source_target_pairs={{0,8},{1,9},{2,10},{3,11},{4,12},{5,13},{6,14},{7,15},{8,0},{9,1},... | collective-permute-start | bytes 405512 | tf_op jit(solution)/shard_map/ppermute | solution.py:189
  37.7 18.9 %copy-start.8 = (bf16[528,128]{1,0:T(8,128)(2,1)}, bf16[528,128]{1,0:T(8,128)(2,1)S(1)}, u32[]{:S(2)}) copy-start(bf16[528,128]{1,0:T(8,128)(2,1)S(1)} %collective-permute-done.3.refs_4_) | copy-start | bytes 405508
  37.7 18.8 %collective-permute-start.8 = (bf16[528,128]{1,0:T(8,128)(2,1)S(1)}, bf16[528,128]{1,0:T(8,128)(2,1)S(1)}, u32[]{:S(2)}, u32[]{:S(2)}) collective-permute-start(bf16[528,128]{1,0:T(8,128)(2,1)S(1)} %collective-permute-done.6.refs_7_), channel_id=1, source_target_pairs={{0,16},{1,17},{2,18},{3,19},{4,20},{5,21},{6,22},{7,23},{8,24},{9,... | collective-permute-start | bytes 405512 | tf_op jit(solution)/shard_map/ppermute | solution.py:189
  42.8 13.8 %copy-start.9 = (bf16[528,128]{1,0:T(8,128)(2,1)}, bf16[528,128]{1,0:T(8,128)(2,1)S(1)}, u32[]{:S(2)}) copy-start(bf16[528,128]{1,0:T(8,128)(2,1)S(1)} %collective-permute-done.4.refs_5_) | copy-start | bytes 405508
  42.8 13.6 %collective-permute-start.9 = (bf16[528,128]{1,0:T(8,128)(2,1)S(1)}, bf16[528,128]{1,0:T(8,128)(2,1)S(1)}, u32[]{:S(2)}, u32[]{:S(2)}) collective-permute-start(bf16[528,128]{1,0:T(8,128)(2,1)S(1)} %collective-permute-done.6.refs_7_), channel_id=1, source_target_pairs={{0,24},{1,25},{2,26},{3,27},{4,28},{5,29},{6,30},{7,31},{8,16},{9,... | collective-permute-start | bytes 405512 | tf_op jit(solution)/shard_map/ppermute | solution.py:189
  42.9 13.8 %copy-start.10 = (bf16[528,128]{1,0:T(8,128)(2,1)}, bf16[528,128]{1,0:T(8,128)(2,1)S(1)}, u32[]{:S(2)}) copy-start(bf16[528,128]{1,0:T(8,128)(2,1)S(1)} %collective-permute-done.5.refs_6_) | copy-start | bytes 405508
  42.9 13.6 %collective-permute-start.11 = (bf16[528,128]{1,0:T(8,128)(2,1)S(1)}, bf16[528,128]{1,0:T(8,128)(2,1)S(1)}, u32[]{:S(2)}, u32[]{:S(2)}) collective-permute-start(bf16[528,128]{1,0:T(8,128)(2,1)S(1)} %collective-permute-done.10.refs_11_), channel_id=1, source_target_pairs={{0,8},{1,9},{2,10},{3,11},{4,12},{5,13},{6,14},{7,15},{8,0},{9,1},... | collective-permute-start | bytes 405512 | tf_op jit(solution)/shard_map/ppermute | solution.py:189
  46.9 9.8 %copy-start.11 = (bf16[528,128]{1,0:T(8,128)(2,1)}, bf16[528,128]{1,0:T(8,128)(2,1)S(1)}, u32[]{:S(2)}) copy-start(bf16[528,128]{1,0:T(8,128)(2,1)S(1)} %collective-permute-done.7.refs_8_) | copy-start | bytes 405508
  46.9 9.6 %collective-permute-start.12 = (bf16[528,128]{1,0:T(8,128)(2,1)S(1)}, bf16[528,128]{1,0:T(8,128)(2,1)S(1)}, u32[]{:S(2)}, u32[]{:S(2)}) collective-permute-start(bf16[528,128]{1,0:T(8,128)(2,1)S(1)} %collective-permute-done.10.refs_11_), channel_id=1, source_target_pairs={{0,16},{1,17},{2,18},{3,19},{4,20},{5,21},{6,22},{7,23},{8,24},{9,... | collective-permute-start | bytes 405512 | tf_op jit(solution)/shard_map/ppermute | solution.py:189
  46.9 1.5 %copy-start = (bf16[1,384,2048]{2,1,0:T(8,128)(2,1)}, bf16[1,384,2048]{2,1,0:T(8,128)(2,1)S(1)}, u32[]{:S(2)}) copy-start(bf16[1,384,2048]{2,1,0:T(8,128)(2,1)S(1)} %collective-permute-done.y_other) | copy-start | bytes 4718596
  46.9 9.6 %collective-permute-start.13 = (bf16[528,128]{1,0:T(8,128)(2,1)S(1)}, bf16[528,128]{1,0:T(8,128)(2,1)S(1)}, u32[]{:S(2)}, u32[]{:S(2)}) collective-permute-start(bf16[528,128]{1,0:T(8,128)(2,1)S(1)} %collective-permute-done.10.refs_11_), channel_id=1, source_target_pairs={{0,24},{1,25},{2,26},{3,27},{4,28},{5,29},{6,30},{7,31},{8,16},{9,... | collective-permute-start | bytes 405512 | tf_op jit(solution)/shard_map/ppermute | solution.py:189
  56.5 0.7 copy-start.12
  56.5 0.7 copy-start.13
  56.5 0.7 copy-start.14
  56.5 0.8 copy-start.15
  56.5 0.8 copy-start.16
  62.5 8.6 %collective-permute-start.14 = (f32[4,128,128]{2,1,0:T(8,128)}, f32[4,128,128]{2,1,0:T(8,128)S(1)}, u32[]{:S(2)}, u32[]{:S(2)}) collective-permute-start(f32[4,128,128]{2,1,0:T(8,128)} %get-tuple-element.24), channel_id=1, source_target_pairs={{0,8},{1,9},{2,10},{3,11},{4,12},{5,13},{6,14},{7,15},{8,0},{9,1},... | collective-permute-start | bytes 786440 | tf_op jit(solution)/shard_map/ppermute | solution.py:189
  64.4 10.0 %collective-permute-start.15 = (f32[4,128,128]{2,1,0:T(8,128)}, f32[4,128,128]{2,1,0:T(8,128)S(1)}, u32[]{:S(2)}, u32[]{:S(2)}) collective-permute-start(f32[4,128,128]{2,1,0:T(8,128)} %get-tuple-element.25), channel_id=1, source_target_pairs={{0,16},{1,17},{2,18},{3,19},{4,20},{5,21},{6,22},{7,23},{8,24},{9,... | collective-permute-start | bytes 786440 | tf_op jit(solution)/shard_map/ppermute | solution.py:189
  64.5 10.0 %collective-permute-start.16 = (f32[4,128,128]{2,1,0:T(8,128)}, f32[4,128,128]{2,1,0:T(8,128)S(1)}, u32[]{:S(2)}, u32[]{:S(2)}) collective-permute-start(f32[4,128,128]{2,1,0:T(8,128)} %get-tuple-element.26), channel_id=1, source_target_pairs={{0,24},{1,25},{2,26},{3,27},{4,28},{5,29},{6,30},{7,31},{8,16},{9,... | collective-permute-start | bytes 786440 | tf_op jit(solution)/shard_map/ppermute | solution.py:189
  71.0 3.4 %copy-start.2 = (f32[4,128,128]{2,1,0:T(8,128)}, f32[4,128,128]{2,1,0:T(8,128)S(1)}, u32[]{:S(2)}) copy-start(f32[4,128,128]{2,1,0:T(8,128)S(1)} %collective-permute-done.14.refs_1_) | copy-start | bytes 786436
  74.4 0.7 copy-start.3
  74.4 0.8 copy-start.4
  77.1 4.9 %collective-permute-start.17 = (f32[128,128]{1,0:T(8,128)}, f32[128,128]{1,0:T(8,128)S(1)}, u32[]{:S(2)}, u32[]{:S(2)}) collective-permute-start(f32[128,128]{1,0:T(8,128)} %get-tuple-element.28), channel_id=1, source_target_pairs={{0,2},{1,3},{2,0},{3,1},{4,6},{5,7},{6,4},{7,5},{8,10},{9,11},{10,... | collective-permute-start | bytes 196616 | tf_op jit(solution)/shard_map/ppermute | solution.py:189
  79.0 5.4 %collective-permute-start.18 = (f32[128,128]{1,0:T(8,128)}, f32[128,128]{1,0:T(8,128)S(1)}, u32[]{:S(2)}, u32[]{:S(2)}) collective-permute-start(f32[128,128]{1,0:T(8,128)} %get-tuple-element.29), channel_id=1, source_target_pairs={{0,4},{1,5},{2,6},{3,7},{4,0},{5,1},{6,2},{7,3},{8,12},{9,13},{10,... | collective-permute-start | bytes 196616 | tf_op jit(solution)/shard_map/ppermute | solution.py:189
  81.2 6.3 %collective-permute-start.19 = (f32[128,128]{1,0:T(8,128)}, f32[128,128]{1,0:T(8,128)S(1)}, u32[]{:S(2)}, u32[]{:S(2)}) collective-permute-start(f32[128,128]{1,0:T(8,128)} %get-tuple-element.30), channel_id=1, source_target_pairs={{0,6},{1,7},{2,4},{3,5},{4,2},{5,3},{6,0},{7,1},{8,14},{9,15},{10,... | collective-permute-start | bytes 196616 | tf_op jit(solution)/shard_map/ppermute | solution.py:189
  82.0 5.4 %copy-start.17 = (f32[128,128]{1,0:T(8,128)}, f32[128,128]{1,0:T(8,128)S(1)}, u32[]{:S(2)}) copy-start(f32[128,128]{1,0:T(8,128)S(1)} %collective-permute-done.17.refs_1_) | copy-start | bytes 196612
  84.3 3.1 %copy-start.18 = (f32[128,128]{1,0:T(8,128)}, f32[128,128]{1,0:T(8,128)S(1)}, u32[]{:S(2)}) copy-start(f32[128,128]{1,0:T(8,128)S(1)} %collective-permute-done.18.refs_2_) | copy-start | bytes 196612
  87.5 0.6 copy-start.19
  89.7 5.1 %collective-permute-start.20 = (f32[128,128]{1,0:T(8,128)}, f32[128,128]{1,0:T(8,128)S(1)}, u32[]{:S(2)}, u32[]{:S(2)}) collective-permute-start(f32[128,128]{1,0:T(8,128)} %shard_map.60), channel_id=1, source_target_pairs={{0,0},{1,1},{2,2},{3,3},{4,4},{5,5},{6,6},{7,7},{8,9},{9,8},{10,11... | collective-permute-start | bytes 196616 | tf_op jit(solution)/shard_map/ppermute | solution.py:189
  91.1 4.7 %collective-permute-start.21 = (f32[128,128]{1,0:T(8,128)}, f32[128,128]{1,0:T(8,128)S(1)}, u32[]{:S(2)}, u32[]{:S(2)}) collective-permute-start(f32[128,128]{1,0:T(8,128)} %shard_map.60), channel_id=1, source_target_pairs={{0,8},{1,9},{2,10},{3,11},{4,12},{5,13},{6,14},{7,15},{8,1},{9,0},... | collective-permute-start | bytes 196616 | tf_op jit(solution)/shard_map/ppermute | solution.py:189
  93.1 4.5 %collective-permute-start.22 = (f32[128,128]{1,0:T(8,128)}, f32[128,128]{1,0:T(8,128)S(1)}, u32[]{:S(2)}, u32[]{:S(2)}) collective-permute-start(f32[128,128]{1,0:T(8,128)} %shard_map.60), channel_id=1, source_target_pairs={{0,16},{1,17},{2,18},{3,19},{4,20},{5,21},{6,22},{7,23},{8,25},{9,... | collective-permute-start | bytes 196616 | tf_op jit(solution)/shard_map/ppermute | solution.py:189
  93.6 5.4 %collective-permute-start.23 = (f32[128,128]{1,0:T(8,128)}, f32[128,128]{1,0:T(8,128)S(1)}, u32[]{:S(2)}, u32[]{:S(2)}) collective-permute-start(f32[128,128]{1,0:T(8,128)} %shard_map.60), channel_id=1, source_target_pairs={{0,24},{1,25},{2,26},{3,27},{4,28},{5,29},{6,30},{7,31},{8,17},{9,... | collective-permute-start | bytes 196616 | tf_op jit(solution)/shard_map/ppermute | solution.py:189
  94.7 4.2 %copy-start.20 = (f32[128,128]{1,0:T(8,128)}, f32[128,128]{1,0:T(8,128)S(1)}, u32[]{:S(2)}) copy-start(f32[128,128]{1,0:T(8,128)S(1)} %collective-permute-done.20.refs_0_) | copy-start | bytes 196612
  95.8 3.1 %copy-start.21 = (f32[128,128]{1,0:T(8,128)}, f32[128,128]{1,0:T(8,128)S(1)}, u32[]{:S(2)}) copy-start(f32[128,128]{1,0:T(8,128)S(1)} %collective-permute-done.21.refs_1_) | copy-start | bytes 196612
  97.5 1.4 %copy-start.22 = (f32[128,128]{1,0:T(8,128)}, f32[128,128]{1,0:T(8,128)S(1)}, u32[]{:S(2)}) copy-start(f32[128,128]{1,0:T(8,128)S(1)} %collective-permute-done.22.refs_2_) | copy-start | bytes 196612
  99.0 0.6 copy-start.23

commit v2 on v1

v2 whole, which is shorter than its diff:
```python
import functools

import jax
import jax.numpy as jnp
from jax import lax
from jax.experimental import pallas as pl
from jax.experimental.pallas import tpu as pltpu
from jax.sharding import PartitionSpec as P

NB = 2
BAND = 5
REACH = BAND // 2
HALF_FLOPS = 10**9
MIB = 2**20
AXES = ("aux", "tile")
VMEM = pl.BlockSpec(memory_space=pltpu.VMEM)
SMEM = pl.BlockSpec(memory_space=pltpu.SMEM)
ANY = pl.BlockSpec(memory_space=pl.ANY)
HBM = pl.BlockSpec(memory_space=pltpu.HBM)
F32, BF16 = jnp.float32, jnp.bfloat16


def shape(dims, dtype):
    return jax.ShapeDtypeStruct(tuple(dims), dtype)


def place():
    t = lax.axis_index("tile")
    return lax.axis_index("aux"), t // 2, t % 2


def chip_slot(a, batch):
    return 2 * ((a % 2) ^ batch) + a // 2


def call(kernel, outs, specs, limit, flops=10**6, **kw):
    return pl.pallas_call(
        kernel, in_specs=specs, out_specs=jax.tree.map(lambda _: VMEM, outs), out_shape=outs,
        compiler_params=pltpu.CompilerParams(vmem_limit_bytes=limit * MIB),
        cost_estimate=pl.CostEstimate(flops=flops, bytes_accessed=10**5, transcendentals=0), **kw,
    )


def pack_kernel(pairs, amps, zmsg, mine, other, *, npart, width):
    a, z, c = place()
    per_dev = amps.shape[1]
    first = lax.axis_index("tile") * per_dev

    def pack(batch, s, dst):
        offsets, live, seen = [], [], [jnp.int32(0)] * BAND
        for k in range(npart):
            p = pairs[batch, s, k]
            o = p - (first + s) + REACH
            ok = p >= 0
            offsets.append(o)
            live.append(ok)
            for n in range(BAND):
                seen[n] = jnp.where(ok & (o == n), 1, seen[n])
        m = jnp.int32(BAND - 1)
        for n in reversed(range(BAND)):
            m = jnp.where(seen[n] == 0, n, m)
        for j in range(npart):
            want = j + jnp.where(j >= m, 1, 0)
            found, at = jnp.int32(0), jnp.int32(0)
            for k in range(npart):
                hit = live[k] & (offsets[k] == want)
                found = jnp.where(hit, 1, found)
                at = jnp.where(hit, k, at)
            block = amps[batch, s, at]
            dst[pl.ds(j * width, width), :] = jnp.where(found == 1, block, jnp.zeros_like(block))
        code = jnp.full((16, width), m.astype(F32), F32)
        dst[pl.ds(npart * width, 16), :] = code.astype(BF16)

    pack(c ^ (a % 2), a // 2, zmsg)
    for s in range(per_dev):
        pack(c, s, mine.at[s])
        pack(1 - c, s, other.at[s])


def half_columns(x_ref, c_ref, start, mine, other, acc, batch_occ):
    core = lax.axis_index("tile") % 2
    rows, occ, ao = x_ref.shape
    cols = mine.shape[2]
    padded = mine.shape[1]
    prod = jnp.dot(
        x_ref[...].reshape(rows * occ, ao), c_ref[:, start : start + cols], preferred_element_type=F32
    )
    for n in range(cols // 128):
        acc[n] = prod[:, n * 128 : (n + 1) * 128]
    for i in range(batch_occ):
        for n in range(cols // 128):
            lanes = slice(n * 128, (n + 1) * 128)
            for dst, b in ((mine, core), (other, 1 - core)):
                part = acc[n, pl.ds(b * batch_occ + i, rows, stride=occ), :]
                dst[i, :rows, lanes] = part.astype(BF16)
    for dst in (mine, other):
        dst[:, rows:, :] = jnp.zeros((batch_occ, padded - rows, cols), BF16)


def first_half_kernel(x_ref, c_hbm, _, mine, other, c_ref, acc, sems, *, batch_occ):
    cols = mine.shape[2]
    parts = c_ref.shape[1] // cols
    get_c = [
        pltpu.make_async_copy(
            c_hbm.at[:, pl.ds(n * cols, cols)], c_ref.at[:, pl.ds(n * cols, cols)], sems.at[n]
        )
        for n in range(parts)
    ]
    for copy in get_c:
        copy.start()
    get_c[0].wait()
    half_columns(x_ref, c_ref, 0, mine, other, acc, batch_occ)
    for copy in get_c[1:]:
        copy.wait()


def half_kernel(x_ref, c_ref, *rest, batch_occ, start):
    mine, other, acc = rest[-3:]
    half_columns(x_ref, c_ref, start, mine, other, acc, batch_occ)


def pair_kernel(owned, *refs, parts, width):
    core = lax.axis_index("tile") % 2
    slots = owned.shape[1]
    y_mine, y_other, (out, tiles, place_of) = refs[:parts], refs[parts : 2 * parts], refs[2 * parts :]
    batch_occ, padded, cols = y_mine[0].shape
    for s in range(slots):
        place_of[owned[core, s]] = s + REACH
    for n in (0, 1, slots + REACH, slots + REACH + 1):
        tiles[:, n * width : (n + 1) * width] = jnp.zeros((2 * padded, width), BF16)
    for i in range(batch_occ):
        for h in range(parts):
            for n in range(cols // width):
                ident = (i * parts + h) * (cols // width) + n
                lanes = pl.ds(pl.multiple_of(place_of[ident] * width, width), width)
                for src, group in enumerate((y_mine, y_other)):
                    rows = slice(src * padded, (src + 1) * padded)
                    tiles[rows, lanes] = group[h][i, :, n * width : (n + 1) * width]
    for t in range(0, slots, 2):
        left = tiles[:, (t + REACH) * width : (t + REACH + 2) * width]
        right = tiles[:, t * width : (t + 2 + 2 * REACH) * width]
        total = lax.dot_general(left, right, (((0,), (0,)), ((), ())), preferred_element_type=F32)
        for u in range(2):
            for o in range(BAND):
                out[t + u, o] = total[u * width : (u + 1) * width, (u + o) * width : (u + o + 1) * width]


def partial_residual(ints, slot, amp, npart, width):
    rows = amp[: npart * width]
    m = amp[npart * width :].astype(F32)[:1, :]
    picked = [jnp.where(m > j, ints[slot, j], ints[slot, j + 1]) for j in range(npart)]
    picked = jnp.concatenate(picked, axis=1)
    high = picked.astype(BF16)
    low = (picked - high.astype(F32)).astype(BF16)
    return jnp.dot(high, rows, preferred_element_type=F32) + jnp.dot(low, rows, preferred_element_type=F32)


def own_kernel(ints, mine, other, out, *, aux_count, npart, width):
    _, z, c = place()
    per_dev = mine.shape[0]
    for s in range(per_dev):
        for src, core in ((mine, c), (other, 1 - c)):
            at = per_dev * core + s
            out[at] = partial_residual(ints, aux_count * z + at, src[s], npart, width)


def far_kernel(ints, *refs, aux_count, distances, npart, width):
    a, z, c = place()
    outs = refs[aux_count:]
    for n, d in enumerate(distances):
        for e in range(aux_count):
            at = chip_slot(a ^ e, c)
            outs[n][at] = partial_residual(ints, aux_count * (z ^ d) + at, refs[e][n], npart, width)


def join_kernel(*refs):
    *ins, _, out = refs
    for n, ref in enumerate(ins):
        out[n] = ref[...]


def sum_kernel(*refs):
    total = refs[0][...]
    for ref in refs[1:-1]:
        total = total + ref[...]
    refs[-1][...] = total


def sum_split_kernel(*refs):
    *ins, keep, give = refs
    core = lax.axis_index("tile") % 2
    per_dev = keep.shape[0]
    for s in range(per_dev):
        for dst, owner in ((keep, core), (give, 1 - core)):
            total = ins[0][per_dev * owner + s]
            for ref in ins[1:]:
                total = total + ref[per_dev * owner + s]
            dst[s] = total


def place_kernel(keep, got, out):
    core = lax.axis_index("tile") % 2
    out[core] = keep[...]
    out[1 - core] = got[...]


def per_device(integrals, coefficients, owned_tiles, pair_list, amplitudes):
    aux_count, tile_count = lax.axis_size("aux"), lax.axis_size("tile")
    chips = tile_count // 2
    rows, occ, ao = integrals.shape
    virt = coefficients.shape[1]
    batch_occ = occ // NB
    _, per_dev, npart, width, _ = amplitudes.shape
    slots = owned_tiles.shape[1]
    assert aux_count == 2 * per_dev and per_dev == 2

    def exchange(x, target):
        perm = []
        for a in range(aux_count):
            for z in range(chips):
                for c in range(2):
                    a2, z2, c2 = target(a, z, c)
                    perm.append((a * tile_count + 2 * z + c, a2 * tile_count + 2 * z2 + c2))
        return lax.ppermute(x, AXES, perm)

    def swap(x):
        return exchange(x, lambda a, z, c: (a, z, 1 - c))

    def round_plane(x):
        return [exchange(x, lambda a, z, c, e=e: (a ^ e, z, c)) for e in range(1, aux_count)]

    parts = 4
    cols = virt // parts
    padded = -(-rows // 16) * 16

    msg_rows = npart * width + 16
    msg = shape((msg_rows, width), BF16)
    pair = shape((per_dev, msg_rows, width), BF16)
    zmsg, mine, other = call(
        functools.partial(pack_kernel, npart=npart, width=width), [msg, pair, pair], [SMEM, VMEM], 12,
            )(pair_list, amplitudes)
    along = [exchange(zmsg, lambda a, z, c, d=d: (a, z ^ d, c ^ (a % 2))) for d in range(1, chips)]
    other = swap(other)
    batches = [range(1, chips - 1), range(chips - 1, chips)]
    far = []

    half = shape((batch_occ, padded, cols), BF16)
    acc = pltpu.VMEM((cols // 128, rows * occ, 128), F32)
    y_mine, y_other = [], []
    after = [zmsg]
    for n in range(parts):
        if n == 0:
            got, send, c = call(
                functools.partial(first_half_kernel, batch_occ=batch_occ),
                [half, half, shape(coefficients.shape, BF16)],
                [VMEM, HBM, ANY], 28, flops=HALF_FLOPS, scratch_shapes=[acc, pltpu.SemaphoreType.DMA((parts,))],
            )(integrals, coefficients, *after)
        else:
            got, send = call(
                functools.partial(half_kernel, batch_occ=batch_occ, start=n * cols),
                [half, half], [VMEM, VMEM] + [ANY] * len(after), 12, flops=HALF_FLOPS, scratch_shapes=[acc],
            )(integrals, c, *after)
        y_mine.append(got)
        y_other.append(swap(send))
        after = [got]
        if n == 2:
            after = far[0][1:]
        if n < len(batches):
            distances = batches[n]
            joined = call(
                join_kernel, shape((len(distances), msg_rows, width), BF16), [VMEM] * len(distances) + [ANY], 12
            )(*[along[d - 1] for d in distances], got)
            far.append([joined] + round_plane(joined))
            after = [joined]

    ints_shape = shape((slots, BAND, width, width), F32)
    tiles_shape = (2 * padded, (slots + BAND - 1) * width)
    ints = call(
        functools.partial(pair_kernel, parts=parts, width=width), ints_shape, [SMEM] + [VMEM] * (2 * parts),
        8 + 4 * slots * BAND * width * width // MIB + 2 * tiles_shape[0] * tiles_shape[1] // MIB,
        scratch_shapes=[pltpu.VMEM(tiles_shape, BF16), pltpu.SMEM((slots,), jnp.int32)],
    )(owned_tiles, *y_mine, *y_other)

    chip_part = shape((aux_count, width, width), F32)
    sizes = dict(aux_count=aux_count, npart=npart, width=width)
    got = [call(functools.partial(own_kernel, **sizes), chip_part, [VMEM] * 3, 12)(ints, mine, other)]
    for distances, amps in zip(batches, far):
        shares = call(
            functools.partial(far_kernel, distances=distances, **sizes),
            [chip_part] * len(distances), [VMEM] * (1 + aux_count), 16,
        )(ints, *amps)
        got += [exchange(share, lambda a, z, c, d=d: (a, z ^ d, c)) for d, share in zip(distances, shares)]
    column = call(sum_kernel, chip_part, [VMEM] * chips, 12)(*got)

    core_part = shape((per_dev, width, width), F32)
    keep, give = call(sum_split_kernel, [core_part] * 2, [VMEM] * aux_count, 12)(column, *round_plane(column))
    return call(place_kernel, shape((NB, per_dev, width, width), F32), [VMEM] * 2, 8)(keep, swap(give))


def solution(mesh):
    in_specs = (
        P(("aux", "tile"), None, None),
        P(),
        P(),
        P(None, "tile", None),
        P(None, "tile", None, None, None),
    )
    out_specs = P(None, "tile", None, None)
    return jax.shard_map(
        per_device, mesh=mesh, in_specs=in_specs, out_specs=out_specs, check_vma=False
    )
```

time: 102 us -> 83 us (0.81)
  the two profiles are of different devices: /device:TPU:0 before, /device:TPU:11 now
where the time goes in v2:
time: 83 us; the launch traced here: 82.8 us
  waiting for transfers between devices  39.1 us (47%)
  Pallas kernels  20.6 us (25%)
  starting transfers between devices  19 us (23%)
  local copies, waits for them, and re-layouts  3.97 us (5%)
    ppermute x21, waiting for transfers between devices, exchange(): return lax.ppermute(x, AXES, perm)  39.1 us
    ppermute x21, starting transfers between devices, exchange(): return lax.ppermute(x, AXES, perm)  19 us
    pallas_call x3, Pallas kernels, per_device(): call(functools.partial(half_kernel, batch_occ=batch_occ, start=n * cols),...  8.3 us
    pallas_call x1, Pallas kernels, per_device(): call(functools.partial(first_half_kernel, batch_occ=batch_occ), [half, ha...  4.81 us
    pallas_call x1, Pallas kernels, per_device(): call(functools.partial(pair_kernel, parts=parts, width=width), ints_shape...  4.05 us
    unnamed x10, local copies, waits for them, and re-layouts  3.97 us
  transfers between devices with their start and end apart: 21, of which 8 were waited for; matrix products, arithmetic and copies ran while one was open for 0% of the time, Pallas kernels for 23%

profile of v2, /device:TPU:11, one launch (start us, length us, event | category | flops | bytes accessed | tf_op | source)
XLA Modules:
  0.0 82.8 jit_solution(10021645899510003448)
XLA Ops:
  0.0 0.0 copy-start.2
  0.0 1.0 %copy-done.2 = bf16[2,2,4,128,128]{4,3,2,1,0:T(8,128)(2,1)S(1)} copy-done((bf16[2,2,4,128,128]{4,3,2,1,0:T(8,128)(2,1)S(1)}, bf16[2,2,4,128,128]{4,3,2,1,0:T(8,128)(2,1)}, u32[]{:S(2)}) %copy-start.2) | copy-done | bytes 524312
  1.0 0.0 copy-start.3
  1.0 0.7 copy-done.3
  1.7 1.0 %shard_map.55 = (bf16[528,128]{1,0:T(8,128)(2,1)S(1)}, bf16[2,528,128]{2,1,0:T(8,128)(2,1)S(1)}, bf16[2,528,128]{2,1,0:T(8,128)(2,1)S(1)}) custom-call(s32[2,2,4]{2,1,0:T(2,128)S(1)} %copy-done.3, bf16[2,2,4,128,128]{4,3,2,1,0:T(8,128)(2,1)S(1)} %copy-done.2), custom_call_target="tpu_custom_call" | custom-call | flops 1000000 | bytes 100000 | tf_op jit(solution)/shard_map/pallas_call | solution.py:239
  2.7 2.9 %collective-permute-start.1 = (bf16[528,128]{1,0:T(8,128)(2,1)S(1)}, bf16[528,128]{1,0:T(8,128)(2,1)S(1)}, u32[]{:S(2)}, u32[]{:S(2)}) collective-permute-start(bf16[528,128]{1,0:T(8,128)(2,1)S(1)} %get-tuple-element.21._), channel_id=1, source_target_pairs={{0,4},{1,5},{2,6},{3,7},{4,0},{5,1},{6,2},{7,3},{8,13},{9,12},{10,... | collective-permute-start | bytes 405512 | tf_op jit(solution)/shard_map/ppermute | solution.py:224
  5.6 0.0 collective-permute-start
  5.6 0.0 copy-start
  5.6 2.2 %copy-done = bf16[372,2,2944]{2,1,0:T(2,128)(2,1)S(1)} copy-done((bf16[372,2,2944]{2,1,0:T(2,128)(2,1)S(1)}, bf16[372,2,2944]{2,1,0:T(2,128)(2,1)}, u32[]{:S(2)}) %copy-start) | copy-done | bytes 4380696
  7.9 0.0 copy-start.1
  7.9 4.8 %shard_map.56 = (bf16[1,384,512]{2,1,0:T(8,128)(2,1)S(1)}, bf16[1,384,512]{2,1,0:T(8,128)(2,1)S(1)}, bf16[2944,2048]{1,0:T(8,128)(2,1)S(1)}) custom-call(bf16[372,2,2944]{2,1,0:T(2,128)(2,1)S(1)} %copy-done, bf16[2944,2048]{1,0:T(8,128)(2,1)} %c_hbm.1, bf16[528,128]{1,0:T(8,128)(2,1)S(1)} %get-tuple-element.21._), custom_call_target="tpu_custom_call" | custom-call | flops 1000000000 | bytes 100000 | tf_op jit(solution)/shard_map/pallas_call | solution.py:253
  12.7 0.0 collective-permute-done.1.refs_1_
  12.7 0.2 collective-permute-done.refs_0_
  12.9 0.7 collective-permute-start.5
  13.6 0.6 collective-permute-start.4
  14.3 1.3 %collective-permute-start.3 = (bf16[2,528,128]{2,1,0:T(8,128)(2,1)S(1)}, bf16[2,528,128]{2,1,0:T(8,128)(2,1)S(1)}, u32[]{:S(2)}, u32[]{:S(2)}) collective-permute-start(bf16[2,528,128]{2,1,0:T(8,128)(2,1)S(1)} %shard_map.57.rest_0_.refs_0_), channel_id=1, source_target_pairs={{0,8},{1,9},{2,10},{3,11},{4,12},{5,13},{6,14},{7,15},{8,0},{9,1},... | collective-permute-start | bytes 811016 | tf_op jit(solution)/shard_map/ppermute | solution.py:224
  15.6 1.3 %collective-permute-start.2 = (bf16[528,128]{1,0:T(8,128)(2,1)S(1)}, bf16[528,128]{1,0:T(8,128)(2,1)S(1)}, u32[]{:S(2)}, u32[]{:S(2)}) collective-permute-start(bf16[528,128]{1,0:T(8,128)(2,1)S(1)} %get-tuple-element.21._), channel_id=1, source_target_pairs={{0,6},{1,7},{2,4},{3,5},{4,2},{5,3},{6,0},{7,1},{8,15},{9,14},{10,... | collective-permute-start | bytes 405512 | tf_op jit(solution)/shard_map/ppermute | solution.py:224
  16.9 0.0 collective-permute-start.6
  16.9 0.0 copy-done.1
  16.9 2.8 %shard_map.58 = (bf16[1,384,512]{2,1,0:T(8,128)(2,1)S(1)}, bf16[1,384,512]{2,1,0:T(8,128)(2,1)S(1)}) custom-call(bf16[372,2,2944]{2,1,0:T(2,128)(2,1)S(1)} %copy-done.1, bf16[2944,2048]{1,0:T(8,128)(2,1)S(1)} %get-tuple-element.23.c_ref, bf16[2,528,128]{2,1,0:T(8,128)(2,1)S(1)} %shard_map.57.rest_0_.refs_0_), custom_call_target="tpu_custom_call" | custom-call | flops 1000000000 | bytes 100000 | tf_op jit(solution)/shard_map/pallas_call | solution.py:259
  19.7 4.5 %collective-permute-done.2.refs_0_ = bf16[528,128]{1,0:T(8,128)(2,1)S(1)} collective-permute-done((bf16[528,128]{1,0:T(8,128)(2,1)S(1)}, bf16[528,128]{1,0:T(8,128)(2,1)S(1)}, u32[]{:S(2)}, u32[]{:S(2)}) %collective-permute-start.2) | collective-permute-done | bytes 135200 | tf_op jit(solution)/shard_map/ppermute | solution.py:224
  24.2 2.8 %shard_map.60 = (bf16[1,384,512]{2,1,0:T(8,128)(2,1)S(1)}, bf16[1,384,512]{2,1,0:T(8,128)(2,1)S(1)}) custom-call(bf16[372,2,2944]{2,1,0:T(2,128)(2,1)S(1)} %copy-done.1, bf16[2944,2048]{1,0:T(8,128)(2,1)S(1)} %get-tuple-element.23.c_ref, bf16[1,528,128]{2,1,0:T(8,128)(2,1)S(1)} %shard_map.59.rest_0_.refs_0_), custom_call_target="tpu_custom_call" | custom-call | flops 1000000000 | bytes 100000 | tf_op jit(solution)/shard_map/pallas_call | solution.py:259
  27.0 0.0 copy-start.4
  27.0 1.0 %collective-permute-start.8 = (bf16[1,384,512]{2,1,0:T(8,128)(2,1)S(1)}, bf16[1,384,512]{2,1,0:T(8,128)(2,1)S(1)}, u32[]{:S(2)}, u32[]{:S(2)}) collective-permute-start(bf16[1,384,512]{2,1,0:T(8,128)(2,1)S(1)} %get-tuple-element.29), channel_id=1, source_target_pairs={{0,1},{1,0},{2,3},{3,2},{4,5},{5,4},{6,7},{7,6},{8,9},{9,8},{10,11... | collective-permute-start | bytes 1179656 | tf_op jit(solution)/shard_map/ppermute | solution.py:224
  27.9 0.0 collective-permute-done.5.rest_2_.refs_3_
  27.9 0.1 collective-permute-start.7
  28.0 0.0 collective-permute-done.4.rest_1_.refs_2_
  28.0 0.0 collective-permute-done.3.rest_0_.refs_1_
  28.0 2.8 %shard_map.61 = (bf16[1,384,512]{2,1,0:T(8,128)(2,1)S(1)}, bf16[1,384,512]{2,1,0:T(8,128)(2,1)S(1)}) custom-call(bf16[372,2,2944]{2,1,0:T(2,128)(2,1)S(1)} %copy-done.1, bf16[2944,2048]{1,0:T(8,128)(2,1)S(1)} %get-tuple-element.23.c_ref, bf16[2,528,128]{2,1,0:T(8,128)(2,1)S(1)} %collective-permute-done.3.rest_0_.refs_1_, ...), custom_call_target="tpu_custom_call" | custom-call | flops 1000000000 | bytes 100000 | tf_op jit(solution)/shard_map/pallas_call | solution.py:259
  30.8 0.7 collective-permute-start.9
  31.5 0.6 collective-permute-start.15
  32.1 0.0 collective-permute-done.6.refs_4_
  32.1 0.6 collective-permute-start.14
  32.6 0.0 collective-permute-done.8.refs_6_
  32.6 1.5 %collective-permute-start.13 = (bf16[1,528,128]{2,1,0:T(8,128)(2,1)S(1)}, bf16[1,528,128]{2,1,0:T(8,128)(2,1)S(1)}, u32[]{:S(2)}, u32[]{:S(2)}) collective-permute-start(bf16[1,528,128]{2,1,0:T(8,128)(2,1)S(1)} %shard_map.59.rest_0_.refs_0_), channel_id=1, source_target_pairs={{0,8},{1,9},{2,10},{3,11},{4,12},{5,13},{6,14},{7,15},{8,0},{9,1},... | collective-permute-start | bytes 405512 | tf_op jit(solution)/shard_map/ppermute | solution.py:224
  34.1 0.0 collective-permute-done.7.refs_5_
  34.2 0.9 %collective-permute-start.10 = (bf16[2,528,128]{2,1,0:T(8,128)(2,1)S(1)}, bf16[2,528,128]{2,1,0:T(8,128)(2,1)S(1)}, u32[]{:S(2)}, u32[]{:S(2)}) collective-permute-start(bf16[2,528,128]{2,1,0:T(8,128)(2,1)S(1)} %get-tuple-element.32), channel_id=1, source_target_pairs={{0,1},{1,0},{2,3},{3,2},{4,5},{5,4},{6,7},{7,6},{8,9},{9,8},{10,11... | collective-permute-start | bytes 811016 | tf_op jit(solution)/shard_map/ppermute | solution.py:224
  35.1 0.0 collective-permute-done.9.refs_7_
  35.1 0.0 copy-done.4
  35.1 4.0 %shard_map.62.ints = f32[16,5,128,128]{3,2,1,0:T(8,128)S(1)} custom-call(s32[2,16]{1,0:T(2,128)S(1)} %copy-done.4, bf16[1,384,512]{2,1,0:T(8,128)(2,1)S(1)} %get-tuple-element.22.refs_2_.refs_0_, bf16[1,384,512]{2,1,0:T(8,128)(2,1)S(1)} %get-tuple-element.24.refs_1_, bf16[1,384,512]{2,1,0:T(8,128)(2,1)S(1)} %get-tuple-element.25.refs_2_, ...), custom_call_target="tpu_custom_call" | custom-call | flops 1000000 | bytes 100000 | tf_op jit(solution)/shard_map/pallas_call | solution.py:278
  39.1 0.7 shard_map.64
  39.9 1.1 %collective-permute-start.11 = (f32[4,128,128]{2,1,0:T(8,128)S(1)}, f32[4,128,128]{2,1,0:T(8,128)S(1)}, u32[]{:S(2)}, u32[]{:S(2)}) collective-permute-start(f32[4,128,128]{2,1,0:T(8,128)S(1)} %get-tuple-element.33), channel_id=1, source_target_pairs={{0,2},{1,3},{2,0},{3,1},{4,6},{5,7},{6,4},{7,5},{8,10},{9,11},{10,... | collective-permute-start | bytes 786440 | tf_op jit(solution)/shard_map/ppermute | solution.py:224
  41.0 0.0 collective-permute-done.15.refs_3_
  41.0 1.1 %collective-permute-start.12 = (f32[4,128,128]{2,1,0:T(8,128)S(1)}, f32[4,128,128]{2,1,0:T(8,128)S(1)}, u32[]{:S(2)}, u32[]{:S(2)}) collective-permute-start(f32[4,128,128]{2,1,0:T(8,128)S(1)} %get-tuple-element.34), channel_id=1, source_target_pairs={{0,4},{1,5},{2,6},{3,7},{4,0},{5,1},{6,2},{7,3},{8,12},{9,13},{10,... | collective-permute-start | bytes 786440 | tf_op jit(solution)/shard_map/ppermute | solution.py:224
  42.0 0.0 collective-permute-done.14.refs_2_
  42.1 0.0 collective-permute-done.13.refs_1_
  42.1 0.4 shard_map.65
  42.5 0.6 collective-permute-start.16
  43.1 0.0 collective-permute-done.10.other
  43.1 0.4 shard_map.63.refs_0_
  43.5 8.2 %collective-permute-done.11.refs_1_ = f32[4,128,128]{2,1,0:T(8,128)S(1)} collective-permute-done((f32[4,128,128]{2,1,0:T(8,128)S(1)}, f32[4,128,128]{2,1,0:T(8,128)S(1)}, u32[]{:S(2)}, u32[]{:S(2)}) %collective-permute-start.11) | collective-permute-done | bytes 262176 | tf_op jit(solution)/shard_map/ppermute | solution.py:224
  51.7 7.2 %collective-permute-done.12.refs_2_ = f32[4,128,128]{2,1,0:T(8,128)S(1)} collective-permute-done((f32[4,128,128]{2,1,0:T(8,128)S(1)}, f32[4,128,128]{2,1,0:T(8,128)S(1)}, u32[]{:S(2)}, u32[]{:S(2)}) %collective-permute-start.12) | collective-permute-done | bytes 262176 | tf_op jit(solution)/shard_map/ppermute | solution.py:224
  58.9 6.7 %collective-permute-done.16.refs_3_ = f32[4,128,128]{2,1,0:T(8,128)S(1)} collective-permute-done((f32[4,128,128]{2,1,0:T(8,128)S(1)}, f32[4,128,128]{2,1,0:T(8,128)S(1)}, u32[]{:S(2)}, u32[]{:S(2)}) %collective-permute-start.16) | collective-permute-done | bytes 262176 | tf_op jit(solution)/shard_map/ppermute | solution.py:224
  65.6 0.1 shard_map.66.refs_0_
  65.7 0.6 collective-permute-start.19
  66.3 0.6 collective-permute-start.18
  66.9 1.5 %collective-permute-start.17 = (f32[4,128,128]{2,1,0:T(8,128)S(1)}, f32[4,128,128]{2,1,0:T(8,128)S(1)}, u32[]{:S(2)}, u32[]{:S(2)}) collective-permute-start(f32[4,128,128]{2,1,0:T(8,128)S(1)} %shard_map.66.refs_0_), channel_id=1, source_target_pairs={{0,8},{1,9},{2,10},{3,11},{4,12},{5,13},{6,14},{7,15},{8,0},{9,1},... | collective-permute-start | bytes 786440 | tf_op jit(solution)/shard_map/ppermute | solution.py:224
  68.4 5.0 %collective-permute-done.19.refs_3_ = f32[4,128,128]{2,1,0:T(8,128)S(1)} collective-permute-done((f32[4,128,128]{2,1,0:T(8,128)S(1)}, f32[4,128,128]{2,1,0:T(8,128)S(1)}, u32[]{:S(2)}, u32[]{:S(2)}) %collective-permute-start.19) | collective-permute-done | bytes 262176 | tf_op jit(solution)/shard_map/ppermute | solution.py:224
  73.5 6.3 %collective-permute-done.18.refs_2_ = f32[4,128,128]{2,1,0:T(8,128)S(1)} collective-permute-done((f32[4,128,128]{2,1,0:T(8,128)S(1)}, f32[4,128,128]{2,1,0:T(8,128)S(1)}, u32[]{:S(2)}, u32[]{:S(2)}) %collective-permute-start.18) | collective-permute-done | bytes 262176 | tf_op jit(solution)/shard_map/ppermute | solution.py:224
  79.7 0.0 collective-permute-done.17.refs_1_
  79.8 1.3 %collective-permute-start.20 = (f32[2,128,128]{2,1,0:T(8,128)S(1)}, f32[2,128,128]{2,1,0:T(8,128)S(1)}, u32[]{:S(2)}, u32[]{:S(2)}) collective-permute-start(f32[2,128,128]{2,1,0:T(8,128)S(1)} %get-tuple-element.36), channel_id=1, source_target_pairs={{0,1},{1,0},{2,3},{3,2},{4,5},{5,4},{6,7},{7,6},{8,9},{9,8},{10,11... | collective-permute-start | bytes 393224 | tf_op jit(solution)/shard_map/ppermute | solution.py:224
  81.1 1.0 %collective-permute-done.20.got = f32[2,128,128]{2,1,0:T(8,128)S(1)} collective-permute-done((f32[2,128,128]{2,1,0:T(8,128)S(1)}, f32[2,128,128]{2,1,0:T(8,128)S(1)}, u32[]{:S(2)}, u32[]{:S(2)}) %collective-permute-start.20) | collective-permute-done | bytes 131104 | tf_op jit(solution)/shard_map/ppermute | solution.py:224
  82.1 0.7 shard_map.68
  (3 shorter events, 0.1 us)
Async XLA Ops:
  0.0 1.0 %copy-start.2 = (bf16[2,2,4,128,128]{4,3,2,1,0:T(8,128)(2,1)S(1)}, bf16[2,2,4,128,128]{4,3,2,1,0:T(8,128)(2,1)}, u32[]{:S(2)}) copy-start(bf16[2,2,4,128,128]{4,3,2,1,0:T(8,128)(2,1)} %amps.1) | copy-start | bytes 1572868
  1.0 0.7 copy-start.3
  2.7 10.0 %collective-permute-start.1 = (bf16[528,128]{1,0:T(8,128)(2,1)S(1)}, bf16[528,128]{1,0:T(8,128)(2,1)S(1)}, u32[]{:S(2)}, u32[]{:S(2)}) collective-permute-start(bf16[528,128]{1,0:T(8,128)(2,1)S(1)} %get-tuple-element.21._), channel_id=1, source_target_pairs={{0,4},{1,5},{2,6},{3,7},{4,0},{5,1},{6,2},{7,3},{8,13},{9,12},{10,... | collective-permute-start | bytes 405512 | tf_op jit(solution)/shard_map/ppermute | solution.py:224
  5.6 7.2 %collective-permute-start = (bf16[528,128]{1,0:T(8,128)(2,1)S(1)}, bf16[528,128]{1,0:T(8,128)(2,1)S(1)}, u32[]{:S(2)}, u32[]{:S(2)}) collective-permute-start(bf16[528,128]{1,0:T(8,128)(2,1)S(1)} %get-tuple-element.21._), channel_id=1, source_target_pairs={{0,2},{1,3},{2,0},{3,1},{4,6},{5,7},{6,4},{7,5},{8,11},{9,10},{10,... | collective-permute-start | bytes 405512 | tf_op jit(solution)/shard_map/ppermute | solution.py:224
  5.6 2.2 %copy-start = (bf16[372,2,2944]{2,1,0:T(2,128)(2,1)S(1)}, bf16[372,2,2944]{2,1,0:T(2,128)(2,1)}, u32[]{:S(2)}) copy-start(bf16[372,2,2944]{2,1,0:T(2,128)(2,1)} %x_ref.7) | copy-start | bytes 13142020
  7.9 9.0 %copy-start.1 = (bf16[372,2,2944]{2,1,0:T(2,128)(2,1)S(1)}, bf16[372,2,2944]{2,1,0:T(2,128)(2,1)}, u32[]{:S(2)}) copy-start(bf16[372,2,2944]{2,1,0:T(2,128)(2,1)} %x_ref.7) | copy-start | bytes 13142020
  12.9 15.1 %collective-permute-start.5 = (bf16[2,528,128]{2,1,0:T(8,128)(2,1)S(1)}, bf16[2,528,128]{2,1,0:T(8,128)(2,1)S(1)}, u32[]{:S(2)}, u32[]{:S(2)}) collective-permute-start(bf16[2,528,128]{2,1,0:T(8,128)(2,1)S(1)} %shard_map.57.rest_0_.refs_0_), channel_id=1, source_target_pairs={{0,24},{1,25},{2,26},{3,27},{4,28},{5,29},{6,30},{7,31},{8,16},{9,... | collective-permute-start | bytes 811016 | tf_op jit(solution)/shard_map/ppermute | solution.py:224
  13.6 14.4 %collective-permute-start.4 = (bf16[2,528,128]{2,1,0:T(8,128)(2,1)S(1)}, bf16[2,528,128]{2,1,0:T(8,128)(2,1)S(1)}, u32[]{:S(2)}, u32[]{:S(2)}) collective-permute-start(bf16[2,528,128]{2,1,0:T(8,128)(2,1)S(1)} %shard_map.57.rest_0_.refs_0_), channel_id=1, source_target_pairs={{0,16},{1,17},{2,18},{3,19},{4,20},{5,21},{6,22},{7,23},{8,24},{9,... | collective-permute-start | bytes 811016 | tf_op jit(solution)/shard_map/ppermute | solution.py:224
  14.3 13.8 %collective-permute-start.3 = (bf16[2,528,128]{2,1,0:T(8,128)(2,1)S(1)}, bf16[2,528,128]{2,1,0:T(8,128)(2,1)S(1)}, u32[]{:S(2)}, u32[]{:S(2)}) collective-permute-start(bf16[2,528,128]{2,1,0:T(8,128)(2,1)S(1)} %shard_map.57.rest_0_.refs_0_), channel_id=1, source_target_pairs={{0,8},{1,9},{2,10},{3,11},{4,12},{5,13},{6,14},{7,15},{8,0},{9,1},... | collective-permute-start | bytes 811016 | tf_op jit(solution)/shard_map/ppermute | solution.py:224
  15.6 8.6 %collective-permute-start.2 = (bf16[528,128]{1,0:T(8,128)(2,1)S(1)}, bf16[528,128]{1,0:T(8,128)(2,1)S(1)}, u32[]{:S(2)}, u32[]{:S(2)}) collective-permute-start(bf16[528,128]{1,0:T(8,128)(2,1)S(1)} %get-tuple-element.21._), channel_id=1, source_target_pairs={{0,6},{1,7},{2,4},{3,5},{4,2},{5,3},{6,0},{7,1},{8,15},{9,14},{10,... | collective-permute-start | bytes 405512 | tf_op jit(solution)/shard_map/ppermute | solution.py:224
  16.9 15.1 %collective-permute-start.6 = (bf16[1,384,512]{2,1,0:T(8,128)(2,1)S(1)}, bf16[1,384,512]{2,1,0:T(8,128)(2,1)S(1)}, u32[]{:S(2)}, u32[]{:S(2)}) collective-permute-start(bf16[1,384,512]{2,1,0:T(8,128)(2,1)S(1)} %get-tuple-element.27), channel_id=1, source_target_pairs={{0,1},{1,0},{2,3},{3,2},{4,5},{5,4},{6,7},{7,6},{8,9},{9,8},{10,11... | collective-permute-start | bytes 1179656 | tf_op jit(solution)/shard_map/ppermute | solution.py:224
  27.0 8.1 %copy-start.4 = (s32[2,16]{1,0:T(2,128)S(1)}, s32[2,16]{1,0:T(2,128)}, u32[]{:S(2)}) copy-start(s32[2,16]{1,0:T(2,128)} %owned.1) | copy-start | bytes 388
  27.0 5.7 %collective-permute-start.8 = (bf16[1,384,512]{2,1,0:T(8,128)(2,1)S(1)}, bf16[1,384,512]{2,1,0:T(8,128)(2,1)S(1)}, u32[]{:S(2)}, u32[]{:S(2)}) collective-permute-start(bf16[1,384,512]{2,1,0:T(8,128)(2,1)S(1)} %get-tuple-element.29), channel_id=1, source_target_pairs={{0,1},{1,0},{2,3},{3,2},{4,5},{5,4},{6,7},{7,6},{8,9},{9,8},{10,11... | collective-permute-start | bytes 1179656 | tf_op jit(solution)/shard_map/ppermute | solution.py:224
  27.9 6.2 %collective-permute-start.7 = (bf16[1,384,512]{2,1,0:T(8,128)(2,1)S(1)}, bf16[1,384,512]{2,1,0:T(8,128)(2,1)S(1)}, u32[]{:S(2)}, u32[]{:S(2)}) collective-permute-start(bf16[1,384,512]{2,1,0:T(8,128)(2,1)S(1)} %get-tuple-element.28), channel_id=1, source_target_pairs={{0,1},{1,0},{2,3},{3,2},{4,5},{5,4},{6,7},{7,6},{8,9},{9,8},{10,11... | collective-permute-start | bytes 1179656 | tf_op jit(solution)/shard_map/ppermute | solution.py:224
  30.8 4.3 %collective-permute-start.9 = (bf16[1,384,512]{2,1,0:T(8,128)(2,1)S(1)}, bf16[1,384,512]{2,1,0:T(8,128)(2,1)S(1)}, u32[]{:S(2)}, u32[]{:S(2)}) collective-permute-start(bf16[1,384,512]{2,1,0:T(8,128)(2,1)S(1)} %get-tuple-element.30), channel_id=1, source_target_pairs={{0,1},{1,0},{2,3},{3,2},{4,5},{5,4},{6,7},{7,6},{8,9},{9,8},{10,11... | collective-permute-start | bytes 1179656 | tf_op jit(solution)/shard_map/ppermute | solution.py:224
  31.5 9.5 %collective-permute-start.15 = (bf16[1,528,128]{2,1,0:T(8,128)(2,1)S(1)}, bf16[1,528,128]{2,1,0:T(8,128)(2,1)S(1)}, u32[]{:S(2)}, u32[]{:S(2)}) collective-permute-start(bf16[1,528,128]{2,1,0:T(8,128)(2,1)S(1)} %shard_map.59.rest_0_.refs_0_), channel_id=1, source_target_pairs={{0,24},{1,25},{2,26},{3,27},{4,28},{5,29},{6,30},{7,31},{8,16},{9,... | collective-permute-start | bytes 405512 | tf_op jit(solution)/shard_map/ppermute | solution.py:224
  32.1 10.0 %collective-permute-start.14 = (bf16[1,528,128]{2,1,0:T(8,128)(2,1)S(1)}, bf16[1,528,128]{2,1,0:T(8,128)(2,1)S(1)}, u32[]{:S(2)}, u32[]{:S(2)}) collective-permute-start(bf16[1,528,128]{2,1,0:T(8,128)(2,1)S(1)} %shard_map.59.rest_0_.refs_0_), channel_id=1, source_target_pairs={{0,16},{1,17},{2,18},{3,19},{4,20},{5,21},{6,22},{7,23},{8,24},{9,... | collective-permute-start | bytes 405512 | tf_op jit(solution)/shard_map/ppermute | solution.py:224
  32.6 9.4 %collective-permute-start.13 = (bf16[1,528,128]{2,1,0:T(8,128)(2,1)S(1)}, bf16[1,528,128]{2,1,0:T(8,128)(2,1)S(1)}, u32[]{:S(2)}, u32[]{:S(2)}) collective-permute-start(bf16[1,528,128]{2,1,0:T(8,128)(2,1)S(1)} %shard_map.59.rest_0_.refs_0_), channel_id=1, source_target_pairs={{0,8},{1,9},{2,10},{3,11},{4,12},{5,13},{6,14},{7,15},{8,0},{9,1},... | collective-permute-start | bytes 405512 | tf_op jit(solution)/shard_map/ppermute | solution.py:224
  34.2 8.9 %collective-permute-start.10 = (bf16[2,528,128]{2,1,0:T(8,128)(2,1)S(1)}, bf16[2,528,128]{2,1,0:T(8,128)(2,1)S(1)}, u32[]{:S(2)}, u32[]{:S(2)}) collective-permute-start(bf16[2,528,128]{2,1,0:T(8,128)(2,1)S(1)} %get-tuple-element.32), channel_id=1, source_target_pairs={{0,1},{1,0},{2,3},{3,2},{4,5},{5,4},{6,7},{7,6},{8,9},{9,8},{10,11... | collective-permute-start | bytes 811016 | tf_op jit(solution)/shard_map/ppermute | solution.py:224
  39.9 11.8 %collective-permute-start.11 = (f32[4,128,128]{2,1,0:T(8,128)S(1)}, f32[4,128,128]{2,1,0:T(8,128)S(1)}, u32[]{:S(2)}, u32[]{:S(2)}) collective-permute-start(f32[4,128,128]{2,1,0:T(8,128)S(1)} %get-tuple-element.33), channel_id=1, source_target_pairs={{0,2},{1,3},{2,0},{3,1},{4,6},{5,7},{6,4},{7,5},{8,10},{9,11},{10,... | collective-permute-start | bytes 786440 | tf_op jit(solution)/shard_map/ppermute | solution.py:224
  41.0 18.0 %collective-permute-start.12 = (f32[4,128,128]{2,1,0:T(8,128)S(1)}, f32[4,128,128]{2,1,0:T(8,128)S(1)}, u32[]{:S(2)}, u32[]{:S(2)}) collective-permute-start(f32[4,128,128]{2,1,0:T(8,128)S(1)} %get-tuple-element.34), channel_id=1, source_target_pairs={{0,4},{1,5},{2,6},{3,7},{4,0},{5,1},{6,2},{7,3},{8,12},{9,13},{10,... | collective-permute-start | bytes 786440 | tf_op jit(solution)/shard_map/ppermute | solution.py:224
  42.5 23.1 %collective-permute-start.16 = (f32[4,128,128]{2,1,0:T(8,128)S(1)}, f32[4,128,128]{2,1,0:T(8,128)S(1)}, u32[]{:S(2)}, u32[]{:S(2)}) collective-permute-start(f32[4,128,128]{2,1,0:T(8,128)S(1)} %shard_map.65), channel_id=1, source_target_pairs={{0,6},{1,7},{2,4},{3,5},{4,2},{5,3},{6,0},{7,1},{8,14},{9,15},{10,... | collective-permute-start | bytes 786440 | tf_op jit(solution)/shard_map/ppermute | solution.py:224
  65.7 7.8 %collective-permute-start.19 = (f32[4,128,128]{2,1,0:T(8,128)S(1)}, f32[4,128,128]{2,1,0:T(8,128)S(1)}, u32[]{:S(2)}, u32[]{:S(2)}) collective-permute-start(f32[4,128,128]{2,1,0:T(8,128)S(1)} %shard_map.66.refs_0_), channel_id=1, source_target_pairs={{0,24},{1,25},{2,26},{3,27},{4,28},{5,29},{6,30},{7,31},{8,16},{9,... | collective-permute-start | bytes 786440 | tf_op jit(solution)/shard_map/ppermute | solution.py:224
  66.3 13.4 %collective-permute-start.18 = (f32[4,128,128]{2,1,0:T(8,128)S(1)}, f32[4,128,128]{2,1,0:T(8,128)S(1)}, u32[]{:S(2)}, u32[]{:S(2)}) collective-permute-start(f32[4,128,128]{2,1,0:T(8,128)S(1)} %shard_map.66.refs_0_), channel_id=1, source_target_pairs={{0,16},{1,17},{2,18},{3,19},{4,20},{5,21},{6,22},{7,23},{8,24},{9,... | collective-permute-start | bytes 786440 | tf_op jit(solution)/shard_map/ppermute | solution.py:224
  66.9 12.8 %collective-permute-start.17 = (f32[4,128,128]{2,1,0:T(8,128)S(1)}, f32[4,128,128]{2,1,0:T(8,128)S(1)}, u32[]{:S(2)}, u32[]{:S(2)}) collective-permute-start(f32[4,128,128]{2,1,0:T(8,128)S(1)} %shard_map.66.refs_0_), channel_id=1, source_target_pairs={{0,8},{1,9},{2,10},{3,11},{4,12},{5,13},{6,14},{7,15},{8,0},{9,1},... | collective-permute-start | bytes 786440 | tf_op jit(solution)/shard_map/ppermute | solution.py:224
  79.8 2.3 %collective-permute-start.20 = (f32[2,128,128]{2,1,0:T(8,128)S(1)}, f32[2,128,128]{2,1,0:T(8,128)S(1)}, u32[]{:S(2)}, u32[]{:S(2)}) collective-permute-start(f32[2,128,128]{2,1,0:T(8,128)S(1)} %get-tuple-element.36), channel_id=1, source_target_pairs={{0,1},{1,0},{2,3},{3,2},{4,5},{5,4},{6,7},{7,6},{8,9},{9,8},{10,11... | collective-permute-start | bytes 393224 | tf_op jit(solution)/shard_map/ppermute | solution.py:224

commit v3 on v2

--- a/solution.py
+++ b/solution.py
@@ -17,7 +17,8 @@
 SMEM = pl.BlockSpec(memory_space=pltpu.SMEM)
 ANY = pl.BlockSpec(memory_space=pl.ANY)
 HBM = pl.BlockSpec(memory_space=pltpu.HBM)
-F32, BF16 = jnp.float32, jnp.bfloat16
+F32, BF16, F16 = jnp.float32, jnp.bfloat16, jnp.float16
+TOP = 15.0
 
 
 def shape(dims, dtype):
@@ -155,6 +156,26 @@
     return jnp.dot(high, rows, preferred_element_type=F32) + jnp.dot(low, rows, preferred_element_type=F32)
 
 
+def encode(blocks, out):
+    count, width, _ = blocks.shape
+    at = lax.broadcasted_iota(jnp.int32, (16, width), 0)
+    codes = jnp.zeros((16, width), F32)
+    for n in range(count):
+        block = blocks[n]
+        peak = jnp.max(jnp.abs(block), axis=0, keepdims=True)
+        peak = jnp.max(peak, axis=1, keepdims=True)
+        power = jnp.ceil(jnp.log2(jnp.maximum(peak, 2.0**-100)))
+        power = jnp.broadcast_to(power, (1, width))
+        out[n * width : (n + 1) * width, :] = block * jnp.exp2(TOP - power)
+        codes = jnp.where(at == n, jnp.broadcast_to(power, (16, width)), codes)
+    out[count * width :, :] = codes
+
+
+def decode(ref, n, width, count):
+    power = ref[count * width :, :][n : n + 1, :]
+    return ref[pl.ds(n * width, width), :] * jnp.exp2(power - TOP)
+
+
 def own_kernel(ints, mine, other, out, *, aux_count, npart, width):
     _, z, c = place()
     per_dev = mine.shape[0]
@@ -166,11 +187,12 @@
 
 def far_kernel(ints, *refs, aux_count, distances, npart, width):
     a, z, c = place()
-    outs = refs[aux_count:]
+    outs, held = refs[aux_count:-1], refs[-1]
     for n, d in enumerate(distances):
         for e in range(aux_count):
             at = chip_slot(a ^ e, c)
-            outs[n][at] = partial_residual(ints, aux_count * (z ^ d) + at, refs[e][n], npart, width)
+            held[n, at] = partial_residual(ints, aux_count * (z ^ d) + at, refs[e][n], npart, width)
+        encode(held.at[n], outs[n])
 
 
 def join_kernel(*refs):
@@ -179,23 +201,30 @@
         out[n] = ref[...]
 
 
-def sum_kernel(*refs):
-    total = refs[0][...]
-    for ref in refs[1:-1]:
-        total = total + ref[...]
-    refs[-1][...] = total
-
-
-def sum_split_kernel(*refs):
-    *ins, keep, give = refs
+def sum_kernel(own, *refs):
+    *ins, total, coded = refs
+    count, width, _ = own.shape
+    for n in range(count):
+        value = own[n]
+        for ref in ins:
+            value = value + decode(ref, n, width, count)
+        total[n] = value
+    encode(total, coded)
+
+
+def sum_split_kernel(own, *refs):
+    *ins, keep, give, held = refs
     core = lax.axis_index("tile") % 2
+    count, width, _ = own.shape
     per_dev = keep.shape[0]
+    for n in range(count):
+        value = own[n]
+        for ref in ins:
+            value = value + decode(ref, n, width, count)
+        held[n] = value
     for s in range(per_dev):
-        for dst, owner in ((keep, core), (give, 1 - core)):
-            total = ins[0][per_dev * owner + s]
-            for ref in ins[1:]:
-                total = total + ref[per_dev * owner + s]
-            dst[s] = total
+        keep[s] = held[per_dev * core + s]
+        give[s] = held[per_dev * (1 - core) + s]
 
 
 def place_kernel(keep, got, out):
@@ -284,16 +313,22 @@
     chip_part = shape((aux_count, width, width), F32)
     sizes = dict(aux_count=aux_count, npart=npart, width=width)
     got = [call(functools.partial(own_kernel, **sizes), chip_part, [VMEM] * 3, 12)(ints, mine, other)]
+    coded = shape((aux_count * width + 16, width), F32)
     for distances, amps in zip(batches, far):
         shares = call(
             functools.partial(far_kernel, distances=distances, **sizes),
-            [chip_part] * len(distances), [VMEM] * (1 + aux_count), 16,
+            [coded] * len(distances), [VMEM] * (1 + aux_count), 16,
+            scratch_shapes=[pltpu.VMEM((len(distances),) + chip_part.shape, F32)],
         )(ints, *amps)
-        got += [exchange(share, lambda a, z, c, d=d: (a, z ^ d, c)) for d, share in zip(distances, shares)]
-    column = call(sum_kernel, chip_part, [VMEM] * chips, 12)(*got)
+        for d, share in zip(distances, shares):
+            got.append(exchange(share.astype(F16), lambda a, z, c, d=d: (a, z ^ d, c)).astype(F32))
+    column, share = call(sum_kernel, [chip_part, coded], [VMEM] * chips, 12)(*got)
 
     core_part = shape((per_dev, width, width), F32)
-    keep, give = call(sum_split_kernel, [core_part] * 2, [VMEM] * aux_count, 12)(column, *round_plane(column))
+    got = [x.astype(F32) for x in round_plane(share.astype(F16))]
+    keep, give = call(
+        sum_split_kernel, [core_part] * 2, [VMEM] * aux_count, 12, scratch_shapes=[pltpu.VMEM(chip_part.shape, F32)]
+    )(column, *got)
     return call(place_kernel, shape((NB, per_dev, width, width), F32), [VMEM] * 2, 8)(keep, swap(give))
 
 

time: 83 us -> 66.2 us (0.80)
  waiting for transfers between devices: 39.1 us -> 23.1 us
  starting transfers between devices: 19 us -> 17.5 us
    ppermute x21, waiting for transfers between devices: 39.1 us -> 23.1 us  [exchange(): return lax.ppermute(x, AXES, perm)]
    ppermute x21, starting transfers between devices: 19 us -> 17.5 us  [exchange(): return lax.ppermute(x, AXES, perm)]
  transfers between devices with their start and end apart: 21 -> 21, of which waited for: 8 -> 7; matrix products, arithmetic and copies ran while one was open for 0% -> 0% of each run, Pallas kernels for 23% -> 29%
where the time goes in v3:
time: 66.2 us; the launch traced here: 66 us
  waiting for transfers between devices  23.1 us (35%)
  Pallas kernels  21 us (32%)
  starting transfers between devices  17.5 us (26%)
  local copies, waits for them, and re-layouts  3.97 us (6%)
    ppermute x21, waiting for transfers between devices, exchange(): return lax.ppermute(x, AXES, perm)  23.1 us
    ppermute x21, starting transfers between devices, exchange(): return lax.ppermute(x, AXES, perm)  17.5 us
    pallas_call x3, Pallas kernels, per_device(): call(functools.partial(half_kernel, batch_occ=batch_occ, start=n * cols),...  8.3 us
    pallas_call x1, Pallas kernels, per_device(): call(functools.partial(first_half_kernel, batch_occ=batch_occ), [half, ha...  4.81 us
    pallas_call x1, Pallas kernels, per_device(): call(functools.partial(pair_kernel, parts=parts, width=width), ints_shape...  4.03 us
    unnamed x10, local copies, waits for them, and re-layouts  3.97 us
    pallas_call x2, Pallas kernels, per_device(): call(functools.partial(far_kernel, distances=distances, **sizes), [coded]...  1.45 us
  transfers between devices with their start and end apart: 21, of which 7 were waited for; matrix products, arithmetic and copies ran while one was open for 0% of the time, Pallas kernels for 29%

profile of v3, /device:TPU:11, one launch (start us, length us, event | category | flops | bytes accessed | tf_op | source)
XLA Modules:
  0.0 66.0 jit_solution(6474891448040174487)
XLA Ops:
  0.0 0.0 copy-start.2
  0.0 1.0 %copy-done.2 = bf16[2,2,4,128,128]{4,3,2,1,0:T(8,128)(2,1)S(1)} copy-done((bf16[2,2,4,128,128]{4,3,2,1,0:T(8,128)(2,1)S(1)}, bf16[2,2,4,128,128]{4,3,2,1,0:T(8,128)(2,1)}, u32[]{:S(2)}) %copy-start.2) | copy-done | bytes 524312
  1.0 0.0 copy-start.3
  1.0 0.7 %copy-done.3 = s32[2,2,4]{2,1,0:T(2,128)S(1)} copy-done((s32[2,2,4]{2,1,0:T(2,128)S(1)}, s32[2,2,4]{2,1,0:T(2,128)}, u32[]{:S(2)}) %copy-start.3) | copy-done | bytes 88
  1.7 1.0 %shard_map.55 = (bf16[528,128]{1,0:T(8,128)(2,1)S(1)}, bf16[2,528,128]{2,1,0:T(8,128)(2,1)S(1)}, bf16[2,528,128]{2,1,0:T(8,128)(2,1)S(1)}) custom-call(s32[2,2,4]{2,1,0:T(2,128)S(1)} %copy-done.3, bf16[2,2,4,128,128]{4,3,2,1,0:T(8,128)(2,1)S(1)} %copy-done.2), custom_call_target="tpu_custom_call" | custom-call | flops 1000000 | bytes 100000 | tf_op jit(solution)/shard_map/pallas_call | solution.py:268
  2.7 2.9 %collective-permute-start.1 = (bf16[528,128]{1,0:T(8,128)(2,1)S(1)}, bf16[528,128]{1,0:T(8,128)(2,1)S(1)}, u32[]{:S(2)}, u32[]{:S(2)}) collective-permute-start(bf16[528,128]{1,0:T(8,128)(2,1)S(1)} %get-tuple-element.23._), channel_id=1, source_target_pairs={{0,4},{1,5},{2,6},{3,7},{4,0},{5,1},{6,2},{7,3},{8,13},{9,12},{10,... | collective-permute-start | bytes 405512 | tf_op jit(solution)/shard_map/ppermute | solution.py:253
  5.6 0.0 collective-permute-start
  5.6 0.0 copy-start
  5.6 2.2 %copy-done = bf16[372,2,2944]{2,1,0:T(2,128)(2,1)S(1)} copy-done((bf16[372,2,2944]{2,1,0:T(2,128)(2,1)S(1)}, bf16[372,2,2944]{2,1,0:T(2,128)(2,1)}, u32[]{:S(2)}) %copy-start) | copy-done | bytes 4380696
  7.9 0.0 copy-start.1
  7.9 4.8 %shard_map.56 = (bf16[1,384,512]{2,1,0:T(8,128)(2,1)S(1)}, bf16[1,384,512]{2,1,0:T(8,128)(2,1)S(1)}, bf16[2944,2048]{1,0:T(8,128)(2,1)S(1)}) custom-call(bf16[372,2,2944]{2,1,0:T(2,128)(2,1)S(1)} %copy-done, bf16[2944,2048]{1,0:T(8,128)(2,1)} %c_hbm.1, bf16[528,128]{1,0:T(8,128)(2,1)S(1)} %get-tuple-element.23._), custom_call_target="tpu_custom_call" | custom-call | flops 1000000000 | bytes 100000 | tf_op jit(solution)/shard_map/pallas_call | solution.py:282
  12.7 0.0 collective-permute-done.1.refs_1_
  12.7 0.2 collective-permute-done.refs_0_
  12.9 0.7 %collective-permute-start.5 = (bf16[2,528,128]{2,1,0:T(8,128)(2,1)S(1)}, bf16[2,528,128]{2,1,0:T(8,128)(2,1)S(1)}, u32[]{:S(2)}, u32[]{:S(2)}) collective-permute-start(bf16[2,528,128]{2,1,0:T(8,128)(2,1)S(1)} %shard_map.57.rest_0_.refs_0_), channel_id=1, source_target_pairs={{0,24},{1,25},{2,26},{3,27},{4,28},{5,29},{6,30},{7,31},{8,16},{9,... | collective-permute-start | bytes 811016 | tf_op jit(solution)/shard_map/ppermute | solution.py:253
  13.6 0.6 collective-permute-start.4
  14.3 1.3 %collective-permute-start.3 = (bf16[2,528,128]{2,1,0:T(8,128)(2,1)S(1)}, bf16[2,528,128]{2,1,0:T(8,128)(2,1)S(1)}, u32[]{:S(2)}, u32[]{:S(2)}) collective-permute-start(bf16[2,528,128]{2,1,0:T(8,128)(2,1)S(1)} %shard_map.57.rest_0_.refs_0_), channel_id=1, source_target_pairs={{0,8},{1,9},{2,10},{3,11},{4,12},{5,13},{6,14},{7,15},{8,0},{9,1},... | collective-permute-start | bytes 811016 | tf_op jit(solution)/shard_map/ppermute | solution.py:253
  15.6 1.3 %collective-permute-start.2 = (bf16[528,128]{1,0:T(8,128)(2,1)S(1)}, bf16[528,128]{1,0:T(8,128)(2,1)S(1)}, u32[]{:S(2)}, u32[]{:S(2)}) collective-permute-start(bf16[528,128]{1,0:T(8,128)(2,1)S(1)} %get-tuple-element.23._), channel_id=1, source_target_pairs={{0,6},{1,7},{2,4},{3,5},{4,2},{5,3},{6,0},{7,1},{8,15},{9,14},{10,... | collective-permute-start | bytes 405512 | tf_op jit(solution)/shard_map/ppermute | solution.py:253
  16.9 0.0 collective-permute-start.6
  16.9 0.0 copy-done.1
  16.9 2.8 %shard_map.58 = (bf16[1,384,512]{2,1,0:T(8,128)(2,1)S(1)}, bf16[1,384,512]{2,1,0:T(8,128)(2,1)S(1)}) custom-call(bf16[372,2,2944]{2,1,0:T(2,128)(2,1)S(1)} %copy-done.1, bf16[2944,2048]{1,0:T(8,128)(2,1)S(1)} %get-tuple-element.25.c_ref, bf16[2,528,128]{2,1,0:T(8,128)(2,1)S(1)} %shard_map.57.rest_0_.refs_0_), custom_call_target="tpu_custom_call" | custom-call | flops 1000000000 | bytes 100000 | tf_op jit(solution)/shard_map/pallas_call | solution.py:288
  19.7 4.5 %collective-permute-done.2.refs_0_ = bf16[528,128]{1,0:T(8,128)(2,1)S(1)} collective-permute-done((bf16[528,128]{1,0:T(8,128)(2,1)S(1)}, bf16[528,128]{1,0:T(8,128)(2,1)S(1)}, u32[]{:S(2)}, u32[]{:S(2)}) %collective-permute-start.2) | collective-permute-done | bytes 135200 | tf_op jit(solution)/shard_map/ppermute | solution.py:253
  24.2 2.8 %shard_map.60 = (bf16[1,384,512]{2,1,0:T(8,128)(2,1)S(1)}, bf16[1,384,512]{2,1,0:T(8,128)(2,1)S(1)}) custom-call(bf16[372,2,2944]{2,1,0:T(2,128)(2,1)S(1)} %copy-done.1, bf16[2944,2048]{1,0:T(8,128)(2,1)S(1)} %get-tuple-element.25.c_ref, bf16[1,528,128]{2,1,0:T(8,128)(2,1)S(1)} %shard_map.59.rest_0_.refs_0_), custom_call_target="tpu_custom_call" | custom-call | flops 1000000000 | bytes 100000 | tf_op jit(solution)/shard_map/pallas_call | solution.py:288
  27.0 0.0 copy-start.4
  27.0 1.0 %collective-permute-start.8 = (bf16[1,384,512]{2,1,0:T(8,128)(2,1)S(1)}, bf16[1,384,512]{2,1,0:T(8,128)(2,1)S(1)}, u32[]{:S(2)}, u32[]{:S(2)}) collective-permute-start(bf16[1,384,512]{2,1,0:T(8,128)(2,1)S(1)} %get-tuple-element.31), channel_id=1, source_target_pairs={{0,1},{1,0},{2,3},{3,2},{4,5},{5,4},{6,7},{7,6},{8,9},{9,8},{10,11... | collective-permute-start | bytes 1179656 | tf_op jit(solution)/shard_map/ppermute | solution.py:253
  27.9 0.0 collective-permute-done.5.rest_2_.refs_3_
  27.9 0.1 collective-permute-start.7
  28.0 0.0 collective-permute-done.4.rest_1_.refs_2_
  28.0 0.0 collective-permute-done.3.rest_0_.refs_1_
  28.0 2.8 %shard_map.61 = (bf16[1,384,512]{2,1,0:T(8,128)(2,1)S(1)}, bf16[1,384,512]{2,1,0:T(8,128)(2,1)S(1)}) custom-call(bf16[372,2,2944]{2,1,0:T(2,128)(2,1)S(1)} %copy-done.1, bf16[2944,2048]{1,0:T(8,128)(2,1)S(1)} %get-tuple-element.25.c_ref, bf16[2,528,128]{2,1,0:T(8,128)(2,1)S(1)} %collective-permute-done.3.rest_0_.refs_1_, ...), custom_call_target="tpu_custom_call" | custom-call | flops 1000000000 | bytes 100000 | tf_op jit(solution)/shard_map/pallas_call | solution.py:288
  30.8 0.7 %collective-permute-start.9 = (bf16[1,384,512]{2,1,0:T(8,128)(2,1)S(1)}, bf16[1,384,512]{2,1,0:T(8,128)(2,1)S(1)}, u32[]{:S(2)}, u32[]{:S(2)}) collective-permute-start(bf16[1,384,512]{2,1,0:T(8,128)(2,1)S(1)} %get-tuple-element.32), channel_id=1, source_target_pairs={{0,1},{1,0},{2,3},{3,2},{4,5},{5,4},{6,7},{7,6},{8,9},{9,8},{10,11... | collective-permute-start | bytes 1179656 | tf_op jit(solution)/shard_map/ppermute | solution.py:253
  31.5 0.1 collective-permute-start.10
  31.6 0.0 collective-permute-done.6.refs_4_
  31.6 0.6 collective-permute-start.15
  32.1 0.0 collective-permute-done.8.refs_6_
  32.1 0.6 collective-permute-start.14
  32.7 0.0 collective-permute-done.7.refs_5_
  32.7 1.5 %collective-permute-start.13 = (bf16[1,528,128]{2,1,0:T(8,128)(2,1)S(1)}, bf16[1,528,128]{2,1,0:T(8,128)(2,1)S(1)}, u32[]{:S(2)}, u32[]{:S(2)}) collective-permute-start(bf16[1,528,128]{2,1,0:T(8,128)(2,1)S(1)} %shard_map.59.rest_0_.refs_0_), channel_id=1, source_target_pairs={{0,8},{1,9},{2,10},{3,11},{4,12},{5,13},{6,14},{7,15},{8,0},{9,1},... | collective-permute-start | bytes 405512 | tf_op jit(solution)/shard_map/ppermute | solution.py:253
  34.2 0.0 collective-permute-done.9.refs_7_
  34.2 0.0 copy-done.4
  34.2 4.0 %shard_map.62.ints = f32[16,5,128,128]{3,2,1,0:T(8,128)S(1)} custom-call(s32[2,16]{1,0:T(2,128)S(1)} %copy-done.4, bf16[1,384,512]{2,1,0:T(8,128)(2,1)S(1)} %get-tuple-element.24.refs_2_.refs_0_, bf16[1,384,512]{2,1,0:T(8,128)(2,1)S(1)} %get-tuple-element.26.refs_1_, bf16[1,384,512]{2,1,0:T(8,128)(2,1)S(1)} %get-tuple-element.27.refs_2_, ...), custom_call_target="tpu_custom_call" | custom-call | flops 1000000 | bytes 100000 | tf_op jit(solution)/shard_map/pallas_call | solution.py:307
  38.3 0.9 %shard_map.64 = (f32[528,128]{1,0:T(8,128)S(1)}, f32[528,128]{1,0:T(8,128)S(1)}) custom-call(f32[16,5,128,128]{3,2,1,0:T(8,128)S(1)} %shard_map.62.ints, bf16[2,528,128]{2,1,0:T(8,128)(2,1)S(1)} %shard_map.57.rest_0_.refs_0_, bf16[2,528,128]{2,1,0:T(8,128)(2,1)S(1)} %collective-permute-done.3.rest_0_.refs_1_, ...), custom_call_target="tpu_custom_call" | custom-call | flops 1000000 | bytes 100000 | tf_op jit(solution)/shard_map/pallas_call | solution.py:318
  39.2 2.1 %collective-permute-start.12 = (f16[528,128]{1,0:T(8,128)(2,1)S(1)}, f16[528,128]{1,0:T(8,128)(2,1)S(1)}, u32[]{:S(2)}, u32[]{:S(2)}) collective-permute-start(f16[528,128]{1,0:T(8,128)(2,1)S(1)} %convert_element_type.32), channel_id=1, source_target_pairs={{0,4},{1,5},{2,6},{3,7},{4,0},{5,1},{6,2},{7,3},{8,12},{9,13},{10,... | collective-permute-start | bytes 405512 | tf_op jit(solution)/shard_map/ppermute | solution.py:253
  41.3 0.0 collective-permute-done.15.refs_3_
  41.3 0.0 collective-permute-start.11
  41.3 0.0 collective-permute-done.14.refs_2_
  41.3 0.0 collective-permute-done.13.refs_1_
  41.4 0.6 shard_map.65
  42.0 0.7 collective-permute-start.16
  42.6 0.0 collective-permute-done.10.other
  42.6 0.4 shard_map.63.own
  43.1 3.8 %collective-permute-done.12 = f16[528,128]{1,0:T(8,128)(2,1)S(1)} collective-permute-done((f16[528,128]{1,0:T(8,128)(2,1)S(1)}, f16[528,128]{1,0:T(8,128)(2,1)S(1)}, u32[]{:S(2)}, u32[]{:S(2)}) %collective-permute-start.12) | collective-permute-done | bytes 135200 | tf_op jit(solution)/shard_map/ppermute | solution.py:253
  46.9 0.0 collective-permute-done.11
  47.0 7.1 %collective-permute-done.16 = f16[528,128]{1,0:T(8,128)(2,1)S(1)} collective-permute-done((f16[528,128]{1,0:T(8,128)(2,1)S(1)}, f16[528,128]{1,0:T(8,128)(2,1)S(1)}, u32[]{:S(2)}, u32[]{:S(2)}) %collective-permute-start.16) | collective-permute-done | bytes 135200 | tf_op jit(solution)/shard_map/ppermute | solution.py:253
  54.1 0.2 shard_map.66
  54.3 0.9 %collective-permute-start.19 = (f16[528,128]{1,0:T(8,128)(2,1)S(1)}, f16[528,128]{1,0:T(8,128)(2,1)S(1)}, u32[]{:S(2)}, u32[]{:S(2)}) collective-permute-start(f16[528,128]{1,0:T(8,128)(2,1)S(1)} %convert_element_type.36), channel_id=1, source_target_pairs={{0,24},{1,25},{2,26},{3,27},{4,28},{5,29},{6,30},{7,31},{8,16},{9,... | collective-permute-start | bytes 405512 | tf_op jit(solution)/shard_map/ppermute | solution.py:253
  55.2 0.4 collective-permute-start.18
  55.6 1.4 %collective-permute-start.17 = (f16[528,128]{1,0:T(8,128)(2,1)S(1)}, f16[528,128]{1,0:T(8,128)(2,1)S(1)}, u32[]{:S(2)}, u32[]{:S(2)}) collective-permute-start(f16[528,128]{1,0:T(8,128)(2,1)S(1)} %convert_element_type.36), channel_id=1, source_target_pairs={{0,8},{1,9},{2,10},{3,11},{4,12},{5,13},{6,14},{7,15},{8,0},{9,1},... | collective-permute-start | bytes 405512 | tf_op jit(solution)/shard_map/ppermute | solution.py:253
  57.0 2.8 %collective-permute-done.19 = f16[528,128]{1,0:T(8,128)(2,1)S(1)} collective-permute-done((f16[528,128]{1,0:T(8,128)(2,1)S(1)}, f16[528,128]{1,0:T(8,128)(2,1)S(1)}, u32[]{:S(2)}, u32[]{:S(2)}) %collective-permute-start.19) | collective-permute-done | bytes 135200 | tf_op jit(solution)/shard_map/ppermute | solution.py:253
  59.8 3.7 %collective-permute-done.18 = f16[528,128]{1,0:T(8,128)(2,1)S(1)} collective-permute-done((f16[528,128]{1,0:T(8,128)(2,1)S(1)}, f16[528,128]{1,0:T(8,128)(2,1)S(1)}, u32[]{:S(2)}, u32[]{:S(2)}) %collective-permute-start.18) | collective-permute-done | bytes 135200 | tf_op jit(solution)/shard_map/ppermute | solution.py:253
  63.5 0.0 collective-permute-done.17
  63.5 0.1 shard_map.67
  63.6 0.6 collective-permute-start.20
  64.3 1.0 %collective-permute-done.20.got = f32[2,128,128]{2,1,0:T(8,128)S(1)} collective-permute-done((f32[2,128,128]{2,1,0:T(8,128)S(1)}, f32[2,128,128]{2,1,0:T(8,128)S(1)}, u32[]{:S(2)}, u32[]{:S(2)}) %collective-permute-start.20) | collective-permute-done | bytes 131104 | tf_op jit(solution)/shard_map/ppermute | solution.py:253
  65.3 0.7 %shard_map.68 = f32[2,2,128,128]{3,2,1,0:T(8,128)} custom-call(f32[2,128,128]{2,1,0:T(8,128)S(1)} %get-tuple-element.39.keep, f32[2,128,128]{2,1,0:T(8,128)S(1)} %collective-permute-done.20.got), custom_call_target="tpu_custom_call" | custom-call | flops 1000000 | bytes 100000 | tf_op jit(solution)/shard_map/pallas_call | solution.py:332
  (12 shorter events, 0.2 us)
Async XLA Ops:
  0.0 1.0 %copy-start.2 = (bf16[2,2,4,128,128]{4,3,2,1,0:T(8,128)(2,1)S(1)}, bf16[2,2,4,128,128]{4,3,2,1,0:T(8,128)(2,1)}, u32[]{:S(2)}) copy-start(bf16[2,2,4,128,128]{4,3,2,1,0:T(8,128)(2,1)} %amps.1) | copy-start | bytes 1572868
  1.0 0.7 %copy-start.3 = (s32[2,2,4]{2,1,0:T(2,128)S(1)}, s32[2,2,4]{2,1,0:T(2,128)}, u32[]{:S(2)}) copy-start(s32[2,2,4]{2,1,0:T(2,128)} %pairs.1) | copy-start | bytes 196
  2.7 10.0 %collective-permute-start.1 = (bf16[528,128]{1,0:T(8,128)(2,1)S(1)}, bf16[528,128]{1,0:T(8,128)(2,1)S(1)}, u32[]{:S(2)}, u32[]{:S(2)}) collective-permute-start(bf16[528,128]{1,0:T(8,128)(2,1)S(1)} %get-tuple-element.23._), channel_id=1, source_target_pairs={{0,4},{1,5},{2,6},{3,7},{4,0},{5,1},{6,2},{7,3},{8,13},{9,12},{10,... | collective-permute-start | bytes 405512 | tf_op jit(solution)/shard_map/ppermute | solution.py:253
  5.6 7.2 %collective-permute-start = (bf16[528,128]{1,0:T(8,128)(2,1)S(1)}, bf16[528,128]{1,0:T(8,128)(2,1)S(1)}, u32[]{:S(2)}, u32[]{:S(2)}) collective-permute-start(bf16[528,128]{1,0:T(8,128)(2,1)S(1)} %get-tuple-element.23._), channel_id=1, source_target_pairs={{0,2},{1,3},{2,0},{3,1},{4,6},{5,7},{6,4},{7,5},{8,11},{9,10},{10,... | collective-permute-start | bytes 405512 | tf_op jit(solution)/shard_map/ppermute | solution.py:253
  5.6 2.2 %copy-start = (bf16[372,2,2944]{2,1,0:T(2,128)(2,1)S(1)}, bf16[372,2,2944]{2,1,0:T(2,128)(2,1)}, u32[]{:S(2)}) copy-start(bf16[372,2,2944]{2,1,0:T(2,128)(2,1)} %x_ref.7) | copy-start | bytes 13142020
  7.9 9.0 %copy-start.1 = (bf16[372,2,2944]{2,1,0:T(2,128)(2,1)S(1)}, bf16[372,2,2944]{2,1,0:T(2,128)(2,1)}, u32[]{:S(2)}) copy-start(bf16[372,2,2944]{2,1,0:T(2,128)(2,1)} %x_ref.7) | copy-start | bytes 13142020
  12.9 15.1 %collective-permute-start.5 = (bf16[2,528,128]{2,1,0:T(8,128)(2,1)S(1)}, bf16[2,528,128]{2,1,0:T(8,128)(2,1)S(1)}, u32[]{:S(2)}, u32[]{:S(2)}) collective-permute-start(bf16[2,528,128]{2,1,0:T(8,128)(2,1)S(1)} %shard_map.57.rest_0_.refs_0_), channel_id=1, source_target_pairs={{0,24},{1,25},{2,26},{3,27},{4,28},{5,29},{6,30},{7,31},{8,16},{9,... | collective-permute-start | bytes 811016 | tf_op jit(solution)/shard_map/ppermute | solution.py:253
  13.6 14.4 %collective-permute-start.4 = (bf16[2,528,128]{2,1,0:T(8,128)(2,1)S(1)}, bf16[2,528,128]{2,1,0:T(8,128)(2,1)S(1)}, u32[]{:S(2)}, u32[]{:S(2)}) collective-permute-start(bf16[2,528,128]{2,1,0:T(8,128)(2,1)S(1)} %shard_map.57.rest_0_.refs_0_), channel_id=1, source_target_pairs={{0,16},{1,17},{2,18},{3,19},{4,20},{5,21},{6,22},{7,23},{8,24},{9,... | collective-permute-start | bytes 811016 | tf_op jit(solution)/shard_map/ppermute | solution.py:253
  14.3 13.8 %collective-permute-start.3 = (bf16[2,528,128]{2,1,0:T(8,128)(2,1)S(1)}, bf16[2,528,128]{2,1,0:T(8,128)(2,1)S(1)}, u32[]{:S(2)}, u32[]{:S(2)}) collective-permute-start(bf16[2,528,128]{2,1,0:T(8,128)(2,1)S(1)} %shard_map.57.rest_0_.refs_0_), channel_id=1, source_target_pairs={{0,8},{1,9},{2,10},{3,11},{4,12},{5,13},{6,14},{7,15},{8,0},{9,1},... | collective-permute-start | bytes 811016 | tf_op jit(solution)/shard_map/ppermute | solution.py:253
  15.6 8.6 %collective-permute-start.2 = (bf16[528,128]{1,0:T(8,128)(2,1)S(1)}, bf16[528,128]{1,0:T(8,128)(2,1)S(1)}, u32[]{:S(2)}, u32[]{:S(2)}) collective-permute-start(bf16[528,128]{1,0:T(8,128)(2,1)S(1)} %get-tuple-element.23._), channel_id=1, source_target_pairs={{0,6},{1,7},{2,4},{3,5},{4,2},{5,3},{6,0},{7,1},{8,15},{9,14},{10,... | collective-permute-start | bytes 405512 | tf_op jit(solution)/shard_map/ppermute | solution.py:253
  16.9 14.7 %collective-permute-start.6 = (bf16[1,384,512]{2,1,0:T(8,128)(2,1)S(1)}, bf16[1,384,512]{2,1,0:T(8,128)(2,1)S(1)}, u32[]{:S(2)}, u32[]{:S(2)}) collective-permute-start(bf16[1,384,512]{2,1,0:T(8,128)(2,1)S(1)} %get-tuple-element.29), channel_id=1, source_target_pairs={{0,1},{1,0},{2,3},{3,2},{4,5},{5,4},{6,7},{7,6},{8,9},{9,8},{10,11... | collective-permute-start | bytes 1179656 | tf_op jit(solution)/shard_map/ppermute | solution.py:253
  27.0 7.3 %copy-start.4 = (s32[2,16]{1,0:T(2,128)S(1)}, s32[2,16]{1,0:T(2,128)}, u32[]{:S(2)}) copy-start(s32[2,16]{1,0:T(2,128)} %owned.1) | copy-start | bytes 388
  27.0 5.2 %collective-permute-start.8 = (bf16[1,384,512]{2,1,0:T(8,128)(2,1)S(1)}, bf16[1,384,512]{2,1,0:T(8,128)(2,1)S(1)}, u32[]{:S(2)}, u32[]{:S(2)}) collective-permute-start(bf16[1,384,512]{2,1,0:T(8,128)(2,1)S(1)} %get-tuple-element.31), channel_id=1, source_target_pairs={{0,1},{1,0},{2,3},{3,2},{4,5},{5,4},{6,7},{7,6},{8,9},{9,8},{10,11... | collective-permute-start | bytes 1179656 | tf_op jit(solution)/shard_map/ppermute | solution.py:253
  27.9 4.8 %collective-permute-start.7 = (bf16[1,384,512]{2,1,0:T(8,128)(2,1)S(1)}, bf16[1,384,512]{2,1,0:T(8,128)(2,1)S(1)}, u32[]{:S(2)}, u32[]{:S(2)}) collective-permute-start(bf16[1,384,512]{2,1,0:T(8,128)(2,1)S(1)} %get-tuple-element.30), channel_id=1, source_target_pairs={{0,1},{1,0},{2,3},{3,2},{4,5},{5,4},{6,7},{7,6},{8,9},{9,8},{10,11... | collective-permute-start | bytes 1179656 | tf_op jit(solution)/shard_map/ppermute | solution.py:253
  30.8 3.4 %collective-permute-start.9 = (bf16[1,384,512]{2,1,0:T(8,128)(2,1)S(1)}, bf16[1,384,512]{2,1,0:T(8,128)(2,1)S(1)}, u32[]{:S(2)}, u32[]{:S(2)}) collective-permute-start(bf16[1,384,512]{2,1,0:T(8,128)(2,1)S(1)} %get-tuple-element.32), channel_id=1, source_target_pairs={{0,1},{1,0},{2,3},{3,2},{4,5},{5,4},{6,7},{7,6},{8,9},{9,8},{10,11... | collective-permute-start | bytes 1179656 | tf_op jit(solution)/shard_map/ppermute | solution.py:253
  31.5 11.1 %collective-permute-start.10 = (bf16[2,528,128]{2,1,0:T(8,128)(2,1)S(1)}, bf16[2,528,128]{2,1,0:T(8,128)(2,1)S(1)}, u32[]{:S(2)}, u32[]{:S(2)}) collective-permute-start(bf16[2,528,128]{2,1,0:T(8,128)(2,1)S(1)} %get-tuple-element.34), channel_id=1, source_target_pairs={{0,1},{1,0},{2,3},{3,2},{4,5},{5,4},{6,7},{7,6},{8,9},{9,8},{10,11... | collective-permute-start | bytes 811016 | tf_op jit(solution)/shard_map/ppermute | solution.py:253
  31.6 9.8 %collective-permute-start.15 = (bf16[1,528,128]{2,1,0:T(8,128)(2,1)S(1)}, bf16[1,528,128]{2,1,0:T(8,128)(2,1)S(1)}, u32[]{:S(2)}, u32[]{:S(2)}) collective-permute-start(bf16[1,528,128]{2,1,0:T(8,128)(2,1)S(1)} %shard_map.59.rest_0_.refs_0_), channel_id=1, source_target_pairs={{0,24},{1,25},{2,26},{3,27},{4,28},{5,29},{6,30},{7,31},{8,16},{9,... | collective-permute-start | bytes 405512 | tf_op jit(solution)/shard_map/ppermute | solution.py:253
  32.1 9.2 %collective-permute-start.14 = (bf16[1,528,128]{2,1,0:T(8,128)(2,1)S(1)}, bf16[1,528,128]{2,1,0:T(8,128)(2,1)S(1)}, u32[]{:S(2)}, u32[]{:S(2)}) collective-permute-start(bf16[1,528,128]{2,1,0:T(8,128)(2,1)S(1)} %shard_map.59.rest_0_.refs_0_), channel_id=1, source_target_pairs={{0,16},{1,17},{2,18},{3,19},{4,20},{5,21},{6,22},{7,23},{8,24},{9,... | collective-permute-start | bytes 405512 | tf_op jit(solution)/shard_map/ppermute | solution.py:253
  32.7 8.6 %collective-permute-start.13 = (bf16[1,528,128]{2,1,0:T(8,128)(2,1)S(1)}, bf16[1,528,128]{2,1,0:T(8,128)(2,1)S(1)}, u32[]{:S(2)}, u32[]{:S(2)}) collective-permute-start(bf16[1,528,128]{2,1,0:T(8,128)(2,1)S(1)} %shard_map.59.rest_0_.refs_0_), channel_id=1, source_target_pairs={{0,8},{1,9},{2,10},{3,11},{4,12},{5,13},{6,14},{7,15},{8,0},{9,1},... | collective-permute-start | bytes 405512 | tf_op jit(solution)/shard_map/ppermute | solution.py:253
  39.2 7.7 %collective-permute-start.12 = (f16[528,128]{1,0:T(8,128)(2,1)S(1)}, f16[528,128]{1,0:T(8,128)(2,1)S(1)}, u32[]{:S(2)}, u32[]{:S(2)}) collective-permute-start(f16[528,128]{1,0:T(8,128)(2,1)S(1)} %convert_element_type.32), channel_id=1, source_target_pairs={{0,4},{1,5},{2,6},{3,7},{4,0},{5,1},{6,2},{7,3},{8,12},{9,13},{10,... | collective-permute-start | bytes 405512 | tf_op jit(solution)/shard_map/ppermute | solution.py:253
  41.3 5.6 %collective-permute-start.11 = (f16[528,128]{1,0:T(8,128)(2,1)S(1)}, f16[528,128]{1,0:T(8,128)(2,1)S(1)}, u32[]{:S(2)}, u32[]{:S(2)}) collective-permute-start(f16[528,128]{1,0:T(8,128)(2,1)S(1)} %convert_element_type.30), channel_id=1, source_target_pairs={{0,2},{1,3},{2,0},{3,1},{4,6},{5,7},{6,4},{7,5},{8,10},{9,11},{10,... | collective-permute-start | bytes 405512 | tf_op jit(solution)/shard_map/ppermute | solution.py:253
  42.0 12.1 %collective-permute-start.16 = (f16[528,128]{1,0:T(8,128)(2,1)S(1)}, f16[528,128]{1,0:T(8,128)(2,1)S(1)}, u32[]{:S(2)}, u32[]{:S(2)}) collective-permute-start(f16[528,128]{1,0:T(8,128)(2,1)S(1)} %convert_element_type.34), channel_id=1, source_target_pairs={{0,6},{1,7},{2,4},{3,5},{4,2},{5,3},{6,0},{7,1},{8,14},{9,15},{10,... | collective-permute-start | bytes 405512 | tf_op jit(solution)/shard_map/ppermute | solution.py:253
  54.3 5.5 %collective-permute-start.19 = (f16[528,128]{1,0:T(8,128)(2,1)S(1)}, f16[528,128]{1,0:T(8,128)(2,1)S(1)}, u32[]{:S(2)}, u32[]{:S(2)}) collective-permute-start(f16[528,128]{1,0:T(8,128)(2,1)S(1)} %convert_element_type.36), channel_id=1, source_target_pairs={{0,24},{1,25},{2,26},{3,27},{4,28},{5,29},{6,30},{7,31},{8,16},{9,... | collective-permute-start | bytes 405512 | tf_op jit(solution)/shard_map/ppermute | solution.py:253
  55.2 8.3 %collective-permute-start.18 = (f16[528,128]{1,0:T(8,128)(2,1)S(1)}, f16[528,128]{1,0:T(8,128)(2,1)S(1)}, u32[]{:S(2)}, u32[]{:S(2)}) collective-permute-start(f16[528,128]{1,0:T(8,128)(2,1)S(1)} %convert_element_type.36), channel_id=1, source_target_pairs={{0,16},{1,17},{2,18},{3,19},{4,20},{5,21},{6,22},{7,23},{8,24},{9,... | collective-permute-start | bytes 405512 | tf_op jit(solution)/shard_map/ppermute | solution.py:253
  55.6 7.9 %collective-permute-start.17 = (f16[528,128]{1,0:T(8,128)(2,1)S(1)}, f16[528,128]{1,0:T(8,128)(2,1)S(1)}, u32[]{:S(2)}, u32[]{:S(2)}) collective-permute-start(f16[528,128]{1,0:T(8,128)(2,1)S(1)} %convert_element_type.36), channel_id=1, source_target_pairs={{0,8},{1,9},{2,10},{3,11},{4,12},{5,13},{6,14},{7,15},{8,0},{9,1},... | collective-permute-start | bytes 405512 | tf_op jit(solution)/shard_map/ppermute | solution.py:253
  63.6 1.6 %collective-permute-start.20 = (f32[2,128,128]{2,1,0:T(8,128)S(1)}, f32[2,128,128]{2,1,0:T(8,128)S(1)}, u32[]{:S(2)}, u32[]{:S(2)}) collective-permute-start(f32[2,128,128]{2,1,0:T(8,128)S(1)} %get-tuple-element.40), channel_id=1, source_target_pairs={{0,1},{1,0},{2,3},{3,2},{4,5},{5,4},{6,7},{7,6},{8,9},{9,8},{10,11... | collective-permute-start | bytes 393224 | tf_op jit(solution)/shard_map/ppermute | solution.py:253

commit v4 on v3

v4 whole, which is shorter than its diff:
```python
import functools

import jax
import jax.numpy as jnp
from jax import lax
from jax.experimental import pallas as pl
from jax.experimental.pallas import tpu as pltpu
from jax.sharding import PartitionSpec as P

NB = 2
BAND = 5
REACH = BAND // 2
PARTS = 8
STEPS = (2, 2, 3, 1)
JOIN_AFTER = (0, 2)
ORDER = {
    "j0": ("C0",),
    "C1": ("j0",),
    "C2": ("C1",),
    "j1": ("C2",),
    "C3": ("x00", "x01", "x02", "j1"),
    "far1": ("far0",),
    "own": ("far1",),
}
MIB = 2**20
AXES = ("aux", "tile")
VMEM = pl.BlockSpec(memory_space=pltpu.VMEM)
SMEM = pl.BlockSpec(memory_space=pltpu.SMEM)
ANY = pl.BlockSpec(memory_space=pl.ANY)
HBM = pl.BlockSpec(memory_space=pltpu.HBM)
F32, BF16, F16 = jnp.float32, jnp.bfloat16, jnp.float16
TOP = 15.0


def shape(dims, dtype):
    return jax.ShapeDtypeStruct(tuple(dims), dtype)


def place():
    t = lax.axis_index("tile")
    return lax.axis_index("aux"), t // 2, t % 2


def chip_slot(a, batch):
    return 2 * ((a % 2) ^ batch) + a // 2


def call(name, kernel, outs, specs, limit, **kw):
    return pl.pallas_call(
        kernel, name=name, in_specs=specs, out_specs=jax.tree.map(lambda _: VMEM, outs), out_shape=outs,
        compiler_params=pltpu.CompilerParams(vmem_limit_bytes=limit * MIB),
        cost_estimate=pl.CostEstimate(flops=10**6, bytes_accessed=10**5, transcendentals=0), **kw,
    )


def pack_kernel(pairs, amps, zmsg, mine, other, token, *, npart, width):
    token[...] = jnp.zeros_like(token)
    a, z, c = place()
    per_dev = amps.shape[1]
    first = lax.axis_index("tile") * per_dev

    def pack(batch, s, dst):
        offsets, live, seen = [], [], [jnp.int32(0)] * BAND
        for k in range(npart):
            p = pairs[batch, s, k]
            o = p - (first + s) + REACH
            ok = p >= 0
            offsets.append(o)
            live.append(ok)
            for n in range(BAND):
                seen[n] = jnp.where(ok & (o == n), 1, seen[n])
        m = jnp.int32(BAND - 1)
        for n in reversed(range(BAND)):
            m = jnp.where(seen[n] == 0, n, m)
        for j in range(npart):
            want = j + jnp.where(j >= m, 1, 0)
            found, at = jnp.int32(0), jnp.int32(0)
            for k in range(npart):
                hit = live[k] & (offsets[k] == want)
                found = jnp.where(hit, 1, found)
                at = jnp.where(hit, k, at)
            block = amps[batch, s, at]
            dst[pl.ds(j * width, width), :] = jnp.where(found == 1, block, jnp.zeros_like(block))
        code = jnp.full((16, width), m.astype(F32), F32)
        dst[pl.ds(npart * width, 16), :] = code.astype(BF16)

    pack(c ^ (a % 2), a // 2, zmsg)
    for s in range(per_dev):
        pack(c, s, mine.at[s])
        pack(1 - c, s, other.at[s])


def half_columns(x_ref, c_ref, start, at, count, mine, other, acc, batch_occ):
    core = lax.axis_index("tile") % 2
    rows, occ, ao = x_ref.shape
    padded = mine.shape[1]
    prod = jnp.dot(
        x_ref[...].reshape(rows * occ, ao), c_ref[:, start : start + count], preferred_element_type=F32
    )
    for n in range(count // 128):
        acc[n] = prod[:, n * 128 : (n + 1) * 128]
    for i in range(batch_occ):
        for n in range(count // 128):
            lanes = slice(at + n * 128, at + (n + 1) * 128)
            for dst, b in ((mine, core), (other, 1 - core)):
                part = acc[n, pl.ds(b * batch_occ + i, rows, stride=occ), :]
                dst[i, :rows, lanes] = part.astype(BF16)
    for dst in (mine, other):
        dst[:, rows:, at : at + count] = jnp.zeros((batch_occ, padded - rows, count), BF16)


def first_half_kernel(x_ref, c_hbm, _, mine, other, c_ref, acc, sems, *, batch_occ):
    piece = mine.shape[2]
    get_c = [
        pltpu.make_async_copy(
            c_hbm.at[:, pl.ds(n, piece)], c_ref.at[:, pl.ds(n, piece)], sems.at[n // piece]
        )
        for n in range(0, c_ref.shape[1], piece)
    ]
    for copy in get_c:
        copy.start()
    get_c[0].wait()
    half_columns(x_ref, c_ref, 0, 0, piece, mine, other, acc, batch_occ)
    for copy in get_c[1:]:
        copy.wait()


def half_kernel(x_ref, c_ref, *rest, batch_occ, start):
    mine, other, acc = rest[-3:]
    most = acc.shape[0] * 128
    cols = mine.shape[2]
    for n in range(0, cols, most):
        half_columns(x_ref, c_ref, start + n, n, min(most, cols - n), mine, other, acc, batch_occ)


def order_kernel(owned, *refs, parts, width):
    core = lax.axis_index("tile") % 2
    slots = owned.shape[1]
    y_mine, y_other, (tiles, place_of) = refs[:parts], refs[parts : 2 * parts], refs[-2:]
    batch_occ, padded, _ = y_mine[0].shape
    virt_tiles = slots // batch_occ
    for s in range(slots):
        place_of[owned[core, s]] = s + REACH
    for n in (0, 1, slots + REACH, slots + REACH + 1):
        tiles[:, n * width : (n + 1) * width] = jnp.zeros((2 * padded, width), BF16)
    for i in range(batch_occ):
        first = 0
        for h in range(parts):
            count = y_mine[h].shape[2] // width
            for n in range(count):
                ident = i * virt_tiles + first + n
                lanes = pl.ds(pl.multiple_of(place_of[ident] * width, width), width)
                for src, group in enumerate((y_mine, y_other)):
                    rows = slice(src * padded, (src + 1) * padded)
                    tiles[rows, lanes] = group[h][i, :, n * width : (n + 1) * width]
            first += count


def pair_ints(tiles, first, ints):
    count, _, width, _ = ints.shape
    for t in range(0, count, 2):
        at = pl.multiple_of((first + t) * width, width)
        left = tiles[:, pl.ds(at + REACH * width, 2 * width)]
        right = tiles[:, pl.ds(at, (2 + 2 * REACH) * width)]
        total = lax.dot_general(left, right, (((0,), (0,)), ((), ())), preferred_element_type=F32)
        for u in range(2):
            for o in range(BAND):
                ints[t + u, o] = total[u * width : (u + 1) * width, (u + o) * width : (u + o + 1) * width]


def partial_residual(ints, slot, amp, npart, width):
    rows = amp[: npart * width]
    m = amp[npart * width :].astype(F32)[:1, :]
    picked = [jnp.where(m > j, ints[slot, j], ints[slot, j + 1]) for j in range(npart)]
    picked = jnp.concatenate(picked, axis=1)
    high = picked.astype(BF16)
    low = (picked - high.astype(F32)).astype(BF16)
    return jnp.dot(high, rows, preferred_element_type=F32) + jnp.dot(low, rows, preferred_element_type=F32)


def encode(blocks, out):
    count, width, _ = blocks.shape
    at = lax.broadcasted_iota(jnp.int32, (16, width), 0)
    codes = jnp.zeros((16, width), F32)
    for n in range(count):
        block = blocks[n]
        peak = jnp.max(jnp.abs(block), axis=0, keepdims=True)
        peak = jnp.max(peak, axis=1, keepdims=True)
        power = jnp.ceil(jnp.log2(jnp.maximum(peak, 2.0**-100)))
        power = jnp.broadcast_to(power, (1, width))
        out[n * width : (n + 1) * width, :] = block * jnp.exp2(TOP - power)
        codes = jnp.where(at == n, jnp.broadcast_to(power, (16, width)), codes)
    out[count * width :, :] = codes


def decode(ref, n, width, count):
    power = ref[count * width :, :][n : n + 1, :]
    return ref[pl.ds(n * width, width), :] * jnp.exp2(power - TOP)


def own_kernel(tiles, mine, other, *refs, aux_count, npart, width):
    out, ints = refs[-2:]
    _, z, c = place()
    per_dev = mine.shape[0]
    pair_ints(tiles, aux_count * z, ints)
    for s in range(per_dev):
        for src, core in ((mine, c), (other, 1 - c)):
            at = per_dev * core + s
            out[at] = partial_residual(ints, at, src[s], npart, width)


def far_kernel(tiles, *refs, aux_count, distances, npart, width):
    a, z, c = place()
    outs, (held, ints) = refs[-2 - len(distances) : -2], refs[-2:]
    for n, d in enumerate(distances):
        pair_ints(tiles, aux_count * (z ^ d), ints)
        for e in range(aux_count):
            at = chip_slot(a ^ e, c)
            held[at] = partial_residual(ints, at, refs[e][n], npart, width)
        encode(held, outs[n])


def join_kernel(*refs):
    out = refs[-1]
    for n in range(out.shape[0]):
        out[n] = refs[n][...]


def sum_kernel(own, *refs):
    *ins, total, coded = refs
    count, width, _ = own.shape
    for n in range(count):
        value = own[n]
        for ref in ins:
            value = value + decode(ref, n, width, count)
        total[n] = value
    encode(total, coded)


def sum_split_kernel(own, *refs):
    *ins, keep, give, held = refs
    core = lax.axis_index("tile") % 2
    count, width, _ = own.shape
    per_dev = keep.shape[0]
    for n in range(count):
        value = own[n]
        for ref in ins:
            value = value + decode(ref, n, width, count)
        held[n] = value
    for s in range(per_dev):
        keep[s] = held[per_dev * core + s]
        give[s] = held[per_dev * (1 - core) + s]


def place_kernel(keep, got, out):
    core = lax.axis_index("tile") % 2
    out[core] = keep[...]
    out[1 - core] = got[...]


def per_device(integrals, coefficients, owned_tiles, pair_list, amplitudes):
    aux_count, tile_count = lax.axis_size("aux"), lax.axis_size("tile")
    chips = tile_count // 2
    rows, occ, ao = integrals.shape
    virt = coefficients.shape[1]
    batch_occ = occ // NB
    _, per_dev, npart, width, _ = amplitudes.shape
    slots = owned_tiles.shape[1]
    assert aux_count == 2 * per_dev and per_dev == 2

    def exchange(x, target):
        perm = []
        for a in range(aux_count):
            for z in range(chips):
                for c in range(2):
                    a2, z2, c2 = target(a, z, c)
                    perm.append((a * tile_count + 2 * z + c, a2 * tile_count + 2 * z2 + c2))
        return lax.ppermute(x, AXES, perm)

    def swap(x):
        return exchange(x, lambda a, z, c: (a, z, 1 - c))

    def round_plane(x):
        return [exchange(x, lambda a, z, c, e=e: (a ^ e, z, c)) for e in range(1, aux_count)]

    cols = virt // PARTS
    padded = -(-rows // 16) * 16

    msg_rows = npart * width + 16
    msg = shape((msg_rows, width), BF16)
    pair = shape((per_dev, msg_rows, width), BF16)
    zmsg, mine, other, token = call(
        "pack", functools.partial(pack_kernel, npart=npart, width=width),
        [msg, pair, pair, shape((8, 128), F32)], [SMEM, VMEM], 12,
    )(pair_list, amplitudes)
    along = [exchange(zmsg, lambda a, z, c, d=d: (a, z ^ d, c ^ (a % 2))) for d in range(1, chips)]
    other = swap(other)
    marks = {"z": zmsg, "o": other}

    def deps_for(name):
        return [marks[key] for key in ORDER.get(name, ())]

    batches = [range(chips - 2, 0, -1), range(chips - 1, chips)]
    far = []

    first_cols = STEPS[0] * cols
    acc = pltpu.VMEM((first_cols // 128, rows * occ, 128), F32)
    y_mine, y_other = [], []
    start = 0
    for step, count in enumerate(STEPS):
        half = shape((batch_occ, padded, count * cols), BF16)
        after = deps_for("C%d" % step)
        if step == 0:
            got, send, c = call(
                "half0", functools.partial(first_half_kernel, batch_occ=batch_occ),
                [half, half, shape(coefficients.shape, BF16)],
                [VMEM, HBM, ANY], 28, scratch_shapes=[acc, pltpu.SemaphoreType.DMA((virt // first_cols,))],
            )(integrals, coefficients, token)
        else:
            got, send = call(
                "half%d" % step, functools.partial(half_kernel, batch_occ=batch_occ, start=start * cols),
                [half, half], [VMEM, VMEM] + [ANY] * len(after), 12, scratch_shapes=[acc],
            )(integrals, c, *after)
        start += count
        y_mine.append(got)
        y_other.append(swap(send))
        marks["C%d" % step] = got
        marks["y%d" % step] = y_other[-1]
        if step in JOIN_AFTER:
            distances = batches[JOIN_AFTER.index(step)]
            after = deps_for("j%d" % len(far))
            joined = call(
                "join%d" % len(far), join_kernel, shape((len(distances), msg_rows, width), BF16),
                [VMEM] * len(distances) + [ANY] * len(after), 12
            )(*[along[d - 1] for d in distances], *after)
            marks["j%d" % len(far)] = joined
            around = round_plane(joined)
            for e, x in enumerate(around):
                marks["x%d%d" % (len(far), e)] = x
            far.append([joined] + around)

    after = deps_for("T")
    tiles = call(
        "order", functools.partial(order_kernel, parts=len(STEPS), width=width),
        shape((2 * padded, (slots + BAND - 1) * width), BF16),
        [SMEM] + [VMEM] * (2 * len(STEPS)) + [ANY] * len(after), 12,
        scratch_shapes=[pltpu.SMEM((slots,), jnp.int32)],
    )(owned_tiles, *y_mine, *y_other, *after)

    chip_part = shape((aux_count, width, width), F32)
    coded = shape((aux_count * width + 16, width), F32)
    ints = pltpu.VMEM((aux_count, BAND, width, width), F32)
    sizes = dict(aux_count=aux_count, npart=npart, width=width)
    got = []
    for n, (distances, amps) in enumerate(zip(batches, far)):
        after = deps_for("far%d" % n)
        shares = call(
            "far%d" % n, functools.partial(far_kernel, distances=distances, **sizes),
            [coded] * len(distances), [VMEM] * (1 + aux_count) + [ANY] * len(after), 16,
            scratch_shapes=[pltpu.VMEM(chip_part.shape, F32), ints],
        )(tiles, *amps, *after)
        marks["far%d" % n] = shares[0]
        for d, share in zip(distances, shares):
            got.append(exchange(share.astype(F16), lambda a, z, c, d=d: (a, z ^ d, c)).astype(F32))
    after = deps_for("own")
    own = call(
        "own", functools.partial(own_kernel, **sizes), chip_part, [VMEM] * 3 + [ANY] * len(after), 12,
        scratch_shapes=[ints],
    )(tiles, mine, other, *after)
    got = [own] + got
    column, share = call("along", sum_kernel, [chip_part, coded], [VMEM] * chips, 12)(*got)

    core_part = shape((per_dev, width, width), F32)
    got = [x.astype(F32) for x in round_plane(share.astype(F16))]
    keep, give = call(
        "around", sum_split_kernel, [core_part] * 2, [VMEM] * aux_count, 12,
        scratch_shapes=[pltpu.VMEM(chip_part.shape, F32)],
    )(column, *got)
    return call("place", place_kernel, shape((NB, per_dev, width, width), F32), [VMEM] * 2, 8)(keep, swap(give))


def solution(mesh):
    in_specs = (
        P(("aux", "tile"), None, None),
        P(),
        P(),
        P(None, "tile", None),
        P(None, "tile", None, None, None),
    )
    out_specs = P(None, "tile", None, None)
    return jax.shard_map(
        per_device, mesh=mesh, in_specs=in_specs, out_specs=out_specs, check_vma=False
    )
```

time: 66.2 us -> 63.9 us (0.965)
  waiting for transfers between devices: 23.1 us -> 20.1 us
  Pallas kernels: 21 us -> 21.8 us
    ppermute x21, waiting for transfers between devices: 23.1 us -> 20.1 us  [exchange(): return lax.ppermute(x, AXES, perm)]
    pallas_call x14, Pallas kernels: 21 us -> 21.8 us  [the longest x3 8.54 us: per_device(): call('half%d' % step, functools.partial(half_kernel, batch_occ=batch_occ,...]
  transfers between devices with their start and end apart: 21 -> 21, of which waited for: 7 -> 7; matrix products, arithmetic and copies ran while one was open for 0% -> 0% of each run, Pallas kernels for 29% -> 31%
where the time goes in v4:
time: 63.9 us; the launch traced here: 63.7 us
  Pallas kernels  21.8 us (34%)
  waiting for transfers between devices  20.1 us (31%)
  starting transfers between devices  17.5 us (27%)
  local copies, waits for them, and re-layouts  3.97 us (6%)
    ppermute x21, waiting for transfers between devices, exchange(): return lax.ppermute(x, AXES, perm)  20.1 us
    ppermute x21, starting transfers between devices, exchange(): return lax.ppermute(x, AXES, perm)  17.5 us
    pallas_call x3, Pallas kernels, per_device(): call('half%d' % step, functools.partial(half_kernel, batch_occ=batch_occ,...  8.54 us
    pallas_call x1, Pallas kernels, per_device(): call('half0', functools.partial(first_half_kernel, batch_occ=batch_occ),...  4.81 us
    pallas_call x2, Pallas kernels, per_device(): call('far%d' % n, functools.partial(far_kernel, distances=distances, **si...  4.06 us
    unnamed x10, local copies, waits for them, and re-layouts  3.97 us
  transfers between devices with their start and end apart: 21, of which 7 were waited for; matrix products, arithmetic and copies ran while one was open for 0% of the time, Pallas kernels for 31%

profile of v4, /device:TPU:11, one launch (start us, length us, event | category | flops | bytes accessed | tf_op | source)
XLA Modules:
  0.0 63.7 jit_solution(10005319893201144678)
XLA Ops:
  0.0 0.0 copy-start.2
  0.0 1.0 %copy-done.2 = bf16[2,2,4,128,128]{4,3,2,1,0:T(8,128)(2,1)S(1)} copy-done((bf16[2,2,4,128,128]{4,3,2,1,0:T(8,128)(2,1)S(1)}, bf16[2,2,4,128,128]{4,3,2,1,0:T(8,128)(2,1)}, u32[]{:S(2)}) %copy-start.2) | copy-done | bytes 524312
  1.0 0.0 copy-start.3
  1.0 0.7 %copy-done.3 = s32[2,2,4]{2,1,0:T(2,128)S(1)} copy-done((s32[2,2,4]{2,1,0:T(2,128)S(1)}, s32[2,2,4]{2,1,0:T(2,128)}, u32[]{:S(2)}) %copy-start.3) | copy-done | bytes 88
  1.7 1.0 %pack.1 = (bf16[528,128]{1,0:T(8,128)(2,1)S(1)}, bf16[2,528,128]{2,1,0:T(8,128)(2,1)S(1)}, bf16[2,528,128]{2,1,0:T(8,128)(2,1)S(1)}, f32[8,128]{1,0:T(8,128)S(1)}) custom-call(s32[2,2,4]{2,1,0:T(2,128)S(1)} %copy-done.3, bf16[2,2,4,128,128]{4,3,2,1,0:T(8,128)(2,1)S(1)} %copy-done.2), custom_call_target="tpu_custom_call" | custom-call | flops 1000000 | bytes 100000 | tf_op jit(solution)/shard_map/pack/pallas_call | solution.py:292
  2.7 0.8 %collective-permute-start.1 = (bf16[528,128]{1,0:T(8,128)(2,1)S(1)}, bf16[528,128]{1,0:T(8,128)(2,1)S(1)}, u32[]{:S(2)}, u32[]{:S(2)}) collective-permute-start(bf16[528,128]{1,0:T(8,128)(2,1)S(1)} %get-tuple-element.27), channel_id=1, source_target_pairs={{0,2},{1,3},{2,0},{3,1},{4,6},{5,7},{6,4},{7,5},{8,11},{9,10},{10,... | collective-permute-start | bytes 405512 | tf_op jit(solution)/shard_map/ppermute | solution.py:278
  3.5 2.2 %collective-permute-start = (bf16[528,128]{1,0:T(8,128)(2,1)S(1)}, bf16[528,128]{1,0:T(8,128)(2,1)S(1)}, u32[]{:S(2)}, u32[]{:S(2)}) collective-permute-start(bf16[528,128]{1,0:T(8,128)(2,1)S(1)} %get-tuple-element.27), channel_id=1, source_target_pairs={{0,4},{1,5},{2,6},{3,7},{4,0},{5,1},{6,2},{7,3},{8,13},{9,12},{10,... | collective-permute-start | bytes 405512 | tf_op jit(solution)/shard_map/ppermute | solution.py:278
  5.7 0.0 copy-start
  5.7 2.2 %copy-done = bf16[372,2,2944]{2,1,0:T(2,128)(2,1)S(1)} copy-done((bf16[372,2,2944]{2,1,0:T(2,128)(2,1)S(1)}, bf16[372,2,2944]{2,1,0:T(2,128)(2,1)}, u32[]{:S(2)}) %copy-start) | copy-done | bytes 4380696
  7.9 0.0 copy-start.1
  7.9 4.8 %half0.1 = (bf16[1,384,512]{2,1,0:T(8,128)(2,1)S(1)}, bf16[1,384,512]{2,1,0:T(8,128)(2,1)S(1)}, bf16[2944,2048]{1,0:T(8,128)(2,1)S(1)}) custom-call(bf16[372,2,2944]{2,1,0:T(2,128)(2,1)S(1)} %copy-done, bf16[2944,2048]{1,0:T(8,128)(2,1)} %c_hbm.1, f32[8,128]{1,0:T(8,128)S(1)} %get-tuple-element.24._), custom_call_target="tpu_custom_call" | custom-call | flops 1000000 | bytes 100000 | tf_op jit(solution)/shard_map/half0/pallas_call | solution.py:314
  12.8 0.0 collective-permute-done.1.refs_1_
  12.8 0.0 collective-permute-done.refs_0_
  12.8 0.8 %collective-permute-start.4 = (bf16[2,528,128]{2,1,0:T(8,128)(2,1)S(1)}, bf16[2,528,128]{2,1,0:T(8,128)(2,1)S(1)}, u32[]{:S(2)}, u32[]{:S(2)}) collective-permute-start(bf16[2,528,128]{2,1,0:T(8,128)(2,1)S(1)} %join0.1.rest_0_.refs_0_), channel_id=1, source_target_pairs={{0,24},{1,25},{2,26},{3,27},{4,28},{5,29},{6,30},{7,31},{8,16},{9,... | collective-permute-start | bytes 811016 | tf_op jit(solution)/shard_map/ppermute | solution.py:278
  13.6 1.6 %collective-permute-start.5 = (bf16[528,128]{1,0:T(8,128)(2,1)S(1)}, bf16[528,128]{1,0:T(8,128)(2,1)S(1)}, u32[]{:S(2)}, u32[]{:S(2)}) collective-permute-start(bf16[528,128]{1,0:T(8,128)(2,1)S(1)} %get-tuple-element.27), channel_id=1, source_target_pairs={{0,6},{1,7},{2,4},{3,5},{4,2},{5,3},{6,0},{7,1},{8,15},{9,14},{10,... | collective-permute-start | bytes 405512 | tf_op jit(solution)/shard_map/ppermute | solution.py:278
  15.2 0.2 collective-permute-start.3
  15.4 0.3 collective-permute-start.2
  15.8 0.0 copy-done.1
  15.8 2.8 %half1.1 = (bf16[1,384,512]{2,1,0:T(8,128)(2,1)S(1)}, bf16[1,384,512]{2,1,0:T(8,128)(2,1)S(1)}) custom-call(bf16[372,2,2944]{2,1,0:T(2,128)(2,1)S(1)} %copy-done.1, bf16[2944,2048]{1,0:T(8,128)(2,1)S(1)} %get-tuple-element.26.c_ref, bf16[2,528,128]{2,1,0:T(8,128)(2,1)S(1)} %join0.1.rest_0_.refs_0_), custom_call_target="tpu_custom_call" | custom-call | flops 1000000 | bytes 100000 | tf_op jit(solution)/shard_map/half1/pallas_call | solution.py:320
  18.5 4.3 %half2.1 = (bf16[1,384,768]{2,1,0:T(8,128)(2,1)S(1)}, bf16[1,384,768]{2,1,0:T(8,128)(2,1)S(1)}) custom-call(bf16[372,2,2944]{2,1,0:T(2,128)(2,1)S(1)} %copy-done.1, bf16[2944,2048]{1,0:T(8,128)(2,1)S(1)} %get-tuple-element.26.c_ref, bf16[1,384,512]{2,1,0:T(8,128)(2,1)S(1)} %get-tuple-element.28.rest_0_.refs_1_), custom_call_target="tpu_custom_call" | custom-call | flops 1000000 | bytes 100000 | tf_op jit(solution)/shard_map/half2/pallas_call | solution.py:320
  22.9 0.0 copy-start.4
  22.9 1.6 %collective-permute-start.8 = (bf16[1,384,768]{2,1,0:T(8,128)(2,1)S(1)}, bf16[1,384,768]{2,1,0:T(8,128)(2,1)S(1)}, u32[]{:S(2)}, u32[]{:S(2)}) collective-permute-start(bf16[1,384,768]{2,1,0:T(8,128)(2,1)S(1)} %get-tuple-element.33), channel_id=1, source_target_pairs={{0,1},{1,0},{2,3},{3,2},{4,5},{5,4},{6,7},{7,6},{8,9},{9,8},{10,11... | collective-permute-start | bytes 1769480 | tf_op jit(solution)/shard_map/ppermute | solution.py:278
  24.5 0.0 collective-permute-done.5.refs_0_
  24.5 0.1 collective-permute-start.6
  24.6 0.0 collective-permute-done.4.rest_2_.refs_3_
  24.6 0.4 collective-permute-start.7
  25.0 3.0 %collective-permute-done.3.rest_1_.refs_2_ = bf16[2,528,128]{2,1,0:T(8,128)(2,1)S(1)} collective-permute-done((bf16[2,528,128]{2,1,0:T(8,128)(2,1)S(1)}, bf16[2,528,128]{2,1,0:T(8,128)(2,1)S(1)}, u32[]{:S(2)}, u32[]{:S(2)}) %collective-permute-start.3) | collective-permute-done | bytes 270368 | tf_op jit(solution)/shard_map/ppermute | solution.py:278
  28.0 0.0 collective-permute-done.2.rest_0_.refs_1_
  28.0 1.4 %half3.1 = (bf16[1,384,256]{2,1,0:T(8,128)(2,1)S(1)}, bf16[1,384,256]{2,1,0:T(8,128)(2,1)S(1)}) custom-call(bf16[372,2,2944]{2,1,0:T(2,128)(2,1)S(1)} %copy-done.1, bf16[2944,2048]{1,0:T(8,128)(2,1)S(1)} %get-tuple-element.26.c_ref, bf16[2,528,128]{2,1,0:T(8,128)(2,1)S(1)} %collective-permute-done.2.rest_0_.refs_1_, ...), custom_call_target="tpu_custom_call" | custom-call | flops 1000000 | bytes 100000 | tf_op jit(solution)/shard_map/half3/pallas_call | solution.py:320
  29.5 0.6 collective-permute-start.9
  30.1 0.1 collective-permute-start.10
  30.2 0.0 collective-permute-done.6.refs_4_
  30.2 0.6 %collective-permute-start.13 = (bf16[1,528,128]{2,1,0:T(8,128)(2,1)S(1)}, bf16[1,528,128]{2,1,0:T(8,128)(2,1)S(1)}, u32[]{:S(2)}, u32[]{:S(2)}) collective-permute-start(bf16[1,528,128]{2,1,0:T(8,128)(2,1)S(1)} %join1.1.rest_3_.refs_0_), channel_id=1, source_target_pairs={{0,24},{1,25},{2,26},{3,27},{4,28},{5,29},{6,30},{7,31},{8,16},{9,... | collective-permute-start | bytes 405512 | tf_op jit(solution)/shard_map/ppermute | solution.py:278
  30.8 0.0 collective-permute-done.7.refs_5_
  30.8 0.6 collective-permute-start.12
  31.4 0.0 collective-permute-done.9.refs_7_
  31.4 1.4 %collective-permute-start.11 = (bf16[1,528,128]{2,1,0:T(8,128)(2,1)S(1)}, bf16[1,528,128]{2,1,0:T(8,128)(2,1)S(1)}, u32[]{:S(2)}, u32[]{:S(2)}) collective-permute-start(bf16[1,528,128]{2,1,0:T(8,128)(2,1)S(1)} %join1.1.rest_3_.refs_0_), channel_id=1, source_target_pairs={{0,8},{1,9},{2,10},{3,11},{4,12},{5,13},{6,14},{7,15},{8,0},{9,1},... | collective-permute-start | bytes 405512 | tf_op jit(solution)/shard_map/ppermute | solution.py:278
  32.8 0.0 collective-permute-done.8.refs_6_
  32.8 0.0 copy-done.4
  32.8 1.2 %order.1.tiles = bf16[768,2560]{1,0:T(8,128)(2,1)S(1)} custom-call(s32[2,16]{1,0:T(2,128)S(1)} %copy-done.4, bf16[1,384,512]{2,1,0:T(8,128)(2,1)S(1)} %get-tuple-element.25.refs_2_.refs_0_, bf16[1,384,512]{2,1,0:T(8,128)(2,1)S(1)} %get-tuple-element.28.rest_0_.refs_1_, bf16[1,384,768]{2,1,0:T(8,128)(2,1)S(1)} %get-tuple-element.29.refs_1_.refs_2_, ...), custom_call_target="tpu_custom_call" | custom-call | flops 1000000 | bytes 100000 | tf_op jit(solution)/shard_map/order/pallas_call | solution.py:343
  34.0 2.7 %far0.1 = (f32[528,128]{1,0:T(8,128)S(1)}, f32[528,128]{1,0:T(8,128)S(1)}) custom-call(bf16[768,2560]{1,0:T(8,128)(2,1)S(1)} %order.1.tiles, bf16[2,528,128]{2,1,0:T(8,128)(2,1)S(1)} %join0.1.rest_0_.refs_0_, bf16[2,528,128]{2,1,0:T(8,128)(2,1)S(1)} %collective-permute-done.2.rest_0_.refs_1_, ...), custom_call_target="tpu_custom_call" | custom-call | flops 1000000 | bytes 100000 | tf_op jit(solution)/shard_map/far0/pallas_call | solution.py:357
  36.8 2.1 %collective-permute-start.14 = (f16[528,128]{1,0:T(8,128)(2,1)S(1)}, f16[528,128]{1,0:T(8,128)(2,1)S(1)}, u32[]{:S(2)}, u32[]{:S(2)}) collective-permute-start(f16[528,128]{1,0:T(8,128)(2,1)S(1)} %convert_element_type.30), channel_id=1, source_target_pairs={{0,4},{1,5},{2,6},{3,7},{4,0},{5,1},{6,2},{7,3},{8,12},{9,13},{10,... | collective-permute-start | bytes 405512 | tf_op jit(solution)/shard_map/ppermute | solution.py:278
  38.9 0.0 collective-permute-done.13.refs_3_
  38.9 0.0 collective-permute-start.15
  38.9 0.0 collective-permute-done.12.refs_2_
  38.9 0.0 collective-permute-done.11.refs_1_
  38.9 1.4 %far1.1.refs_0_ = f32[528,128]{1,0:T(8,128)S(1)} custom-call(bf16[768,2560]{1,0:T(8,128)(2,1)S(1)} %order.1.tiles, bf16[1,528,128]{2,1,0:T(8,128)(2,1)S(1)} %join1.1.rest_3_.refs_0_, bf16[1,528,128]{2,1,0:T(8,128)(2,1)S(1)} %collective-permute-done.11.refs_1_, bf16[1,528,128]{2,1,0:T(8,128)(2,1)S(1)} %collective-permute-done.12.refs_2_, ...), custom_call_target="tpu_custom_call" | custom-call | flops 1000000 | bytes 100000 | tf_op jit(solution)/shard_map/far1/pallas_call | solution.py:357
  40.4 0.6 collective-permute-start.16
  41.0 0.0 collective-permute-done.10.other
  41.0 1.2 %own.1 = f32[4,128,128]{2,1,0:T(8,128)S(1)} custom-call(bf16[768,2560]{1,0:T(8,128)(2,1)S(1)} %order.1.tiles, bf16[2,528,128]{2,1,0:T(8,128)(2,1)S(1)} %get-tuple-element.35.mine, bf16[2,528,128]{2,1,0:T(8,128)(2,1)S(1)} %collective-permute-done.10.other, f32[528,128]{1,0:T(8,128)S(1)} %far1.1.refs_0_), custom_call_target="tpu_custom_call" | custom-call | flops 1000000 | bytes 100000 | tf_op jit(solution)/shard_map/own/pallas_call | solution.py:366
  42.2 1.2 %collective-permute-done.14 = f16[528,128]{1,0:T(8,128)(2,1)S(1)} collective-permute-done((f16[528,128]{1,0:T(8,128)(2,1)S(1)}, f16[528,128]{1,0:T(8,128)(2,1)S(1)}, u32[]{:S(2)}, u32[]{:S(2)}) %collective-permute-start.14) | collective-permute-done | bytes 135200 | tf_op jit(solution)/shard_map/ppermute | solution.py:278
  43.5 1.0 %collective-permute-done.15 = f16[528,128]{1,0:T(8,128)(2,1)S(1)} collective-permute-done((f16[528,128]{1,0:T(8,128)(2,1)S(1)}, f16[528,128]{1,0:T(8,128)(2,1)S(1)}, u32[]{:S(2)}, u32[]{:S(2)}) %collective-permute-start.15) | collective-permute-done | bytes 135200 | tf_op jit(solution)/shard_map/ppermute | solution.py:278
  44.5 7.2 %collective-permute-done.16 = f16[528,128]{1,0:T(8,128)(2,1)S(1)} collective-permute-done((f16[528,128]{1,0:T(8,128)(2,1)S(1)}, f16[528,128]{1,0:T(8,128)(2,1)S(1)}, u32[]{:S(2)}, u32[]{:S(2)}) %collective-permute-start.16) | collective-permute-done | bytes 135200 | tf_op jit(solution)/shard_map/ppermute | solution.py:278
  51.7 0.2 along.1
  51.9 1.0 %collective-permute-start.19 = (f16[528,128]{1,0:T(8,128)(2,1)S(1)}, f16[528,128]{1,0:T(8,128)(2,1)S(1)}, u32[]{:S(2)}, u32[]{:S(2)}) collective-permute-start(f16[528,128]{1,0:T(8,128)(2,1)S(1)} %convert_element_type.36), channel_id=1, source_target_pairs={{0,24},{1,25},{2,26},{3,27},{4,28},{5,29},{6,30},{7,31},{8,16},{9,... | collective-permute-start | bytes 405512 | tf_op jit(solution)/shard_map/ppermute | solution.py:278
  52.9 0.3 collective-permute-start.18
  53.3 1.4 %collective-permute-start.17 = (f16[528,128]{1,0:T(8,128)(2,1)S(1)}, f16[528,128]{1,0:T(8,128)(2,1)S(1)}, u32[]{:S(2)}, u32[]{:S(2)}) collective-permute-start(f16[528,128]{1,0:T(8,128)(2,1)S(1)} %convert_element_type.36), channel_id=1, source_target_pairs={{0,8},{1,9},{2,10},{3,11},{4,12},{5,13},{6,14},{7,15},{8,0},{9,1},... | collective-permute-start | bytes 405512 | tf_op jit(solution)/shard_map/ppermute | solution.py:278
  54.6 2.7 %collective-permute-done.19 = f16[528,128]{1,0:T(8,128)(2,1)S(1)} collective-permute-done((f16[528,128]{1,0:T(8,128)(2,1)S(1)}, f16[528,128]{1,0:T(8,128)(2,1)S(1)}, u32[]{:S(2)}, u32[]{:S(2)}) %collective-permute-start.19) | collective-permute-done | bytes 135200 | tf_op jit(solution)/shard_map/ppermute | solution.py:278
  57.4 3.9 %collective-permute-done.18 = f16[528,128]{1,0:T(8,128)(2,1)S(1)} collective-permute-done((f16[528,128]{1,0:T(8,128)(2,1)S(1)}, f16[528,128]{1,0:T(8,128)(2,1)S(1)}, u32[]{:S(2)}, u32[]{:S(2)}) %collective-permute-start.18) | collective-permute-done | bytes 135200 | tf_op jit(solution)/shard_map/ppermute | solution.py:278
  61.3 0.0 collective-permute-done.17
  61.4 0.1 around.1
  61.5 0.6 collective-permute-start.20
  62.0 1.0 %collective-permute-done.20.got = f32[2,128,128]{2,1,0:T(8,128)S(1)} collective-permute-done((f32[2,128,128]{2,1,0:T(8,128)S(1)}, f32[2,128,128]{2,1,0:T(8,128)S(1)}, u32[]{:S(2)}, u32[]{:S(2)}) %collective-permute-start.20) | collective-permute-done | bytes 131104 | tf_op jit(solution)/shard_map/ppermute | solution.py:278
  63.0 0.7 %place.1 = f32[2,2,128,128]{3,2,1,0:T(8,128)} custom-call(f32[2,128,128]{2,1,0:T(8,128)S(1)} %get-tuple-element.41.keep, f32[2,128,128]{2,1,0:T(8,128)S(1)} %collective-permute-done.20.got), custom_call_target="tpu_custom_call" | custom-call | flops 1000000 | bytes 100000 | tf_op jit(solution)/shard_map/place/pallas_call | solution.py:379
  (12 shorter events, 0.2 us)
Async XLA Ops:
  0.0 1.0 %copy-start.2 = (bf16[2,2,4,128,128]{4,3,2,1,0:T(8,128)(2,1)S(1)}, bf16[2,2,4,128,128]{4,3,2,1,0:T(8,128)(2,1)}, u32[]{:S(2)}) copy-start(bf16[2,2,4,128,128]{4,3,2,1,0:T(8,128)(2,1)} %amps.1) | copy-start | bytes 1572868
  1.0 0.7 %copy-start.3 = (s32[2,2,4]{2,1,0:T(2,128)S(1)}, s32[2,2,4]{2,1,0:T(2,128)}, u32[]{:S(2)}) copy-start(s32[2,2,4]{2,1,0:T(2,128)} %pairs.1) | copy-start | bytes 196
  2.7 10.1 %collective-permute-start.1 = (bf16[528,128]{1,0:T(8,128)(2,1)S(1)}, bf16[528,128]{1,0:T(8,128)(2,1)S(1)}, u32[]{:S(2)}, u32[]{:S(2)}) collective-permute-start(bf16[528,128]{1,0:T(8,128)(2,1)S(1)} %get-tuple-element.27), channel_id=1, source_target_pairs={{0,2},{1,3},{2,0},{3,1},{4,6},{5,7},{6,4},{7,5},{8,11},{9,10},{10,... | collective-permute-start | bytes 405512 | tf_op jit(solution)/shard_map/ppermute | solution.py:278
  3.5 9.3 %collective-permute-start = (bf16[528,128]{1,0:T(8,128)(2,1)S(1)}, bf16[528,128]{1,0:T(8,128)(2,1)S(1)}, u32[]{:S(2)}, u32[]{:S(2)}) collective-permute-start(bf16[528,128]{1,0:T(8,128)(2,1)S(1)} %get-tuple-element.27), channel_id=1, source_target_pairs={{0,4},{1,5},{2,6},{3,7},{4,0},{5,1},{6,2},{7,3},{8,13},{9,12},{10,... | collective-permute-start | bytes 405512 | tf_op jit(solution)/shard_map/ppermute | solution.py:278
  5.7 2.2 %copy-start = (bf16[372,2,2944]{2,1,0:T(2,128)(2,1)S(1)}, bf16[372,2,2944]{2,1,0:T(2,128)(2,1)}, u32[]{:S(2)}) copy-start(bf16[372,2,2944]{2,1,0:T(2,128)(2,1)} %x_ref.7) | copy-start | bytes 13142020
  7.9 7.8 %copy-start.1 = (bf16[372,2,2944]{2,1,0:T(2,128)(2,1)S(1)}, bf16[372,2,2944]{2,1,0:T(2,128)(2,1)}, u32[]{:S(2)}) copy-start(bf16[372,2,2944]{2,1,0:T(2,128)(2,1)} %x_ref.7) | copy-start | bytes 13142020
  12.8 11.8 %collective-permute-start.4 = (bf16[2,528,128]{2,1,0:T(8,128)(2,1)S(1)}, bf16[2,528,128]{2,1,0:T(8,128)(2,1)S(1)}, u32[]{:S(2)}, u32[]{:S(2)}) collective-permute-start(bf16[2,528,128]{2,1,0:T(8,128)(2,1)S(1)} %join0.1.rest_0_.refs_0_), channel_id=1, source_target_pairs={{0,24},{1,25},{2,26},{3,27},{4,28},{5,29},{6,30},{7,31},{8,16},{9,... | collective-permute-start | bytes 811016 | tf_op jit(solution)/shard_map/ppermute | solution.py:278
  13.6 10.9 %collective-permute-start.5 = (bf16[528,128]{1,0:T(8,128)(2,1)S(1)}, bf16[528,128]{1,0:T(8,128)(2,1)S(1)}, u32[]{:S(2)}, u32[]{:S(2)}) collective-permute-start(bf16[528,128]{1,0:T(8,128)(2,1)S(1)} %get-tuple-element.27), channel_id=1, source_target_pairs={{0,6},{1,7},{2,4},{3,5},{4,2},{5,3},{6,0},{7,1},{8,15},{9,14},{10,... | collective-permute-start | bytes 405512 | tf_op jit(solution)/shard_map/ppermute | solution.py:278
  15.2 12.8 %collective-permute-start.3 = (bf16[2,528,128]{2,1,0:T(8,128)(2,1)S(1)}, bf16[2,528,128]{2,1,0:T(8,128)(2,1)S(1)}, u32[]{:S(2)}, u32[]{:S(2)}) collective-permute-start(bf16[2,528,128]{2,1,0:T(8,128)(2,1)S(1)} %join0.1.rest_0_.refs_0_), channel_id=1, source_target_pairs={{0,16},{1,17},{2,18},{3,19},{4,20},{5,21},{6,22},{7,23},{8,24},{9,... | collective-permute-start | bytes 811016 | tf_op jit(solution)/shard_map/ppermute | solution.py:278
  15.4 12.6 %collective-permute-start.2 = (bf16[2,528,128]{2,1,0:T(8,128)(2,1)S(1)}, bf16[2,528,128]{2,1,0:T(8,128)(2,1)S(1)}, u32[]{:S(2)}, u32[]{:S(2)}) collective-permute-start(bf16[2,528,128]{2,1,0:T(8,128)(2,1)S(1)} %join0.1.rest_0_.refs_0_), channel_id=1, source_target_pairs={{0,8},{1,9},{2,10},{3,11},{4,12},{5,13},{6,14},{7,15},{8,0},{9,1},... | collective-permute-start | bytes 811016 | tf_op jit(solution)/shard_map/ppermute | solution.py:278
  22.9 9.9 %copy-start.4 = (s32[2,16]{1,0:T(2,128)S(1)}, s32[2,16]{1,0:T(2,128)}, u32[]{:S(2)}) copy-start(s32[2,16]{1,0:T(2,128)} %owned.1) | copy-start | bytes 388
  22.9 9.9 %collective-permute-start.8 = (bf16[1,384,768]{2,1,0:T(8,128)(2,1)S(1)}, bf16[1,384,768]{2,1,0:T(8,128)(2,1)S(1)}, u32[]{:S(2)}, u32[]{:S(2)}) collective-permute-start(bf16[1,384,768]{2,1,0:T(8,128)(2,1)S(1)} %get-tuple-element.33), channel_id=1, source_target_pairs={{0,1},{1,0},{2,3},{3,2},{4,5},{5,4},{6,7},{7,6},{8,9},{9,8},{10,11... | collective-permute-start | bytes 1769480 | tf_op jit(solution)/shard_map/ppermute | solution.py:278
  24.5 5.6 %collective-permute-start.6 = (bf16[1,384,512]{2,1,0:T(8,128)(2,1)S(1)}, bf16[1,384,512]{2,1,0:T(8,128)(2,1)S(1)}, u32[]{:S(2)}, u32[]{:S(2)}) collective-permute-start(bf16[1,384,512]{2,1,0:T(8,128)(2,1)S(1)} %get-tuple-element.31), channel_id=1, source_target_pairs={{0,1},{1,0},{2,3},{3,2},{4,5},{5,4},{6,7},{7,6},{8,9},{9,8},{10,11... | collective-permute-start | bytes 1179656 | tf_op jit(solution)/shard_map/ppermute | solution.py:278
  24.6 6.2 %collective-permute-start.7 = (bf16[1,384,512]{2,1,0:T(8,128)(2,1)S(1)}, bf16[1,384,512]{2,1,0:T(8,128)(2,1)S(1)}, u32[]{:S(2)}, u32[]{:S(2)}) collective-permute-start(bf16[1,384,512]{2,1,0:T(8,128)(2,1)S(1)} %get-tuple-element.32), channel_id=1, source_target_pairs={{0,1},{1,0},{2,3},{3,2},{4,5},{5,4},{6,7},{7,6},{8,9},{9,8},{10,11... | collective-permute-start | bytes 1179656 | tf_op jit(solution)/shard_map/ppermute | solution.py:278
  29.5 1.9 %collective-permute-start.9 = (bf16[1,384,256]{2,1,0:T(8,128)(2,1)S(1)}, bf16[1,384,256]{2,1,0:T(8,128)(2,1)S(1)}, u32[]{:S(2)}, u32[]{:S(2)}) collective-permute-start(bf16[1,384,256]{2,1,0:T(8,128)(2,1)S(1)} %get-tuple-element.34), channel_id=1, source_target_pairs={{0,1},{1,0},{2,3},{3,2},{4,5},{5,4},{6,7},{7,6},{8,9},{9,8},{10,11... | collective-permute-start | bytes 589832 | tf_op jit(solution)/shard_map/ppermute | solution.py:278
  30.1 10.9 %collective-permute-start.10 = (bf16[2,528,128]{2,1,0:T(8,128)(2,1)S(1)}, bf16[2,528,128]{2,1,0:T(8,128)(2,1)S(1)}, u32[]{:S(2)}, u32[]{:S(2)}) collective-permute-start(bf16[2,528,128]{2,1,0:T(8,128)(2,1)S(1)} %get-tuple-element.36), channel_id=1, source_target_pairs={{0,1},{1,0},{2,3},{3,2},{4,5},{5,4},{6,7},{7,6},{8,9},{9,8},{10,11... | collective-permute-start | bytes 811016 | tf_op jit(solution)/shard_map/ppermute | solution.py:278
  30.2 8.8 %collective-permute-start.13 = (bf16[1,528,128]{2,1,0:T(8,128)(2,1)S(1)}, bf16[1,528,128]{2,1,0:T(8,128)(2,1)S(1)}, u32[]{:S(2)}, u32[]{:S(2)}) collective-permute-start(bf16[1,528,128]{2,1,0:T(8,128)(2,1)S(1)} %join1.1.rest_3_.refs_0_), channel_id=1, source_target_pairs={{0,24},{1,25},{2,26},{3,27},{4,28},{5,29},{6,30},{7,31},{8,16},{9,... | collective-permute-start | bytes 405512 | tf_op jit(solution)/shard_map/ppermute | solution.py:278
  30.8 8.1 %collective-permute-start.12 = (bf16[1,528,128]{2,1,0:T(8,128)(2,1)S(1)}, bf16[1,528,128]{2,1,0:T(8,128)(2,1)S(1)}, u32[]{:S(2)}, u32[]{:S(2)}) collective-permute-start(bf16[1,528,128]{2,1,0:T(8,128)(2,1)S(1)} %join1.1.rest_3_.refs_0_), channel_id=1, source_target_pairs={{0,16},{1,17},{2,18},{3,19},{4,20},{5,21},{6,22},{7,23},{8,24},{9,... | collective-permute-start | bytes 405512 | tf_op jit(solution)/shard_map/ppermute | solution.py:278
  31.4 7.6 %collective-permute-start.11 = (bf16[1,528,128]{2,1,0:T(8,128)(2,1)S(1)}, bf16[1,528,128]{2,1,0:T(8,128)(2,1)S(1)}, u32[]{:S(2)}, u32[]{:S(2)}) collective-permute-start(bf16[1,528,128]{2,1,0:T(8,128)(2,1)S(1)} %join1.1.rest_3_.refs_0_), channel_id=1, source_target_pairs={{0,8},{1,9},{2,10},{3,11},{4,12},{5,13},{6,14},{7,15},{8,0},{9,1},... | collective-permute-start | bytes 405512 | tf_op jit(solution)/shard_map/ppermute | solution.py:278
  36.8 6.7 %collective-permute-start.14 = (f16[528,128]{1,0:T(8,128)(2,1)S(1)}, f16[528,128]{1,0:T(8,128)(2,1)S(1)}, u32[]{:S(2)}, u32[]{:S(2)}) collective-permute-start(f16[528,128]{1,0:T(8,128)(2,1)S(1)} %convert_element_type.30), channel_id=1, source_target_pairs={{0,4},{1,5},{2,6},{3,7},{4,0},{5,1},{6,2},{7,3},{8,12},{9,13},{10,... | collective-permute-start | bytes 405512 | tf_op jit(solution)/shard_map/ppermute | solution.py:278
  38.9 5.5 %collective-permute-start.15 = (f16[528,128]{1,0:T(8,128)(2,1)S(1)}, f16[528,128]{1,0:T(8,128)(2,1)S(1)}, u32[]{:S(2)}, u32[]{:S(2)}) collective-permute-start(f16[528,128]{1,0:T(8,128)(2,1)S(1)} %convert_element_type.32), channel_id=1, source_target_pairs={{0,2},{1,3},{2,0},{3,1},{4,6},{5,7},{6,4},{7,5},{8,10},{9,11},{10,... | collective-permute-start | bytes 405512 | tf_op jit(solution)/shard_map/ppermute | solution.py:278
  40.4 11.3 %collective-permute-start.16 = (f16[528,128]{1,0:T(8,128)(2,1)S(1)}, f16[528,128]{1,0:T(8,128)(2,1)S(1)}, u32[]{:S(2)}, u32[]{:S(2)}) collective-permute-start(f16[528,128]{1,0:T(8,128)(2,1)S(1)} %convert_element_type.34), channel_id=1, source_target_pairs={{0,6},{1,7},{2,4},{3,5},{4,2},{5,3},{6,0},{7,1},{8,14},{9,15},{10,... | collective-permute-start | bytes 405512 | tf_op jit(solution)/shard_map/ppermute | solution.py:278
  51.9 5.4 %collective-permute-start.19 = (f16[528,128]{1,0:T(8,128)(2,1)S(1)}, f16[528,128]{1,0:T(8,128)(2,1)S(1)}, u32[]{:S(2)}, u32[]{:S(2)}) collective-permute-start(f16[528,128]{1,0:T(8,128)(2,1)S(1)} %convert_element_type.36), channel_id=1, source_target_pairs={{0,24},{1,25},{2,26},{3,27},{4,28},{5,29},{6,30},{7,31},{8,16},{9,... | collective-permute-start | bytes 405512 | tf_op jit(solution)/shard_map/ppermute | solution.py:278
  52.9 8.4 %collective-permute-start.18 = (f16[528,128]{1,0:T(8,128)(2,1)S(1)}, f16[528,128]{1,0:T(8,128)(2,1)S(1)}, u32[]{:S(2)}, u32[]{:S(2)}) collective-permute-start(f16[528,128]{1,0:T(8,128)(2,1)S(1)} %convert_element_type.36), channel_id=1, source_target_pairs={{0,16},{1,17},{2,18},{3,19},{4,20},{5,21},{6,22},{7,23},{8,24},{9,... | collective-permute-start | bytes 405512 | tf_op jit(solution)/shard_map/ppermute | solution.py:278
  53.3 8.1 %collective-permute-start.17 = (f16[528,128]{1,0:T(8,128)(2,1)S(1)}, f16[528,128]{1,0:T(8,128)(2,1)S(1)}, u32[]{:S(2)}, u32[]{:S(2)}) collective-permute-start(f16[528,128]{1,0:T(8,128)(2,1)S(1)} %convert_element_type.36), channel_id=1, source_target_pairs={{0,8},{1,9},{2,10},{3,11},{4,12},{5,13},{6,14},{7,15},{8,0},{9,1},... | collective-permute-start | bytes 405512 | tf_op jit(solution)/shard_map/ppermute | solution.py:278
  61.5 1.5 %collective-permute-start.20 = (f32[2,128,128]{2,1,0:T(8,128)S(1)}, f32[2,128,128]{2,1,0:T(8,128)S(1)}, u32[]{:S(2)}, u32[]{:S(2)}) collective-permute-start(f32[2,128,128]{2,1,0:T(8,128)S(1)} %get-tuple-element.42), channel_id=1, source_target_pairs={{0,1},{1,0},{2,3},{3,2},{4,5},{5,4},{6,7},{7,6},{8,9},{9,8},{10,11... | collective-permute-start | bytes 393224 | tf_op jit(solution)/shard_map/ppermute | solution.py:278

commit v5 on v4

--- a/solution.py
+++ b/solution.py
@@ -98,7 +98,7 @@
         x_ref[...].reshape(rows * occ, ao), c_ref[:, start : start + count], preferred_element_type=F32
     )
     for n in range(count // 128):
-        acc[n] = prod[:, n * 128 : (n + 1) * 128]
+        acc[n, : rows * occ, :] = prod[:, n * 128 : (n + 1) * 128]
     for i in range(batch_occ):
         for n in range(count // 128):
             lanes = slice(at + n * 128, at + (n + 1) * 128)
@@ -304,7 +304,7 @@
     far = []
 
     first_cols = STEPS[0] * cols
-    acc = pltpu.VMEM((first_cols // 128, rows * occ, 128), F32)
+    acc = pltpu.VMEM((first_cols // 128, (-(-rows // 8) * 8 + 8) * occ, 128), F32)
     y_mine, y_other = [], []
     start = 0
     for step, count in enumerate(STEPS):

time: 63.9 us -> 64 us (level)
  transfers between devices with their start and end apart: 21 -> 21, of which waited for: 7 -> 8; matrix products, arithmetic and copies ran while one was open for 0% -> 0% of each run, Pallas kernels for 31% -> 31%
where the time goes in v5:
time: 64 us; the launch traced here: 63.8 us
  Pallas kernels  22 us (34%)
  waiting for transfers between devices  20 us (31%)
  starting transfers between devices  17.4 us (27%)
  local copies, waits for them, and re-layouts  3.97 us (6%)
    ppermute x21, waiting for transfers between devices, exchange(): return lax.ppermute(x, AXES, perm)  20 us
    ppermute x21, starting transfers between devices, exchange(): return lax.ppermute(x, AXES, perm)  17.4 us
    pallas_call x3, Pallas kernels, per_device(): call('half%d' % step, functools.partial(half_kernel, batch_occ=batch_occ,...  8.64 us
    pallas_call x1, Pallas kernels, per_device(): call('half0', functools.partial(first_half_kernel, batch_occ=batch_occ),...  4.85 us
    pallas_call x2, Pallas kernels, per_device(): call('far%d' % n, functools.partial(far_kernel, distances=distances, **si...  4.04 us
    unnamed x10, local copies, waits for them, and re-layouts  3.97 us
  transfers between devices with their start and end apart: 21, of which 8 were waited for; matrix products, arithmetic and copies ran while one was open for 0% of the time, Pallas kernels for 31%

profile of v5, /device:TPU:11, one launch (start us, length us, event | category | flops | bytes accessed | tf_op | source)
XLA Modules:
  0.0 63.8 jit_solution(13431709135063042712)
XLA Ops:
  0.0 0.0 copy-start.2
  0.0 1.0 %copy-done.2 = bf16[2,2,4,128,128]{4,3,2,1,0:T(8,128)(2,1)S(1)} copy-done((bf16[2,2,4,128,128]{4,3,2,1,0:T(8,128)(2,1)S(1)}, bf16[2,2,4,128,128]{4,3,2,1,0:T(8,128)(2,1)}, u32[]{:S(2)}) %copy-start.2) | copy-done | bytes 524312
  1.0 0.0 copy-start.3
  1.0 0.7 %copy-done.3 = s32[2,2,4]{2,1,0:T(2,128)S(1)} copy-done((s32[2,2,4]{2,1,0:T(2,128)S(1)}, s32[2,2,4]{2,1,0:T(2,128)}, u32[]{:S(2)}) %copy-start.3) | copy-done | bytes 88
  1.7 1.0 %pack.1 = (bf16[528,128]{1,0:T(8,128)(2,1)S(1)}, bf16[2,528,128]{2,1,0:T(8,128)(2,1)S(1)}, bf16[2,528,128]{2,1,0:T(8,128)(2,1)S(1)}, f32[8,128]{1,0:T(8,128)S(1)}) custom-call(s32[2,2,4]{2,1,0:T(2,128)S(1)} %copy-done.3, bf16[2,2,4,128,128]{4,3,2,1,0:T(8,128)(2,1)S(1)} %copy-done.2), custom_call_target="tpu_custom_call" | custom-call | flops 1000000 | bytes 100000 | tf_op jit(solution)/shard_map/pack/pallas_call | solution.py:292
  2.7 0.8 %collective-permute-start.1 = (bf16[528,128]{1,0:T(8,128)(2,1)S(1)}, bf16[528,128]{1,0:T(8,128)(2,1)S(1)}, u32[]{:S(2)}, u32[]{:S(2)}) collective-permute-start(bf16[528,128]{1,0:T(8,128)(2,1)S(1)} %get-tuple-element.27), channel_id=1, source_target_pairs={{0,2},{1,3},{2,0},{3,1},{4,6},{5,7},{6,4},{7,5},{8,11},{9,10},{10,... | collective-permute-start | bytes 405512 | tf_op jit(solution)/shard_map/ppermute | solution.py:278
  3.5 2.2 %collective-permute-start = (bf16[528,128]{1,0:T(8,128)(2,1)S(1)}, bf16[528,128]{1,0:T(8,128)(2,1)S(1)}, u32[]{:S(2)}, u32[]{:S(2)}) collective-permute-start(bf16[528,128]{1,0:T(8,128)(2,1)S(1)} %get-tuple-element.27), channel_id=1, source_target_pairs={{0,4},{1,5},{2,6},{3,7},{4,0},{5,1},{6,2},{7,3},{8,13},{9,12},{10,... | collective-permute-start | bytes 405512 | tf_op jit(solution)/shard_map/ppermute | solution.py:278
  5.7 0.0 copy-start
  5.7 2.2 %copy-done = bf16[372,2,2944]{2,1,0:T(2,128)(2,1)S(1)} copy-done((bf16[372,2,2944]{2,1,0:T(2,128)(2,1)S(1)}, bf16[372,2,2944]{2,1,0:T(2,128)(2,1)}, u32[]{:S(2)}) %copy-start) | copy-done | bytes 4380696
  7.9 0.0 copy-start.1
  7.9 4.9 %half0.1 = (bf16[1,384,512]{2,1,0:T(8,128)(2,1)S(1)}, bf16[1,384,512]{2,1,0:T(8,128)(2,1)S(1)}, bf16[2944,2048]{1,0:T(8,128)(2,1)S(1)}) custom-call(bf16[372,2,2944]{2,1,0:T(2,128)(2,1)S(1)} %copy-done, bf16[2944,2048]{1,0:T(8,128)(2,1)} %c_hbm.1, f32[8,128]{1,0:T(8,128)S(1)} %get-tuple-element.24._), custom_call_target="tpu_custom_call" | custom-call | flops 1000000 | bytes 100000 | tf_op jit(solution)/shard_map/half0/pallas_call | solution.py:314
  12.8 0.0 collective-permute-done.1.refs_1_
  12.8 0.0 collective-permute-done.refs_0_
  12.9 0.8 %collective-permute-start.4 = (bf16[2,528,128]{2,1,0:T(8,128)(2,1)S(1)}, bf16[2,528,128]{2,1,0:T(8,128)(2,1)S(1)}, u32[]{:S(2)}, u32[]{:S(2)}) collective-permute-start(bf16[2,528,128]{2,1,0:T(8,128)(2,1)S(1)} %join0.1.rest_0_.refs_0_), channel_id=1, source_target_pairs={{0,24},{1,25},{2,26},{3,27},{4,28},{5,29},{6,30},{7,31},{8,16},{9,... | collective-permute-start | bytes 811016 | tf_op jit(solution)/shard_map/ppermute | solution.py:278
  13.7 1.6 %collective-permute-start.5 = (bf16[528,128]{1,0:T(8,128)(2,1)S(1)}, bf16[528,128]{1,0:T(8,128)(2,1)S(1)}, u32[]{:S(2)}, u32[]{:S(2)}) collective-permute-start(bf16[528,128]{1,0:T(8,128)(2,1)S(1)} %get-tuple-element.27), channel_id=1, source_target_pairs={{0,6},{1,7},{2,4},{3,5},{4,2},{5,3},{6,0},{7,1},{8,15},{9,14},{10,... | collective-permute-start | bytes 405512 | tf_op jit(solution)/shard_map/ppermute | solution.py:278
  15.2 0.2 collective-permute-start.3
  15.5 0.3 collective-permute-start.2
  15.8 0.0 copy-done.1
  15.8 2.8 %half1.1 = (bf16[1,384,512]{2,1,0:T(8,128)(2,1)S(1)}, bf16[1,384,512]{2,1,0:T(8,128)(2,1)S(1)}) custom-call(bf16[372,2,2944]{2,1,0:T(2,128)(2,1)S(1)} %copy-done.1, bf16[2944,2048]{1,0:T(8,128)(2,1)S(1)} %get-tuple-element.26.c_ref, bf16[2,528,128]{2,1,0:T(8,128)(2,1)S(1)} %join0.1.rest_0_.refs_0_), custom_call_target="tpu_custom_call" | custom-call | flops 1000000 | bytes 100000 | tf_op jit(solution)/shard_map/half1/pallas_call | solution.py:320
  18.6 4.4 %half2.1 = (bf16[1,384,768]{2,1,0:T(8,128)(2,1)S(1)}, bf16[1,384,768]{2,1,0:T(8,128)(2,1)S(1)}) custom-call(bf16[372,2,2944]{2,1,0:T(2,128)(2,1)S(1)} %copy-done.1, bf16[2944,2048]{1,0:T(8,128)(2,1)S(1)} %get-tuple-element.26.c_ref, bf16[1,384,512]{2,1,0:T(8,128)(2,1)S(1)} %get-tuple-element.28.rest_0_.refs_1_), custom_call_target="tpu_custom_call" | custom-call | flops 1000000 | bytes 100000 | tf_op jit(solution)/shard_map/half2/pallas_call | solution.py:320
  23.0 0.0 copy-start.4
  23.0 1.6 %collective-permute-start.8 = (bf16[1,384,768]{2,1,0:T(8,128)(2,1)S(1)}, bf16[1,384,768]{2,1,0:T(8,128)(2,1)S(1)}, u32[]{:S(2)}, u32[]{:S(2)}) collective-permute-start(bf16[1,384,768]{2,1,0:T(8,128)(2,1)S(1)} %get-tuple-element.33), channel_id=1, source_target_pairs={{0,1},{1,0},{2,3},{3,2},{4,5},{5,4},{6,7},{7,6},{8,9},{9,8},{10,11... | collective-permute-start | bytes 1769480 | tf_op jit(solution)/shard_map/ppermute | solution.py:278
  24.6 0.0 collective-permute-done.5.refs_0_
  24.6 0.1 collective-permute-start.6
  24.7 0.0 collective-permute-done.4.rest_2_.refs_3_
  24.7 0.4 collective-permute-start.7
  25.2 2.9 %collective-permute-done.3.rest_1_.refs_2_ = bf16[2,528,128]{2,1,0:T(8,128)(2,1)S(1)} collective-permute-done((bf16[2,528,128]{2,1,0:T(8,128)(2,1)S(1)}, bf16[2,528,128]{2,1,0:T(8,128)(2,1)S(1)}, u32[]{:S(2)}, u32[]{:S(2)}) %collective-permute-start.3) | collective-permute-done | bytes 270368 | tf_op jit(solution)/shard_map/ppermute | solution.py:278
  28.1 0.0 collective-permute-done.2.rest_0_.refs_1_
  28.1 1.4 %half3.1 = (bf16[1,384,256]{2,1,0:T(8,128)(2,1)S(1)}, bf16[1,384,256]{2,1,0:T(8,128)(2,1)S(1)}) custom-call(bf16[372,2,2944]{2,1,0:T(2,128)(2,1)S(1)} %copy-done.1, bf16[2944,2048]{1,0:T(8,128)(2,1)S(1)} %get-tuple-element.26.c_ref, bf16[2,528,128]{2,1,0:T(8,128)(2,1)S(1)} %collective-permute-done.2.rest_0_.refs_1_, ...), custom_call_target="tpu_custom_call" | custom-call | flops 1000000 | bytes 100000 | tf_op jit(solution)/shard_map/half3/pallas_call | solution.py:320
  29.5 0.6 collective-permute-start.9
  30.1 0.1 collective-permute-start.10
  30.2 0.0 collective-permute-done.6.refs_4_
  30.2 0.6 %collective-permute-start.13 = (bf16[1,528,128]{2,1,0:T(8,128)(2,1)S(1)}, bf16[1,528,128]{2,1,0:T(8,128)(2,1)S(1)}, u32[]{:S(2)}, u32[]{:S(2)}) collective-permute-start(bf16[1,528,128]{2,1,0:T(8,128)(2,1)S(1)} %join1.1.rest_3_.refs_0_), channel_id=1, source_target_pairs={{0,24},{1,25},{2,26},{3,27},{4,28},{5,29},{6,30},{7,31},{8,16},{9,... | collective-permute-start | bytes 405512 | tf_op jit(solution)/shard_map/ppermute | solution.py:278
  30.9 0.0 collective-permute-done.7.refs_5_
  30.9 0.6 collective-permute-start.12
  31.4 0.0 collective-permute-done.9.refs_7_
  31.4 1.4 %collective-permute-start.11 = (bf16[1,528,128]{2,1,0:T(8,128)(2,1)S(1)}, bf16[1,528,128]{2,1,0:T(8,128)(2,1)S(1)}, u32[]{:S(2)}, u32[]{:S(2)}) collective-permute-start(bf16[1,528,128]{2,1,0:T(8,128)(2,1)S(1)} %join1.1.rest_3_.refs_0_), channel_id=1, source_target_pairs={{0,8},{1,9},{2,10},{3,11},{4,12},{5,13},{6,14},{7,15},{8,0},{9,1},... | collective-permute-start | bytes 405512 | tf_op jit(solution)/shard_map/ppermute | solution.py:278
  32.9 0.0 collective-permute-done.8.refs_6_
  32.9 0.0 copy-done.4
  32.9 1.2 %order.1.tiles = bf16[768,2560]{1,0:T(8,128)(2,1)S(1)} custom-call(s32[2,16]{1,0:T(2,128)S(1)} %copy-done.4, bf16[1,384,512]{2,1,0:T(8,128)(2,1)S(1)} %get-tuple-element.25.refs_2_.refs_0_, bf16[1,384,512]{2,1,0:T(8,128)(2,1)S(1)} %get-tuple-element.28.rest_0_.refs_1_, bf16[1,384,768]{2,1,0:T(8,128)(2,1)S(1)} %get-tuple-element.29.refs_1_.refs_2_, ...), custom_call_target="tpu_custom_call" | custom-call | flops 1000000 | bytes 100000 | tf_op jit(solution)/shard_map/order/pallas_call | solution.py:343
  34.1 2.7 %far0.1 = (f32[528,128]{1,0:T(8,128)S(1)}, f32[528,128]{1,0:T(8,128)S(1)}) custom-call(bf16[768,2560]{1,0:T(8,128)(2,1)S(1)} %order.1.tiles, bf16[2,528,128]{2,1,0:T(8,128)(2,1)S(1)} %join0.1.rest_0_.refs_0_, bf16[2,528,128]{2,1,0:T(8,128)(2,1)S(1)} %collective-permute-done.2.rest_0_.refs_1_, ...), custom_call_target="tpu_custom_call" | custom-call | flops 1000000 | bytes 100000 | tf_op jit(solution)/shard_map/far0/pallas_call | solution.py:357
  36.8 2.1 %collective-permute-start.14 = (f16[528,128]{1,0:T(8,128)(2,1)S(1)}, f16[528,128]{1,0:T(8,128)(2,1)S(1)}, u32[]{:S(2)}, u32[]{:S(2)}) collective-permute-start(f16[528,128]{1,0:T(8,128)(2,1)S(1)} %convert_element_type.30), channel_id=1, source_target_pairs={{0,4},{1,5},{2,6},{3,7},{4,0},{5,1},{6,2},{7,3},{8,12},{9,13},{10,... | collective-permute-start | bytes 405512 | tf_op jit(solution)/shard_map/ppermute | solution.py:278
  38.9 0.0 collective-permute-done.13.refs_3_
  38.9 0.0 collective-permute-start.15
  38.9 0.1 collective-permute-done.12.refs_2_
  39.0 0.0 collective-permute-done.11.refs_1_
  39.0 1.4 %far1.1.refs_0_ = f32[528,128]{1,0:T(8,128)S(1)} custom-call(bf16[768,2560]{1,0:T(8,128)(2,1)S(1)} %order.1.tiles, bf16[1,528,128]{2,1,0:T(8,128)(2,1)S(1)} %join1.1.rest_3_.refs_0_, bf16[1,528,128]{2,1,0:T(8,128)(2,1)S(1)} %collective-permute-done.11.refs_1_, bf16[1,528,128]{2,1,0:T(8,128)(2,1)S(1)} %collective-permute-done.12.refs_2_, ...), custom_call_target="tpu_custom_call" | custom-call | flops 1000000 | bytes 100000 | tf_op jit(solution)/shard_map/far1/pallas_call | solution.py:357
  40.4 0.6 collective-permute-start.16
  41.0 0.0 collective-permute-done.10.other
  41.0 1.2 %own.1 = f32[4,128,128]{2,1,0:T(8,128)S(1)} custom-call(bf16[768,2560]{1,0:T(8,128)(2,1)S(1)} %order.1.tiles, bf16[2,528,128]{2,1,0:T(8,128)(2,1)S(1)} %get-tuple-element.35.mine, bf16[2,528,128]{2,1,0:T(8,128)(2,1)S(1)} %collective-permute-done.10.other, f32[528,128]{1,0:T(8,128)S(1)} %far1.1.refs_0_), custom_call_target="tpu_custom_call" | custom-call | flops 1000000 | bytes 100000 | tf_op jit(solution)/shard_map/own/pallas_call | solution.py:366
  42.3 1.2 %collective-permute-done.14 = f16[528,128]{1,0:T(8,128)(2,1)S(1)} collective-permute-done((f16[528,128]{1,0:T(8,128)(2,1)S(1)}, f16[528,128]{1,0:T(8,128)(2,1)S(1)}, u32[]{:S(2)}, u32[]{:S(2)}) %collective-permute-start.14) | collective-permute-done | bytes 135200 | tf_op jit(solution)/shard_map/ppermute | solution.py:278
  43.5 0.9 %collective-permute-done.15 = f16[528,128]{1,0:T(8,128)(2,1)S(1)} collective-permute-done((f16[528,128]{1,0:T(8,128)(2,1)S(1)}, f16[528,128]{1,0:T(8,128)(2,1)S(1)}, u32[]{:S(2)}, u32[]{:S(2)}) %collective-permute-start.15) | collective-permute-done | bytes 135200 | tf_op jit(solution)/shard_map/ppermute | solution.py:278
  44.4 7.3 %collective-permute-done.16 = f16[528,128]{1,0:T(8,128)(2,1)S(1)} collective-permute-done((f16[528,128]{1,0:T(8,128)(2,1)S(1)}, f16[528,128]{1,0:T(8,128)(2,1)S(1)}, u32[]{:S(2)}, u32[]{:S(2)}) %collective-permute-start.16) | collective-permute-done | bytes 135200 | tf_op jit(solution)/shard_map/ppermute | solution.py:278
  51.7 0.2 along.1
  52.0 1.0 %collective-permute-start.19 = (f16[528,128]{1,0:T(8,128)(2,1)S(1)}, f16[528,128]{1,0:T(8,128)(2,1)S(1)}, u32[]{:S(2)}, u32[]{:S(2)}) collective-permute-start(f16[528,128]{1,0:T(8,128)(2,1)S(1)} %convert_element_type.36), channel_id=1, source_target_pairs={{0,24},{1,25},{2,26},{3,27},{4,28},{5,29},{6,30},{7,31},{8,16},{9,... | collective-permute-start | bytes 405512 | tf_op jit(solution)/shard_map/ppermute | solution.py:278
  53.0 0.3 collective-permute-start.18
  53.3 1.4 %collective-permute-start.17 = (f16[528,128]{1,0:T(8,128)(2,1)S(1)}, f16[528,128]{1,0:T(8,128)(2,1)S(1)}, u32[]{:S(2)}, u32[]{:S(2)}) collective-permute-start(f16[528,128]{1,0:T(8,128)(2,1)S(1)} %convert_element_type.36), channel_id=1, source_target_pairs={{0,8},{1,9},{2,10},{3,11},{4,12},{5,13},{6,14},{7,15},{8,0},{9,1},... | collective-permute-start | bytes 405512 | tf_op jit(solution)/shard_map/ppermute | solution.py:278
  54.7 2.7 %collective-permute-done.19 = f16[528,128]{1,0:T(8,128)(2,1)S(1)} collective-permute-done((f16[528,128]{1,0:T(8,128)(2,1)S(1)}, f16[528,128]{1,0:T(8,128)(2,1)S(1)}, u32[]{:S(2)}, u32[]{:S(2)}) %collective-permute-start.19) | collective-permute-done | bytes 135200 | tf_op jit(solution)/shard_map/ppermute | solution.py:278
  57.4 3.9 %collective-permute-done.18 = f16[528,128]{1,0:T(8,128)(2,1)S(1)} collective-permute-done((f16[528,128]{1,0:T(8,128)(2,1)S(1)}, f16[528,128]{1,0:T(8,128)(2,1)S(1)}, u32[]{:S(2)}, u32[]{:S(2)}) %collective-permute-start.18) | collective-permute-done | bytes 135200 | tf_op jit(solution)/shard_map/ppermute | solution.py:278
  61.4 0.0 collective-permute-done.17
  61.4 0.1 around.1
  61.5 0.6 collective-permute-start.20
  62.0 1.0 %collective-permute-done.20.got = f32[2,128,128]{2,1,0:T(8,128)S(1)} collective-permute-done((f32[2,128,128]{2,1,0:T(8,128)S(1)}, f32[2,128,128]{2,1,0:T(8,128)S(1)}, u32[]{:S(2)}, u32[]{:S(2)}) %collective-permute-start.20) | collective-permute-done | bytes 131104 | tf_op jit(solution)/shard_map/ppermute | solution.py:278
  63.0 0.7 %place.1 = f32[2,2,128,128]{3,2,1,0:T(8,128)} custom-call(f32[2,128,128]{2,1,0:T(8,128)S(1)} %get-tuple-element.41.keep, f32[2,128,128]{2,1,0:T(8,128)S(1)} %collective-permute-done.20.got), custom_call_target="tpu_custom_call" | custom-call | flops 1000000 | bytes 100000 | tf_op jit(solution)/shard_map/place/pallas_call | solution.py:379
  (12 shorter events, 0.2 us)
Async XLA Ops:
  0.0 1.0 %copy-start.2 = (bf16[2,2,4,128,128]{4,3,2,1,0:T(8,128)(2,1)S(1)}, bf16[2,2,4,128,128]{4,3,2,1,0:T(8,128)(2,1)}, u32[]{:S(2)}) copy-start(bf16[2,2,4,128,128]{4,3,2,1,0:T(8,128)(2,1)} %amps.1) | copy-start | bytes 1572868
  1.0 0.7 %copy-start.3 = (s32[2,2,4]{2,1,0:T(2,128)S(1)}, s32[2,2,4]{2,1,0:T(2,128)}, u32[]{:S(2)}) copy-start(s32[2,2,4]{2,1,0:T(2,128)} %pairs.1) | copy-start | bytes 196
  2.7 10.1 %collective-permute-start.1 = (bf16[528,128]{1,0:T(8,128)(2,1)S(1)}, bf16[528,128]{1,0:T(8,128)(2,1)S(1)}, u32[]{:S(2)}, u32[]{:S(2)}) collective-permute-start(bf16[528,128]{1,0:T(8,128)(2,1)S(1)} %get-tuple-element.27), channel_id=1, source_target_pairs={{0,2},{1,3},{2,0},{3,1},{4,6},{5,7},{6,4},{7,5},{8,11},{9,10},{10,... | collective-permute-start | bytes 405512 | tf_op jit(solution)/shard_map/ppermute | solution.py:278
  3.5 9.3 %collective-permute-start = (bf16[528,128]{1,0:T(8,128)(2,1)S(1)}, bf16[528,128]{1,0:T(8,128)(2,1)S(1)}, u32[]{:S(2)}, u32[]{:S(2)}) collective-permute-start(bf16[528,128]{1,0:T(8,128)(2,1)S(1)} %get-tuple-element.27), channel_id=1, source_target_pairs={{0,4},{1,5},{2,6},{3,7},{4,0},{5,1},{6,2},{7,3},{8,13},{9,12},{10,... | collective-permute-start | bytes 405512 | tf_op jit(solution)/shard_map/ppermute | solution.py:278
  5.7 2.2 %copy-start = (bf16[372,2,2944]{2,1,0:T(2,128)(2,1)S(1)}, bf16[372,2,2944]{2,1,0:T(2,128)(2,1)}, u32[]{:S(2)}) copy-start(bf16[372,2,2944]{2,1,0:T(2,128)(2,1)} %x_ref.7) | copy-start | bytes 13142020
  7.9 7.8 %copy-start.1 = (bf16[372,2,2944]{2,1,0:T(2,128)(2,1)S(1)}, bf16[372,2,2944]{2,1,0:T(2,128)(2,1)}, u32[]{:S(2)}) copy-start(bf16[372,2,2944]{2,1,0:T(2,128)(2,1)} %x_ref.7) | copy-start | bytes 13142020
  12.9 11.9 %collective-permute-start.4 = (bf16[2,528,128]{2,1,0:T(8,128)(2,1)S(1)}, bf16[2,528,128]{2,1,0:T(8,128)(2,1)S(1)}, u32[]{:S(2)}, u32[]{:S(2)}) collective-permute-start(bf16[2,528,128]{2,1,0:T(8,128)(2,1)S(1)} %join0.1.rest_0_.refs_0_), channel_id=1, source_target_pairs={{0,24},{1,25},{2,26},{3,27},{4,28},{5,29},{6,30},{7,31},{8,16},{9,... | collective-permute-start | bytes 811016 | tf_op jit(solution)/shard_map/ppermute | solution.py:278
  13.7 11.0 %collective-permute-start.5 = (bf16[528,128]{1,0:T(8,128)(2,1)S(1)}, bf16[528,128]{1,0:T(8,128)(2,1)S(1)}, u32[]{:S(2)}, u32[]{:S(2)}) collective-permute-start(bf16[528,128]{1,0:T(8,128)(2,1)S(1)} %get-tuple-element.27), channel_id=1, source_target_pairs={{0,6},{1,7},{2,4},{3,5},{4,2},{5,3},{6,0},{7,1},{8,15},{9,14},{10,... | collective-permute-start | bytes 405512 | tf_op jit(solution)/shard_map/ppermute | solution.py:278
  15.2 12.8 %collective-permute-start.3 = (bf16[2,528,128]{2,1,0:T(8,128)(2,1)S(1)}, bf16[2,528,128]{2,1,0:T(8,128)(2,1)S(1)}, u32[]{:S(2)}, u32[]{:S(2)}) collective-permute-start(bf16[2,528,128]{2,1,0:T(8,128)(2,1)S(1)} %join0.1.rest_0_.refs_0_), channel_id=1, source_target_pairs={{0,16},{1,17},{2,18},{3,19},{4,20},{5,21},{6,22},{7,23},{8,24},{9,... | collective-permute-start | bytes 811016 | tf_op jit(solution)/shard_map/ppermute | solution.py:278
  15.5 12.6 %collective-permute-start.2 = (bf16[2,528,128]{2,1,0:T(8,128)(2,1)S(1)}, bf16[2,528,128]{2,1,0:T(8,128)(2,1)S(1)}, u32[]{:S(2)}, u32[]{:S(2)}) collective-permute-start(bf16[2,528,128]{2,1,0:T(8,128)(2,1)S(1)} %join0.1.rest_0_.refs_0_), channel_id=1, source_target_pairs={{0,8},{1,9},{2,10},{3,11},{4,12},{5,13},{6,14},{7,15},{8,0},{9,1},... | collective-permute-start | bytes 811016 | tf_op jit(solution)/shard_map/ppermute | solution.py:278
  23.0 9.9 %copy-start.4 = (s32[2,16]{1,0:T(2,128)S(1)}, s32[2,16]{1,0:T(2,128)}, u32[]{:S(2)}) copy-start(s32[2,16]{1,0:T(2,128)} %owned.1) | copy-start | bytes 388
  23.0 9.9 %collective-permute-start.8 = (bf16[1,384,768]{2,1,0:T(8,128)(2,1)S(1)}, bf16[1,384,768]{2,1,0:T(8,128)(2,1)S(1)}, u32[]{:S(2)}, u32[]{:S(2)}) collective-permute-start(bf16[1,384,768]{2,1,0:T(8,128)(2,1)S(1)} %get-tuple-element.33), channel_id=1, source_target_pairs={{0,1},{1,0},{2,3},{3,2},{4,5},{5,4},{6,7},{7,6},{8,9},{9,8},{10,11... | collective-permute-start | bytes 1769480 | tf_op jit(solution)/shard_map/ppermute | solution.py:278
  24.6 5.6 %collective-permute-start.6 = (bf16[1,384,512]{2,1,0:T(8,128)(2,1)S(1)}, bf16[1,384,512]{2,1,0:T(8,128)(2,1)S(1)}, u32[]{:S(2)}, u32[]{:S(2)}) collective-permute-start(bf16[1,384,512]{2,1,0:T(8,128)(2,1)S(1)} %get-tuple-element.31), channel_id=1, source_target_pairs={{0,1},{1,0},{2,3},{3,2},{4,5},{5,4},{6,7},{7,6},{8,9},{9,8},{10,11... | collective-permute-start | bytes 1179656 | tf_op jit(solution)/shard_map/ppermute | solution.py:278
  24.7 6.1 %collective-permute-start.7 = (bf16[1,384,512]{2,1,0:T(8,128)(2,1)S(1)}, bf16[1,384,512]{2,1,0:T(8,128)(2,1)S(1)}, u32[]{:S(2)}, u32[]{:S(2)}) collective-permute-start(bf16[1,384,512]{2,1,0:T(8,128)(2,1)S(1)} %get-tuple-element.32), channel_id=1, source_target_pairs={{0,1},{1,0},{2,3},{3,2},{4,5},{5,4},{6,7},{7,6},{8,9},{9,8},{10,11... | collective-permute-start | bytes 1179656 | tf_op jit(solution)/shard_map/ppermute | solution.py:278
  29.5 1.9 %collective-permute-start.9 = (bf16[1,384,256]{2,1,0:T(8,128)(2,1)S(1)}, bf16[1,384,256]{2,1,0:T(8,128)(2,1)S(1)}, u32[]{:S(2)}, u32[]{:S(2)}) collective-permute-start(bf16[1,384,256]{2,1,0:T(8,128)(2,1)S(1)} %get-tuple-element.34), channel_id=1, source_target_pairs={{0,1},{1,0},{2,3},{3,2},{4,5},{5,4},{6,7},{7,6},{8,9},{9,8},{10,11... | collective-permute-start | bytes 589832 | tf_op jit(solution)/shard_map/ppermute | solution.py:278
  30.1 10.9 %collective-permute-start.10 = (bf16[2,528,128]{2,1,0:T(8,128)(2,1)S(1)}, bf16[2,528,128]{2,1,0:T(8,128)(2,1)S(1)}, u32[]{:S(2)}, u32[]{:S(2)}) collective-permute-start(bf16[2,528,128]{2,1,0:T(8,128)(2,1)S(1)} %get-tuple-element.36), channel_id=1, source_target_pairs={{0,1},{1,0},{2,3},{3,2},{4,5},{5,4},{6,7},{7,6},{8,9},{9,8},{10,11... | collective-permute-start | bytes 811016 | tf_op jit(solution)/shard_map/ppermute | solution.py:278
  30.2 8.7 %collective-permute-start.13 = (bf16[1,528,128]{2,1,0:T(8,128)(2,1)S(1)}, bf16[1,528,128]{2,1,0:T(8,128)(2,1)S(1)}, u32[]{:S(2)}, u32[]{:S(2)}) collective-permute-start(bf16[1,528,128]{2,1,0:T(8,128)(2,1)S(1)} %join1.1.rest_3_.refs_0_), channel_id=1, source_target_pairs={{0,24},{1,25},{2,26},{3,27},{4,28},{5,29},{6,30},{7,31},{8,16},{9,... | collective-permute-start | bytes 405512 | tf_op jit(solution)/shard_map/ppermute | solution.py:278
  30.9 8.1 %collective-permute-start.12 = (bf16[1,528,128]{2,1,0:T(8,128)(2,1)S(1)}, bf16[1,528,128]{2,1,0:T(8,128)(2,1)S(1)}, u32[]{:S(2)}, u32[]{:S(2)}) collective-permute-start(bf16[1,528,128]{2,1,0:T(8,128)(2,1)S(1)} %join1.1.rest_3_.refs_0_), channel_id=1, source_target_pairs={{0,16},{1,17},{2,18},{3,19},{4,20},{5,21},{6,22},{7,23},{8,24},{9,... | collective-permute-start | bytes 405512 | tf_op jit(solution)/shard_map/ppermute | solution.py:278
  31.4 7.6 %collective-permute-start.11 = (bf16[1,528,128]{2,1,0:T(8,128)(2,1)S(1)}, bf16[1,528,128]{2,1,0:T(8,128)(2,1)S(1)}, u32[]{:S(2)}, u32[]{:S(2)}) collective-permute-start(bf16[1,528,128]{2,1,0:T(8,128)(2,1)S(1)} %join1.1.rest_3_.refs_0_), channel_id=1, source_target_pairs={{0,8},{1,9},{2,10},{3,11},{4,12},{5,13},{6,14},{7,15},{8,0},{9,1},... | collective-permute-start | bytes 405512 | tf_op jit(solution)/shard_map/ppermute | solution.py:278
  36.8 6.7 %collective-permute-start.14 = (f16[528,128]{1,0:T(8,128)(2,1)S(1)}, f16[528,128]{1,0:T(8,128)(2,1)S(1)}, u32[]{:S(2)}, u32[]{:S(2)}) collective-permute-start(f16[528,128]{1,0:T(8,128)(2,1)S(1)} %convert_element_type.30), channel_id=1, source_target_pairs={{0,4},{1,5},{2,6},{3,7},{4,0},{5,1},{6,2},{7,3},{8,12},{9,13},{10,... | collective-permute-start | bytes 405512 | tf_op jit(solution)/shard_map/ppermute | solution.py:278
  38.9 5.5 %collective-permute-start.15 = (f16[528,128]{1,0:T(8,128)(2,1)S(1)}, f16[528,128]{1,0:T(8,128)(2,1)S(1)}, u32[]{:S(2)}, u32[]{:S(2)}) collective-permute-start(f16[528,128]{1,0:T(8,128)(2,1)S(1)} %convert_element_type.32), channel_id=1, source_target_pairs={{0,2},{1,3},{2,0},{3,1},{4,6},{5,7},{6,4},{7,5},{8,10},{9,11},{10,... | collective-permute-start | bytes 405512 | tf_op jit(solution)/shard_map/ppermute | solution.py:278
  40.4 11.3 %collective-permute-start.16 = (f16[528,128]{1,0:T(8,128)(2,1)S(1)}, f16[528,128]{1,0:T(8,128)(2,1)S(1)}, u32[]{:S(2)}, u32[]{:S(2)}) collective-permute-start(f16[528,128]{1,0:T(8,128)(2,1)S(1)} %convert_element_type.34), channel_id=1, source_target_pairs={{0,6},{1,7},{2,4},{3,5},{4,2},{5,3},{6,0},{7,1},{8,14},{9,15},{10,... | collective-permute-start | bytes 405512 | tf_op jit(solution)/shard_map/ppermute | solution.py:278
  52.0 5.4 %collective-permute-start.19 = (f16[528,128]{1,0:T(8,128)(2,1)S(1)}, f16[528,128]{1,0:T(8,128)(2,1)S(1)}, u32[]{:S(2)}, u32[]{:S(2)}) collective-permute-start(f16[528,128]{1,0:T(8,128)(2,1)S(1)} %convert_element_type.36), channel_id=1, source_target_pairs={{0,24},{1,25},{2,26},{3,27},{4,28},{5,29},{6,30},{7,31},{8,16},{9,... | collective-permute-start | bytes 405512 | tf_op jit(solution)/shard_map/ppermute | solution.py:278
  53.0 8.4 %collective-permute-start.18 = (f16[528,128]{1,0:T(8,128)(2,1)S(1)}, f16[528,128]{1,0:T(8,128)(2,1)S(1)}, u32[]{:S(2)}, u32[]{:S(2)}) collective-permute-start(f16[528,128]{1,0:T(8,128)(2,1)S(1)} %convert_element_type.36), channel_id=1, source_target_pairs={{0,16},{1,17},{2,18},{3,19},{4,20},{5,21},{6,22},{7,23},{8,24},{9,... | collective-permute-start | bytes 405512 | tf_op jit(solution)/shard_map/ppermute | solution.py:278
  53.3 8.0 %collective-permute-start.17 = (f16[528,128]{1,0:T(8,128)(2,1)S(1)}, f16[528,128]{1,0:T(8,128)(2,1)S(1)}, u32[]{:S(2)}, u32[]{:S(2)}) collective-permute-start(f16[528,128]{1,0:T(8,128)(2,1)S(1)} %convert_element_type.36), channel_id=1, source_target_pairs={{0,8},{1,9},{2,10},{3,11},{4,12},{5,13},{6,14},{7,15},{8,0},{9,1},... | collective-permute-start | bytes 405512 | tf_op jit(solution)/shard_map/ppermute | solution.py:278
  61.5 1.5 %collective-permute-start.20 = (f32[2,128,128]{2,1,0:T(8,128)S(1)}, f32[2,128,128]{2,1,0:T(8,128)S(1)}, u32[]{:S(2)}, u32[]{:S(2)}) collective-permute-start(f32[2,128,128]{2,1,0:T(8,128)S(1)} %get-tuple-element.42), channel_id=1, source_target_pairs={{0,1},{1,0},{2,3},{3,2},{4,5},{5,4},{6,7},{7,6},{8,9},{9,8},{10,11... | collective-permute-start | bytes 393224 | tf_op jit(solution)/shard_map/ppermute | solution.py:278
